TPU v7x, 32 devices: a whole 2x2x4 slice. The times are simulated.
32 devices in a mesh: tm: 4 (over y, core), lat: 4 (over z), lon: 2 (over x).
Axes of the slice: x: 2, y: 2, z: 4, core: 2. Of those that a mesh axis runs over, the one named last changes fastest.
Arguments:
- residuals: bfloat16 [256, 180, 256], P('tm', 'lat', 'lon'), may hold values from -10 to 10
- diffusivity: float32 [180, 256], P('lat', 'lon'), may hold values from 0.03 to 0.24
Outputs:
- projected: bfloat16 [256, 180, 256], P('tm', 'lat', 'lon')
All inputs are finite; a program needn't handle non-finite values.
Results may differ from a plain program's by a relative error of at most 0.019.
Values may be sent and summed in bfloat16 or wider, within the bound.
No kernel may reach another device: no remote copies, remote signals or barrier semaphores. Data moves between devices by JAX's collectives and lax.ppermute only.
A program may use at most 64 MiB of HBM per device.

v0:
```python
import math

import jax
import jax.numpy as jnp
from jax import lax
from jax.sharding import PartitionSpec as P

RANK = 32
PASSES = 4
POWER = 3


exact_precision = lax.Precision.HIGHEST


def with_halo(block, sides, width, periodic):
    for axis, dim in sides:
        count = lax.axis_size(axis)
        forward = [(i, i + 1) for i in range(count - 1)]
        if periodic:
            forward.append((count - 1, 0))
        backward = [(target, source) for source, target in forward]
        low = lax.ppermute(
            lax.slice_in_dim(block, block.shape[dim] - width, None, axis=dim), axis, forward
        )
        high = lax.ppermute(lax.slice_in_dim(block, 0, width, axis=dim), axis, backward)
        block = jnp.concatenate([low, block, high], axis=dim)
    return block


def swapped(block, axis, stride):
    count = lax.axis_size(axis)
    route = []
    for low in range(count):
        high = low | 1 << stride
        if high != low and high < count:
            route += [(low, high), (high, low)]
    return lax.ppermute(block, axis, route)


def stencil(current, coeffs):
    center = current[:, 1:-1, 1:-1]
    middle = coeffs[:, 1:-1, 1:-1]
    northward = 0.5 * (middle + coeffs[:, :-2, 1:-1]) * (current[:, :-2, 1:-1] - center)
    southward = 0.5 * (middle + coeffs[:, 2:, 1:-1]) * (current[:, 2:, 1:-1] - center)
    westward = 0.5 * (middle + coeffs[:, 1:-1, :-2]) * (current[:, 1:-1, :-2] - center)
    eastward = 0.5 * (middle + coeffs[:, 1:-1, 2:]) * (current[:, 1:-1, 2:] - center)
    return center + (northward + southward + westward + eastward)


def orthonormal(block):
    inner = jnp.dot(block.T, block, precision=exact_precision)
    lower = jnp.linalg.cholesky(inner)
    return jax.scipy.linalg.solve_triangular(lower, block.T, lower=True).T


def top_space(gram):
    basis = orthonormal(gram[:, :RANK])
    for step_index in range(POWER):
        basis = orthonormal(jnp.dot(gram, basis, precision=exact_precision))
    return basis


def mode_block(stacked, gram):
    basis = top_space(gram).astype(jnp.bfloat16)
    modes = jnp.dot(basis.T, stacked, preferred_element_type=jnp.float32).astype(jnp.bfloat16)
    return (basis, modes)


def shards(residuals, diffusivity):
    snap_count, height, width = residuals.shape
    current = residuals.astype(jnp.float32)
    coeffs = diffusivity[None]
    field_ext, coeff_ext = (
        with_halo(current.astype(jnp.bfloat16), (("lon", 2),), PASSES, True).astype(current.dtype),
        with_halo(coeffs.astype(jnp.bfloat16), (("lon", 2),), PASSES, True).astype(coeffs.dtype),
    )
    field_ext, coeff_ext = (
        with_halo(field_ext.astype(jnp.bfloat16), (("lat", 1),), PASSES, False).astype(
            field_ext.dtype
        ),
        with_halo(coeff_ext.astype(jnp.bfloat16), (("lat", 1),), PASSES, False).astype(
            coeff_ext.dtype
        ),
    )
    global_rows = lax.axis_index("lat") * height - PASSES + jnp.arange(height + 2 * PASSES)
    inside = ((global_rows >= 0) & (global_rows < height * lax.axis_size("lat"))).astype(
        jnp.float32
    )
    for pass_index in range(PASSES):
        field_ext = stencil(field_ext, coeff_ext)
        coeff_ext = coeff_ext[:, 1:-1, 1:-1]
        inside = inside[1:-1]
        field_ext = field_ext * inside[None, :, None]
    current = field_ext
    rows = (lax.axis_index("lat") * height + jnp.arange(height)).astype(jnp.float32)
    latitude = (rows + 0.5) * math.pi / (height * lax.axis_size("lat")) - math.pi / 2
    scale = jnp.sqrt(jnp.cos(latitude))
    weighted = (
        (current * scale[None, :, None]).astype(jnp.bfloat16).reshape(snap_count, height * width)
    )
    gram = lax.psum(
        jnp.dot(weighted, weighted.T, preferred_element_type=jnp.float32), ("lat", "lon")
    )
    basis, modes = mode_block(weighted, gram)
    levels_count = lax.axis_size("tm").bit_length() - 1
    for level_index in range(levels_count):
        partner = swapped(modes, "tm", level_index)
        upper_bit = lax.axis_index("tm") >> level_index & 1
        lower_first = jnp.concatenate([modes, partner], axis=0)
        upper_first = jnp.concatenate([partner, modes], axis=0)
        stacked = jnp.where(upper_bit == 0, lower_first, upper_first)
        gram = lax.psum(
            jnp.dot(stacked, stacked.T, preferred_element_type=jnp.float32), ("lat", "lon")
        )
        basis, modes = mode_block(stacked, gram)
    basis_f = basis.astype(jnp.float32)
    curvature = jnp.dot(
        basis_f.T, jnp.dot(gram, basis_f, precision=exact_precision), precision=exact_precision
    )
    factor = jnp.linalg.cholesky(curvature)
    coef = lax.psum(jnp.dot(weighted, modes.T, preferred_element_type=jnp.float32), ("lat", "lon"))
    solved = jax.scipy.linalg.cho_solve((factor, True), coef.T).T.astype(jnp.bfloat16)
    projected = jnp.dot(solved, modes, preferred_element_type=jnp.float32).astype(jnp.bfloat16)
    return projected.reshape(snap_count, height, width)


def solution(mesh):
    return jax.shard_map(
        shards,
        mesh=mesh,
        in_specs=(P("tm", "lat", "lon"), P("lat", "lon")),
        out_specs=P("tm", "lat", "lon"),
        check_vma=False,
    )
```

profile of v0, /device:TPU:0, one launch (start us, length us, event | category | flops | bytes accessed | tf_op | source)
XLA Modules:
  0.0 291.4 jit_solution(18148282656198801997)
XLA Ops:
  0.8 2.9 %collective-permute-start.4 = (bf16[1,45,4]{2,1,0:T(8,128)(2,1)S(1)}, bf16[1,45,4]{2,1,0:T(8,128)(2,1)S(1)}, u32[]{:S(2)}, u32[]{:S(2)}) collective-permute-start(bf16[1,45,4]{2,1,0:T(8,128)(2,1)S(1)} %get-tuple-element.29), channel_id=1, source_target_pairs={{0,1},{1,0},{2,3},{3,2},{4,5},{5,4},{6,7},{7,6},{8,9},{9,8},{10,11... | collective-permute-start | bytes 1088 | tf_op jit(solution)/shard_map/ppermute | solution.py:23
  8.6 3.9 %collective-permute-start.6 = (bf16[1,4,136]{2,1,0:T(4,128)(2,1)S(1)}, bf16[1,4,136]{2,1,0:T(4,128)(2,1)S(1)}, u32[]{:S(2)}, u32[]{:S(2)}) collective-permute-start(bf16[1,4,136]{2,1,0:T(4,128)(2,1)S(1)} %get-tuple-element.27), channel_id=1, source_target_pairs={{0,2},{2,4},{4,6},{1,3},{3,5},{5,7},{8,10},{10,12},{12,14},{9,11},... | collective-permute-start | bytes 3272 | tf_op jit(solution)/shard_map/ppermute | solution.py:23
  14.1 3.9 %collective-permute-done.7 = bf16[1,4,136]{2,1,0:T(4,128)(2,1)S(1)} collective-permute-done((bf16[1,4,136]{2,1,0:T(4,128)(2,1)S(1)}, bf16[1,4,136]{2,1,0:T(4,128)(2,1)S(1)}, u32[]{:S(2)}, u32[]{:S(2)}) %collective-permute-start.7) | collective-permute-done | bytes 1120 | tf_op jit(solution)/shard_map/ppermute | solution.py:26
  19.6 3.5 %collective-permute-start.2 = (bf16[64,4,136]{2,0,1:T(8,128)(2,1)S(1)}, bf16[64,4,136]{2,0,1:T(8,128)(2,1)S(1)}, u32[]{:S(2)}, u32[]{:S(2)}) collective-permute-start(bf16[64,4,136]{2,0,1:T(8,128)(2,1)S(1)} %get-tuple-element.6), channel_id=1, source_target_pairs={{0,2},{2,4},{4,6},{1,3},{3,5},{5,7},{8,10},{10,12},{12,14},{9,11},... | collective-permute-start | bytes 208904 | tf_op jit(solution)/shard_map/ppermute | solution.py:23
  25.6 4.4 %collective-permute-done.3 = bf16[64,4,136]{2,0,1:T(8,128)(2,1)S(1)} collective-permute-done((bf16[64,4,136]{2,0,1:T(8,128)(2,1)S(1)}, bf16[64,4,136]{2,0,1:T(8,128)(2,1)S(1)}, u32[]{:S(2)}, u32[]{:S(2)}) %collective-permute-start.3) | collective-permute-done | bytes 69664 | tf_op jit(solution)/shard_map/ppermute | solution.py:26
  30.8 5.0 %fusion.3 = f32[64,51,134]{2,0,1:T(8,128)S(1)} fusion(f32[64,53,136]{2,0,1:T(8,128)S(1)} %maximum_convert_fusion, f32[51]{0:T(128)S(1)} %slice.216, f32[51,134]{1,0:T(8,128)S(1)} %get-tuple-element.24, f32[51,134]{1,0:T(8,128)S(1)} %get-tuple-element.25, f32[51,134]{1,0:T(8,128)S(1)} %get-tuple-element.26, f32[51,134]{1,0:T(8,128)S(1)} %get-tuple-element.23), kind=kLoop, calls=%fused_computation.8 | loop fusion | flops 5685888 | bytes 10606572 | tf_op jit(solution)/shard_map/mul | solution.py:94
  35.8 4.7 %fusion.12 = f32[64,49,132]{2,0,1:T(8,128)S(1)} fusion(f32[64,51,134]{2,0,1:T(8,128)S(1)} %fusion.3, f32[49]{0:T(128)S(1)} %slice.227, f32[49,132]{1,0:T(8,128)S(1)} %get-tuple-element.20, f32[49,132]{1,0:T(8,128)S(1)} %get-tuple-element.21, f32[49,132]{1,0:T(8,128)S(1)} %get-tuple-element.22, f32[49,132]{1,0:T(8,128)S(1)} %get-tuple-element.19), kind=kLoop, calls=%fused_computation.21 | loop fusion | flops 5381376 | bytes 10038532 | tf_op jit(solution)/shard_map/mul | solution.py:94
  40.5 3.6 %fusion.21 = f32[64,47,130]{2,0,1:T(8,128)S(1)} fusion(f32[64,49,132]{2,0,1:T(8,128)S(1)} %fusion.12, f32[47]{0:T(128)S(1)} %slice.238, f32[47,130]{1,0:T(8,128)S(1)} %get-tuple-element.16, f32[47,130]{1,0:T(8,128)S(1)} %get-tuple-element.17, f32[47,130]{1,0:T(8,128)S(1)} %get-tuple-element.18, f32[47,130]{1,0:T(8,128)S(1)} %get-tuple-element.15), kind=kLoop, calls=%fused_computation.34 | loop fusion | flops 5083520 | bytes 9482908 | tf_op jit(solution)/shard_map/mul | solution.py:94
  46.1 3.5 %convolution_bitcast_fusion = f32[64,64]{1,0:T(8,128)S(1)} fusion(f32[64,47,130]{2,0,1:T(8,128)S(1)} %fusion.21, f32[45]{0:T(128)S(1)} %cosine_sqrt_fusion, f32[45]{0:T(128)S(1)} %slice.249, f32[45,128]{1,0:T(8,128)S(1)} %get-tuple-element.13, f32[45,128]{1,0:T(8,128)S(1)} %get-tuple-element.14, f32[45,128]{1,0:T(8,128)S(1)} %get-tuple-element.12, ...), kind=kOutput, calls=%fused_computation.60 | convolution fusion | flops 58245120 | bytes 14960640 | tf_op jit(solution)/shard_map/dot_general | solution.py:103
  49.6 34.4 %psum.28 = f32[64,64]{1,0:T(8,128)S(1)} all-reduce(f32[64,64]{1,0:T(8,128)S(1)} %convolution_bitcast_fusion), channel_id=1, replica_groups=mesh['tm'=4,'lat'=4,'lon'=2] {'lat','lon'}, use_global_device_ids=true, to_apply=%region_0.0 | all-reduce | flops 4096 | bytes 32768 | tf_op jit(solution)/shard_map/psum | solution.py:102
  84.3 2.9 %cholesky.209 = f32[32,32]{1,0:T(8,128)S(1)} custom-call(f32[32,32]{1,0:T(8,128)S(1)} %fusion.148), custom_call_target="Cholesky" | custom-call | tf_op jit(solution)/shard_map/jit(cholesky)/cholesky | solution.py:53
  88.6 2.4 custom-call.22
  91.7 2.9 %cholesky.220 = f32[32,32]{1,0:T(8,128)S(1)} custom-call(f32[32,32]{1,0:T(8,128)S(1)} %fusion.146), custom_call_target="Cholesky" | custom-call | tf_op jit(solution)/shard_map/jit(cholesky)/cholesky | solution.py:53
  99.0 2.9 %cholesky.231 = f32[32,32]{1,0:T(8,128)S(1)} custom-call(f32[32,32]{1,0:T(8,128)S(1)} %fusion.142), custom_call_target="Cholesky" | custom-call | tf_op jit(solution)/shard_map/jit(cholesky)/cholesky | solution.py:53
  103.3 2.4 custom-call.24
  106.4 2.9 %cholesky.242 = f32[32,32]{1,0:T(8,128)S(1)} custom-call(f32[32,32]{1,0:T(8,128)S(1)} %fusion.138), custom_call_target="Cholesky" | custom-call | tf_op jit(solution)/shard_map/jit(cholesky)/cholesky | solution.py:53
  115.7 33.0 %psum.29 = f32[64,64]{1,0:T(8,128)S(1)} all-reduce(f32[64,64]{1,0:T(8,128)S(1)} %fusion.45), channel_id=1, replica_groups=mesh['tm'=4,'lat'=4,'lon'=2] {'lat','lon'}, use_global_device_ids=true, to_apply=%region_3.6 | all-reduce | flops 4096 | bytes 32768 | tf_op jit(solution)/shard_map/psum | solution.py:113
  149.1 2.9 %cholesky.253 = f32[32,32]{1,0:T(8,128)S(1)} custom-call(f32[32,32]{1,0:T(8,128)S(1)} %fusion.135), custom_call_target="Cholesky" | custom-call | tf_op jit(solution)/shard_map/jit(cholesky)/cholesky | solution.py:53
  156.4 2.9 %cholesky.264 = f32[32,32]{1,0:T(8,128)S(1)} custom-call(f32[32,32]{1,0:T(8,128)S(1)} %fusion.133), custom_call_target="Cholesky" | custom-call | tf_op jit(solution)/shard_map/jit(cholesky)/cholesky | solution.py:53
  160.7 2.4 custom-call.27
  163.8 2.9 %cholesky.275 = f32[32,32]{1,0:T(8,128)S(1)} custom-call(f32[32,32]{1,0:T(8,128)S(1)} %fusion.129), custom_call_target="Cholesky" | custom-call | tf_op jit(solution)/shard_map/jit(cholesky)/cholesky | solution.py:53
  171.1 2.9 %cholesky.286 = f32[32,32]{1,0:T(8,128)S(1)} custom-call(f32[32,32]{1,0:T(8,128)S(1)} %fusion.125), custom_call_target="Cholesky" | custom-call | tf_op jit(solution)/shard_map/jit(cholesky)/cholesky | solution.py:53
  179.9 6.0 %collective-permute-done.9 = bf16[32,5760]{1,0:T(8,128)(2,1)S(1)} collective-permute-done((bf16[32,5760]{1,0:T(8,128)(2,1)S(1)}, bf16[32,5760]{1,0:T(8,128)(2,1)S(1)}, u32[]{:S(2)}, u32[]{:S(2)}) %collective-permute-start.9) | collective-permute-done | bytes 368672 | tf_op jit(solution)/shard_map/ppermute | solution.py:38
  186.3 33.3 %psum.30 = f32[64,64]{1,0:T(8,128)S(1)} all-reduce(f32[64,64]{1,0:T(8,128)S(1)} %fusion.44), channel_id=1, replica_groups=mesh['tm'=4,'lat'=4,'lon'=2] {'lat','lon'}, use_global_device_ids=true, to_apply=%region_4.7 | all-reduce | flops 4096 | bytes 32768 | tf_op jit(solution)/shard_map/psum | solution.py:113
  219.9 2.9 %cholesky.297 = f32[32,32]{1,0:T(8,128)S(1)} custom-call(f32[32,32]{1,0:T(8,128)S(1)} %fusion.122), custom_call_target="Cholesky" | custom-call | tf_op jit(solution)/shard_map/jit(cholesky)/cholesky | solution.py:53
  224.2 2.4 custom-call.30
  227.3 2.9 %cholesky.308 = f32[32,32]{1,0:T(8,128)S(1)} custom-call(f32[32,32]{1,0:T(8,128)S(1)} %fusion.120), custom_call_target="Cholesky" | custom-call | tf_op jit(solution)/shard_map/jit(cholesky)/cholesky | solution.py:53
  231.5 2.4 custom-call.31
  234.6 2.9 %cholesky.319 = f32[32,32]{1,0:T(8,128)S(1)} custom-call(f32[32,32]{1,0:T(8,128)S(1)} %fusion.116), custom_call_target="Cholesky" | custom-call | tf_op jit(solution)/shard_map/jit(cholesky)/cholesky | solution.py:53
  242.0 2.9 %cholesky.330 = f32[32,32]{1,0:T(8,128)S(1)} custom-call(f32[32,32]{1,0:T(8,128)S(1)} %fusion.112), custom_call_target="Cholesky" | custom-call | tf_op jit(solution)/shard_map/jit(cholesky)/cholesky | solution.py:53
  249.3 2.9 %cholesky.341 = f32[32,32]{1,0:T(8,128)S(1)} custom-call(f32[32,32]{1,0:T(8,128)S(1)} %fusion.109), custom_call_target="Cholesky" | custom-call | tf_op jit(solution)/shard_map/jit(cholesky)/cholesky | solution.py:121
  256.6 33.0 %psum.31 = f32[32,64]{1,0:T(8,128)S(1)} all-reduce(f32[32,64]{1,0:T(8,128)S(1)} %fusion.39), channel_id=1, replica_groups=mesh['tm'=4,'lat'=4,'lon'=2] {'lat','lon'}, use_global_device_ids=true, to_apply=%region_5.8 | all-reduce | flops 2048 | bytes 16384 | tf_op jit(solution)/shard_map/psum | solution.py:122
  (156 shorter events, 65.4 us)
Async XLA Ops:
  0.8 7.7 %collective-permute-start.4 = (bf16[1,45,4]{2,1,0:T(8,128)(2,1)S(1)}, bf16[1,45,4]{2,1,0:T(8,128)(2,1)S(1)}, u32[]{:S(2)}, u32[]{:S(2)}) collective-permute-start(bf16[1,45,4]{2,1,0:T(8,128)(2,1)S(1)} %get-tuple-element.29), channel_id=1, source_target_pairs={{0,1},{1,0},{2,3},{3,2},{4,5},{5,4},{6,7},{7,6},{8,9},{9,8},{10,11... | collective-permute-start | bytes 1088 | tf_op jit(solution)/shard_map/ppermute | solution.py:23
  3.8 4.8 %collective-permute-start.5 = (bf16[1,45,4]{2,1,0:T(8,128)(2,1)S(1)}, bf16[1,45,4]{2,1,0:T(8,128)(2,1)S(1)}, u32[]{:S(2)}, u32[]{:S(2)}) collective-permute-start(bf16[1,45,4]{2,1,0:T(8,128)(2,1)S(1)} %get-tuple-element.30), channel_id=1, source_target_pairs={{1,0},{0,1},{3,2},{2,3},{5,4},{4,5},{7,6},{6,7},{9,8},{8,9},{11,10... | collective-permute-start | bytes 1088 | tf_op jit(solution)/shard_map/ppermute | solution.py:26
  5.9 12.6 %collective-permute-start = (bf16[64,45,4]{0,1,2:T(8,128)(2,1)S(1)}, bf16[64,45,4]{0,1,2:T(8,128)(2,1)S(1)}, u32[]{:S(2)}, u32[]{:S(2)}) collective-permute-start(bf16[64,45,4]{0,1,2:T(8,128)(2,1)S(1)} %copy.51), channel_id=1, source_target_pairs={{0,1},{1,0},{2,3},{3,2},{4,5},{5,4},{6,7},{7,6},{8,9},{9,8},{10,11... | collective-permute-start | bytes 69128 | tf_op jit(solution)/shard_map/ppermute | solution.py:23
  8.3 10.6 %collective-permute-start.1 = (bf16[64,45,4]{0,1,2:T(8,128)(2,1)S(1)}, bf16[64,45,4]{0,1,2:T(8,128)(2,1)S(1)}, u32[]{:S(2)}, u32[]{:S(2)}) collective-permute-start(bf16[64,45,4]{0,1,2:T(8,128)(2,1)S(1)} %copy.52), channel_id=1, source_target_pairs={{1,0},{0,1},{3,2},{2,3},{5,4},{4,5},{7,6},{6,7},{9,8},{8,9},{11,10... | collective-permute-start | bytes 69128 | tf_op jit(solution)/shard_map/ppermute | solution.py:26
  8.6 5.5 %collective-permute-start.6 = (bf16[1,4,136]{2,1,0:T(4,128)(2,1)S(1)}, bf16[1,4,136]{2,1,0:T(4,128)(2,1)S(1)}, u32[]{:S(2)}, u32[]{:S(2)}) collective-permute-start(bf16[1,4,136]{2,1,0:T(4,128)(2,1)S(1)} %get-tuple-element.27), channel_id=1, source_target_pairs={{0,2},{2,4},{4,6},{1,3},{3,5},{5,7},{8,10},{10,12},{12,14},{9,11},... | collective-permute-start | bytes 3272 | tf_op jit(solution)/shard_map/ppermute | solution.py:23
  12.5 5.5 %collective-permute-start.7 = (bf16[1,4,136]{2,1,0:T(4,128)(2,1)S(1)}, bf16[1,4,136]{2,1,0:T(4,128)(2,1)S(1)}, u32[]{:S(2)}, u32[]{:S(2)}) collective-permute-start(bf16[1,4,136]{2,1,0:T(4,128)(2,1)S(1)} %get-tuple-element.28), channel_id=1, source_target_pairs={{2,0},{4,2},{6,4},{3,1},{5,3},{7,5},{10,8},{12,10},{14,12},{11,9},... | collective-permute-start | bytes 3272 | tf_op jit(solution)/shard_map/ppermute | solution.py:26
  18.1 1.3 copy-start
  19.6 6.0 %collective-permute-start.2 = (bf16[64,4,136]{2,0,1:T(8,128)(2,1)S(1)}, bf16[64,4,136]{2,0,1:T(8,128)(2,1)S(1)}, u32[]{:S(2)}, u32[]{:S(2)}) collective-permute-start(bf16[64,4,136]{2,0,1:T(8,128)(2,1)S(1)} %get-tuple-element.6), channel_id=1, source_target_pairs={{0,2},{2,4},{4,6},{1,3},{3,5},{5,7},{8,10},{10,12},{12,14},{9,11},... | collective-permute-start | bytes 208904 | tf_op jit(solution)/shard_map/ppermute | solution.py:23
  23.1 6.9 %collective-permute-start.3 = (bf16[64,4,136]{2,0,1:T(8,128)(2,1)S(1)}, bf16[64,4,136]{2,0,1:T(8,128)(2,1)S(1)}, u32[]{:S(2)}, u32[]{:S(2)}) collective-permute-start(bf16[64,4,136]{2,0,1:T(8,128)(2,1)S(1)} %get-tuple-element.8), channel_id=1, source_target_pairs={{2,0},{4,2},{6,4},{3,1},{5,3},{7,5},{10,8},{12,10},{14,12},{11,9},... | collective-permute-start | bytes 208904 | tf_op jit(solution)/shard_map/ppermute | solution.py:26
  113.6 1.8 collective-permute-start.8
  178.3 7.6 %collective-permute-start.9 = (bf16[32,5760]{1,0:T(8,128)(2,1)S(1)}, bf16[32,5760]{1,0:T(8,128)(2,1)S(1)}, u32[]{:S(2)}, u32[]{:S(2)}) collective-permute-start(bf16[32,5760]{1,0:T(8,128)(2,1)S(1)} %convolution_convert_fusion.2), channel_id=1, source_target_pairs={{0,16},{16,0},{8,24},{24,8},{1,17},{17,1},{9,25},{25,9},{2,18},{18... | collective-permute-start | bytes 1105928 | tf_op jit(solution)/shard_map/ppermute | solution.py:38
where the time goes:
time: 292 us; the launch traced here: 291 us
  blocking collectives  134 us (46%)
  other arithmetic  105 us (36%)
  waiting for transfers between devices  17 us (6%)
  starting transfers between devices  16.8 us (6%)
  matrix products  12.7 us (4%)
  local copies, waits for them, and re-layouts  5.67 us (2%)
    psum x2, blocking collectives, shards(): lax.psum(jnp.dot(stacked, stacked.T, preferred_element_type=jnp.float32),...  66.3 us
    another operation x36, other arithmetic, orthonormal(): lower = jnp.linalg.cholesky(inner)  43.2 us
    another operation x24, other arithmetic, orthonormal(): return jax.scipy.linalg.solve_triangular(lower, block.T, lower=True).T  37 us
    psum x1, blocking collectives, shards(): lax.psum(jnp.dot(weighted, weighted.T, preferred_element_type=jnp.float32...  34.4 us
    psum x1, blocking collectives, shards(): lax.psum(jnp.dot(weighted, modes.T, preferred_element_type=jnp.float32),...  33 us
    mul x3, other arithmetic, shards(): field_ext = field_ext * inside[None, :, None]  13.3 us
    ppermute x4, starting transfers between devices, with_halo(): lax.ppermute(lax.slice_in_dim(block, block.shape[dim] - width, None, axis...  12.4 us
    ppermute x4, waiting for transfers between devices, with_halo(): lax.ppermute(lax.slice_in_dim(block, 0, width, axis=dim), axis, backward)  8.24 us
  transfers between devices with their start and end apart: 10, of which 5 were waited for; matrix products, arithmetic and copies ran while one was open for 1% of the time, Pallas kernels for 0%

commit v1 on v0

v1 whole, which is shorter than its diff:
```python
import functools
import math

import jax
import jax.numpy as jnp
from jax import lax
from jax.experimental import pallas as pl
from jax.experimental.pallas import tpu as pltpu
from jax.sharding import PartitionSpec as P

RANK = 32
PASSES = 4
LANES = 128
MSG = 80
SEG = 32
exact = lax.Precision.HIGHEST
VMEM = pltpu.VMEM


def whole():
    return pl.BlockSpec(memory_space=VMEM)


def kernel_call(body, outs, scratch=(), flops=1 << 20):
    return pl.pallas_call(
        body,
        out_shape=outs,
        out_specs=jax.tree.map(lambda _: whole(), outs),
        scratch_shapes=list(scratch),
        compiler_params=pltpu.CompilerParams(vmem_limit_bytes=48 << 20),
        cost_estimate=pl.CostEstimate(flops=flops, bytes_accessed=1 << 20, transcendentals=0),
    )


def lane_iota(shape):
    return lax.broadcasted_iota(jnp.int32, shape, len(shape) - 1)


def roll(x, shift):
    return pltpu.roll(x, shift % LANES, x.ndim - 1)


def pack_body(x_ref, d_ref, m_ref, north_ref, south_ref):
    rows = x_ref.shape[0]
    snaps = x_ref.shape[1]
    lane = lane_iota((1, LANES))
    pad = jnp.zeros((MSG - snaps - 2, LANES), jnp.float32)

    def plane(i):
        d = d_ref[i : i + 1, :]
        high = d.astype(jnp.bfloat16).astype(jnp.float32)
        return jnp.concatenate([x_ref[i].astype(jnp.float32), high, d - high, pad], axis=0)

    for p in range(m_ref.shape[0]):
        acc = jnp.zeros((MSG, LANES), jnp.float32)
        for q in range(min(16, rows - 16 * p)):
            v = plane(16 * p + q)
            acc = jnp.where((lane >= 8 * q) & (lane < 8 * q + 4), roll(v, 8 * q), acc)
            acc = jnp.where((lane >= 8 * q + 4) & (lane < 8 * q + 8), roll(v, 8 * q + 8), acc)
        m_ref[p] = acc.astype(jnp.bfloat16)
    for r in range(PASSES):
        north_ref[r] = plane(r).astype(jnp.bfloat16)
        south_ref[r] = plane(rows - PASSES + r).astype(jnp.bfloat16)


def halo_exchange(x, d):
    rows = x.shape[0]
    planes = -(-rows // 16)
    shape = lambda n: jax.ShapeDtypeStruct((n, MSG, LANES), jnp.bfloat16)
    packed, north, south = kernel_call(pack_body, (shape(planes), shape(PASSES), shape(PASSES)))(x, d)
    lons, lats = lax.axis_size("lon"), lax.axis_size("lat")
    forward = [(i, (i + 1) % lons) for i in range(lons)]
    side = lax.ppermute(packed, "lon", forward)
    if lons > 2:
        from_east = lax.ppermute(packed, "lon", [(b, a) for a, b in forward])
        side = jnp.where(lane_iota((1, 1, LANES)) % 8 < 4, from_east, side)
    up = [(i, i + 1) for i in range(lats - 1)]
    down = [(b, a) for a, b in up]
    last = (rows - PASSES) // 16
    from_north = lax.ppermute(jnp.concatenate([south, side[last : last + 1]]), "lat", up)
    from_south = lax.ppermute(jnp.concatenate([north, side[:1]]), "lat", down)
    return side, from_north, from_south


def smooth_body(x_ref, d_ref, side_ref, north_ref, south_ref, y_ref, u, s, dm, ds, ce, cs, se, ss, scale):
    rows, snaps, _ = x_ref.shape
    lats = lax.axis_size("lat")
    lat = lax.axis_index("lat")
    ext = rows + 2 * PASSES
    lane = lane_iota((1, LANES))
    groups = snaps // 8
    last_q = (rows - PASSES) % 16

    def halo(e, lo, hi):
        if e < PASSES:
            ref, p, q = north_ref, PASSES, last_q + e
        elif e < rows + PASSES:
            ref, p, q = side_ref, (e - PASSES) // 16, (e - PASSES) % 16
        else:
            ref, p, q = south_ref, PASSES, e - rows - PASSES
        return ref[p, lo:hi, :], q

    def in_strip(shape_lane, own_high, own_low, edge):
        at = shape_lane % SEG
        return jnp.where(at < 12, own_high, jnp.where(at < 20, edge, own_low))

    u[PASSES : PASSES + rows] = x_ref[...].astype(jnp.float32)
    dm[PASSES : PASSES + rows, :] = d_ref[...]
    dm[ext:, :] = jnp.zeros((dm.shape[0] - ext, LANES), jnp.float32)
    ds[ext:, :] = jnp.zeros((dm.shape[0] - ext, LANES), jnp.float32)
    for r in range(PASSES):
        for e, ref in ((r, north_ref), (rows + PASSES + r, south_ref)):
            u[e] = ref[r, :snaps, :].astype(jnp.float32)
            term = ref[r, snaps : snaps + 16, :].astype(jnp.float32)
            dm[e : e + 1, :] = term[0:1] + term[1:2]
    for e in range(ext):
        piece, q = halo(e, snaps, snaps + 16)
        piece = piece.astype(jnp.float32)
        ds[e : e + 1, :] = roll(piece[0:1] + piece[1:2], 12 - 8 * q)
        piece, q = halo(e, 0, snaps)
        piece = piece.astype(jnp.float32)
        for h in range(groups // 4):
            acc = None
            for g in range(4):
                at = 8 * (4 * h + g)
                own = u[e, at : at + 8, :]
                part = in_strip(
                    lane,
                    roll(own, 12 + SEG * g),
                    roll(own, 20 + SEG * g),
                    roll(piece[at : at + 8], 12 + SEG * g - 8 * q),
                )
                acc = part if g == 0 else jnp.where(lane >= SEG * g, part, acc)
            s[e, 8 * h : 8 * h + 8, :] = acc
    d = dm[...]
    first = in_strip(lane, roll(d, 12), roll(d, 20), ds[...])
    strip = first
    for g in range(1, 4):
        strip = jnp.where(lane >= SEG * g, roll(first, SEG * g), strip)
    ce[...] = 0.5 * (d + roll(d, -1))
    se[...] = 0.5 * (strip + roll(strip, -1))
    ds[...] = strip
    cs[0 : ext - 1, :] = 0.5 * (dm[0 : ext - 1, :] + dm[1:ext, :])
    ss[0 : ext - 1, :] = 0.5 * (ds[0 : ext - 1, :] + ds[1:ext, :])
    row = lax.broadcasted_iota(jnp.int32, scale.shape, 0) + lat * rows
    angle = (row.astype(jnp.float32) + 0.5) * math.pi / (rows * lats) - math.pi / 2
    scale[...] = jnp.sqrt(jnp.maximum(jnp.cos(angle), 0.0))

    def updated(field, e, carry, south_c, east_c):
        current, above = carry
        below = field[e + 1]
        south = south_c[pl.ds(e, 1), :] * (below - current)
        east = east_c[pl.ds(e, 1), :] * (roll(current, -1) - current)
        fresh = current + ((south - above) + (east - roll(east, 1)))
        return fresh, (below, south)

    def entry(field, e, south_c):
        current = field[e]
        return current, south_c[e : e + 1, :] * (current - field[e - 1])

    for step in range(PASSES):
        final = step == PASSES - 1

        def body(e, carry):
            main, edge = carry
            fresh, main = updated(u, e, main, cs, ce)
            fresh_edge, edge = updated(s, e, edge, ss, se)
            if not final:
                u[e] = fresh
                s[e] = fresh_edge
            else:
                parts = []
                for g in range(groups):
                    strip_part = fresh_edge[8 * (g // 4) : 8 * (g // 4) + 8]
                    base = SEG * (g % 4)
                    low = roll(strip_part, -(20 + base))
                    high = roll(strip_part, 116 - base)
                    body_part = fresh[8 * g : 8 * g + 8]
                    merged = jnp.where(lane < PASSES, low, jnp.where(lane >= LANES - PASSES, high, body_part))
                    parts.append(merged)
                i = e - PASSES
                merged = jnp.concatenate(parts, axis=0) * scale[pl.ds(i, 1), :]
                y_ref[i] = merged.astype(jnp.bfloat16)
            return main, edge

        start = step + 1
        lax.fori_loop(start, ext - 1 - step, body, (entry(u, start, cs), entry(s, start, ss)))
        if not final:

            @pl.when(lat == 0)
            def _():
                u[PASSES - 1] = jnp.zeros(u.shape[1:], jnp.float32)
                s[PASSES - 1] = jnp.zeros(s.shape[1:], jnp.float32)

            @pl.when(lat == lats - 1)
            def _():
                u[rows + PASSES] = jnp.zeros(u.shape[1:], jnp.float32)
                s[rows + PASSES] = jnp.zeros(s.shape[1:], jnp.float32)


def smooth(x, d, side, north, south):
    rows, snaps, width = x.shape
    ext = rows + 2 * PASSES
    tall = -(-ext // 8) * 8
    field = lambda n: VMEM((ext, n, width), jnp.float32)
    plane = VMEM((tall, width), jnp.float32)
    return kernel_call(
        smooth_body,
        jax.ShapeDtypeStruct((rows, snaps, width), jnp.bfloat16),
        [field(snaps), field(snaps // 4)] + [plane] * 7,
    )(x, d, side, north, south)


def mm(a, b):
    return jnp.dot(a, b, precision=exact, preferred_element_type=jnp.float32)


def mmt(a, b):
    return lax.dot_general(
        a, b, (((1,), (1,)), ((), ())), precision=exact, preferred_element_type=jnp.float32
    )


def whitened(s, zt, block=16):
    n = s.shape[0]
    a = jnp.concatenate([s, zt], axis=1)
    w = a.shape[1]
    row = lax.broadcasted_iota(jnp.int32, (n, w), 0)
    diagonal = row == lane_iota((n, w))
    floor = jnp.broadcast_to(
        jnp.sum(jnp.where(diagonal, a, 0.0), axis=1, keepdims=True) * 1e-7 + 1e-37, (n, w)
    )
    for k0 in range(0, n, block):
        cols = [jnp.broadcast_to(a[:, k0 + j : k0 + j + 1], (n, w)) for j in range(block)]
        for p in range(block):
            k = k0 + p
            if k == n - 1:
                continue
            inverse = 1.0 / jnp.maximum(cols[p][k : k + 1, :], floor[k : k + 1, :])
            below = jnp.where(row > k, cols[p], 0.0)
            for j in range(p + 1, block):
                cols[j] = cols[j] - below * (cols[j][k : k + 1, :] * inverse)
            a = a - below * (a[k : k + 1, :] * inverse)
    pivots = jnp.sum(jnp.where(diagonal, a, 0.0), axis=1, keepdims=True)
    return a[:, n:] * lax.rsqrt(jnp.maximum(pivots, floor[:, :1]))


def power_basis(h, upper_first):
    n = h.shape[0]
    eye = lax.broadcasted_iota(jnp.int32, (n, n), 0) == lane_iota((n, n))
    top = jnp.max(jnp.max(jnp.where(eye, h, 0.0), axis=1, keepdims=True), axis=0, keepdims=True)
    unit = 1.0 / jnp.maximum(top, 1e-30)
    h2 = mm(h, h) * (unit * unit)
    start = h2[:RANK]
    if upper_first is not None:
        start = jnp.where(upper_first, h2[RANK:], start)
    return mm(whitened(mmt(start, start), start), h2)


def top_rows(h, upper_first=None):
    zt = power_basis(h, upper_first)
    return whitened(mmt(zt, zt), zt)


def dot_t(a, b):
    return lax.dot_general(a, b, (((1,), (1,)), ((), ())), preferred_element_type=jnp.float32)


def pair_gram_body(own_ref, other_ref, o_ref):
    acc = None
    for i in range(own_ref.shape[0]):
        own = own_ref[i]
        part = dot_t(own, jnp.concatenate([own, other_ref[i]], axis=0))
        acc = part if acc is None else acc + part
    for j in range(o_ref.shape[0]):
        o_ref[j] = acc


def odd(level):
    return (lax.axis_index("tm") >> level & 1) == 1


def leaf_body(g_ref, gp_ref, own_ref, other_ref, modes_ref, h_ref, c_ref):
    n = own_ref.shape[1]
    own_rows, other_rows = g_ref[...], gp_ref[...]
    gram = jnp.concatenate([own_rows, pltpu.roll(other_rows, n, 1)], axis=0)
    q_own = top_rows(own_rows[:, :n])
    q_other = top_rows(other_rows[:, :n])
    zero = jnp.zeros_like(q_own)
    basis = jnp.concatenate(
        [jnp.concatenate([q_own, zero], axis=1), jnp.concatenate([zero, q_other], axis=1)], axis=0
    )
    merged = mmt(mm(basis, gram), basis)
    w = mm(top_rows(merged, odd(0)), basis).astype(jnp.bfloat16)
    wf = w.astype(jnp.float32)
    gw = mmt(gram, wf)
    c_ref[...] = gw[:n]
    h_ref[...] = mm(wf, gw)
    for i in range(own_ref.shape[0]):
        stacked = jnp.concatenate([own_ref[i], other_ref[i]], axis=0)
        modes_ref[i] = jnp.dot(w, stacked, preferred_element_type=jnp.float32).astype(jnp.bfloat16)


def cross_body(other_ref, y_ref, own_ref, o_ref):
    acc = None
    for i in range(y_ref.shape[0]):
        other = other_ref[i]
        part = dot_t(other, jnp.concatenate([y_ref[i], own_ref[i], other], axis=0))
        acc = part if acc is None else acc + part
    for j in range(o_ref.shape[0]):
        o_ref[j] = acc


def merged_gram(p_ref, h_ref, c_ref, n):
    total = p_ref[0]
    for j in range(1, p_ref.shape[0]):
        total = total + p_ref[j]
    mixed = total[:, n : n + RANK]
    gram = jnp.concatenate(
        [
            jnp.concatenate([h_ref[...], mixed.T], axis=1),
            jnp.concatenate([mixed, total[:, n + RANK :]], axis=1),
        ],
        axis=0,
    )
    coef = jnp.concatenate([c_ref[...], total[:, :n].T], axis=1)
    return gram, coef


def merge_body(level, p_ref, h_ref, c_ref, own_ref, other_ref, modes_ref, hn_ref, cn_ref):
    gram, coef = merged_gram(p_ref, h_ref, c_ref, c_ref.shape[0])
    w = top_rows(gram, odd(level)).astype(jnp.bfloat16)
    wf = w.astype(jnp.float32)
    cn_ref[...] = mmt(coef, wf)
    hn_ref[...] = mmt(mm(wf, gram), wf)
    for i in range(own_ref.shape[0]):
        stacked = jnp.concatenate([own_ref[i], other_ref[i]], axis=0)
        modes_ref[i] = jnp.dot(w, stacked, preferred_element_type=jnp.float32).astype(jnp.bfloat16)


def project_body(level, p_ref, h_ref, c_ref, own_ref, other_ref, o_ref):
    gram, coef = merged_gram(p_ref, h_ref, c_ref, c_ref.shape[0])
    zt = power_basis(gram, odd(level))
    r = whitened(mmt(mm(zt, gram), zt), zt)
    weights = mm(mmt(coef, r), r).astype(jnp.bfloat16)
    for i in range(own_ref.shape[0]):
        stacked = jnp.concatenate([own_ref[i], other_ref[i]], axis=0)
        o_ref[i] = jnp.dot(weights, stacked, preferred_element_type=jnp.float32).astype(jnp.bfloat16)


def exchanged(block, level):
    count = lax.axis_size("tm")
    return lax.ppermute(block, "tm", [(i, i ^ 1 << level) for i in range(count)])


def gathered(parts):
    return lax.all_to_all(parts, ("lat", "lon"), 0, 0, tiled=True)


def shards(residuals, diffusivity):
    snaps, rows, width = residuals.shape
    tiles = lax.axis_size("lat") * lax.axis_size("lon")
    levels = lax.axis_size("tm").bit_length() - 1
    f32 = lambda *shape: jax.ShapeDtypeStruct(shape, jnp.float32)
    b16 = lambda *shape: jax.ShapeDtypeStruct(shape, jnp.bfloat16)
    x = jnp.transpose(residuals, (1, 0, 2))
    y = smooth(x, diffusivity, *halo_exchange(x, diffusivity))
    other = exchanged(y, 0)
    parts = gathered(kernel_call(pair_gram_body, f32(tiles, snaps, 2 * snaps))(y, other))
    gram = jnp.sum(parts, axis=0)
    small = (f32(RANK, RANK), f32(snaps, RANK))
    modes, h, c = kernel_call(leaf_body, (b16(rows, RANK, width),) + small)(
        gram, exchanged(gram, 0), y, other
    )
    for level in range(1, levels):
        other = exchanged(modes, level)
        parts = gathered(kernel_call(cross_body, f32(tiles, RANK, snaps + 2 * RANK))(other, y, modes))
        if level < levels - 1:
            modes, h, c = kernel_call(
                functools.partial(merge_body, level), (b16(rows, RANK, width),) + small
            )(parts, h, c, modes, other)
    out = kernel_call(functools.partial(project_body, levels - 1), b16(rows, snaps, width))(
        parts, h, c, modes, other
    )
    return jnp.transpose(out, (1, 0, 2))


def solution(mesh):
    return jax.shard_map(
        shards,
        mesh=mesh,
        in_specs=(P("tm", "lat", "lon"), P("lat", "lon")),
        out_specs=P("tm", "lat", "lon"),
        check_vma=False,
    )
```

time: 292 us -> 104 us (0.36)
  blocking collectives: 134 us -> 24.5 us
  other arithmetic: 105 us -> 0.04 us
  Pallas kernels: 0 us -> 47.1 us
  matrix products: 12.7 us -> 0 us
  starting transfers between devices: 16.8 us -> 10 us
  local copies, waits for them, and re-layouts: 5.67 us -> 1.86 us
  waiting for transfers between devices: 17 us -> 20 us
    psum x4 -> x0, blocking collectives: 134 us -> none  [the longest x2 66.3 us: shards(): lax.psum(jnp.dot(stacked, stacked.T, preferred_element_type=jnp.float32),...]
    another operation x65 -> x0, other arithmetic: 86.9 us -> none  [the longest x36 43.2 us: orthonormal(): lower = jnp.linalg.cholesky(inner)]
    pallas_call x0 -> x6, Pallas kernels: none -> 47.1 us  [the longest x1 33.4 us: smooth(): kernel_call(smooth_body, jax.ShapeDtypeStruct((rows, snaps, width), jnp.b...]
    all_to_all x0 -> x2, blocking collectives: none -> 24.5 us  [gathered(): return lax.all_to_all(parts, ('lat', 'lon'), 0, 0, tiled=True)]
    mul x7 -> x0, other arithmetic: 13.8 us -> none  [the longest x3 13.3 us: shards(): field_ext = field_ext * inside[None, :, None]]
    dot_general x31 -> x0, matrix products: 9.53 us -> none  [the longest x1 3.52 us: shards(): jnp.dot(weighted, weighted.T, preferred_element_type=jnp.float32)]
    ppermute x10 -> x6, starting transfers between devices: 16.8 us -> 10 us  [the longest x1 4.02 us: halo_exchange(): lax.ppermute(jnp.concatenate([south, side[last:last + 1]]), 'lat', up)]
    another operation x14 -> x0, matrix products: 3.18 us -> none  [the longest x12 2.84 us: orthonormal(): return jax.scipy.linalg.solve_triangular(lower, block.T, lower=True).T]
  transfers between devices with their start and end apart: 10 -> 6, of which waited for: 5 -> 6; matrix products, arithmetic and copies ran while one was open for 1% -> 0% of each run, Pallas kernels for 0% -> 0%
where the time goes in v1:
time: 104 us
  Pallas kernels  47.1 us (45%)
  blocking collectives  24.5 us (24%)
  waiting for transfers between devices  20 us (19%)
  starting transfers between devices  10 us (10%)
  local copies, waits for them, and re-layouts  1.86 us (2%)
    pallas_call x1, Pallas kernels, smooth(): kernel_call(smooth_body, jax.ShapeDtypeStruct((rows, snaps, width), jnp.b...  33.4 us
    all_to_all x2, blocking collectives, gathered(): return lax.all_to_all(parts, ('lat', 'lon'), 0, 0, tiled=True)  24.5 us
    ppermute x3, waiting for transfers between devices, exchanged(): lax.ppermute(block, 'tm', [(i, i ^ 1 << level) for i in range(count)])  12.5 us
    pallas_call x1, Pallas kernels, shards(): kernel_call(leaf_body, (b16(rows, RANK, width),) + small)  7.03 us
    ppermute x1, waiting for transfers between devices, halo_exchange(): from_south = lax.ppermute(jnp.concatenate([north, side[:1]]), 'lat', down)  4.35 us
    pallas_call x1, Pallas kernels, shards(): kernel_call(functools.partial(project_body, levels - 1), b16(rows, snaps,...  4.15 us
    ppermute x1, starting transfers between devices, halo_exchange(): lax.ppermute(jnp.concatenate([south, side[last:last + 1]]), 'lat', up)  4.02 us
    ppermute x1, starting transfers between devices, halo_exchange(): side = lax.ppermute(packed, 'lon', forward)  3 us
  transfers between devices with their start and end apart: 6, of which 6 were waited for; matrix products, arithmetic and copies ran while one was open for 0% of the time, Pallas kernels for 0%

profile of v1, /device:TPU:0, one launch (start us, length us, event | category | flops | bytes accessed | tf_op | source)
XLA Modules:
  0.0 103.6 jit_solution(4692006004897139641)
XLA Ops:
  0.0 0.0 copy-start
  0.0 1.1 %copy-done = bf16[64,45,128]{2,0,1:T(8,128)(2,1)S(1)} copy-done((bf16[64,45,128]{2,0,1:T(8,128)(2,1)S(1)}, bf16[64,45,128]{2,0,1:T(8,128)(2,1)}, u32[]{:S(2)}) %copy-start) | copy-done | bytes 737304
  1.1 0.0 copy-start.1
  1.1 0.7 copy-done.1
  1.9 0.5 shard_map.28
  2.4 3.0 %collective-permute-start = (bf16[3,80,128]{2,1,0:T(8,128)(2,1)S(1)}, bf16[3,80,128]{2,1,0:T(8,128)(2,1)S(1)}, u32[]{:S(2)}, u32[]{:S(2)}) collective-permute-start(bf16[3,80,128]{2,1,0:T(8,128)(2,1)S(1)} %get-tuple-element.11), channel_id=1, source_target_pairs={{0,1},{1,0},{2,3},{3,2},{4,5},{5,4},{6,7},{7,6},{8,9},{9,8},{10,11... | collective-permute-start | bytes 184328 | tf_op jit(solution)/shard_map/ppermute | solution.py:73
  5.4 2.2 %collective-permute-done.side_ref = bf16[3,80,128]{2,1,0:T(8,128)(2,1)S(1)} collective-permute-done((bf16[3,80,128]{2,1,0:T(8,128)(2,1)S(1)}, bf16[3,80,128]{2,1,0:T(8,128)(2,1)S(1)}, u32[]{:S(2)}, u32[]{:S(2)}) %collective-permute-start) | collective-permute-done | bytes 61472 | tf_op jit(solution)/shard_map/ppermute | solution.py:73
  7.6 4.0 %collective-permute-start.1 = (bf16[5,80,128]{2,1,0:T(8,128)(2,1)S(1)}, bf16[5,80,128]{2,1,0:T(8,128)(2,1)S(1)}, u32[]{:S(2)}, u32[]{:S(2)}) collective-permute-start(bf16[5,80,128]{2,1,0:T(8,128)(2,1)S(1)} %pad_maximum_fusion), channel_id=1, source_target_pairs={{0,2},{2,4},{4,6},{1,3},{3,5},{5,7},{8,10},{10,12},{12,14},{9,11},... | collective-permute-start | bytes 307208 | tf_op jit(solution)/shard_map/ppermute | solution.py:80
  11.6 1.3 %collective-permute-start.2 = (bf16[5,80,128]{2,1,0:T(8,128)(2,1)S(1)}, bf16[5,80,128]{2,1,0:T(8,128)(2,1)S(1)}, u32[]{:S(2)}, u32[]{:S(2)}) collective-permute-start(bf16[5,80,128]{2,1,0:T(8,128)(2,1)S(1)} %pad_maximum_fusion.1), channel_id=1, source_target_pairs={{2,0},{4,2},{6,4},{3,1},{5,3},{7,5},{10,8},{12,10},{14,12},{11,9},... | collective-permute-start | bytes 307208 | tf_op jit(solution)/shard_map/ppermute | solution.py:81
  12.9 0.9 collective-permute-done.1.north_ref
  13.9 4.3 %collective-permute-done.2.south_ref = bf16[5,80,128]{2,1,0:T(8,128)(2,1)S(1)} collective-permute-done((bf16[5,80,128]{2,1,0:T(8,128)(2,1)S(1)}, bf16[5,80,128]{2,1,0:T(8,128)(2,1)S(1)}, u32[]{:S(2)}, u32[]{:S(2)}) %collective-permute-start.2) | collective-permute-done | bytes 102432 | tf_op jit(solution)/shard_map/ppermute | solution.py:81
  18.2 33.4 %shard_map.29.own_ref.y_ref = bf16[45,64,128]{2,1,0:T(8,128)(2,1)S(1)} custom-call(bf16[45,64,128]{2,1,0:T(8,128)(2,1)S(1)} %bitcast.3, f32[45,128]{1,0:T(8,128)S(1)} %copy-done.1, bf16[3,80,128]{2,1,0:T(8,128)(2,1)S(1)} %collective-permute-done.side_ref, bf16[5,80,128]{2,1,0:T(8,128)(2,1)S(1)} %collective-permute-done.1.north_ref, ...), custom_call_target="tpu_custom_call" | custom-call | flops 1048576 | bytes 1048576 | tf_op jit(solution)/shard_map/pallas_call | solution.py:207
  51.6 0.1 collective-permute-start.3
  51.7 2.2 %collective-permute-done.3.other_ref = bf16[45,64,128]{2,1,0:T(8,128)(2,1)S(1)} collective-permute-done((bf16[45,64,128]{2,1,0:T(8,128)(2,1)S(1)}, bf16[45,64,128]{2,1,0:T(8,128)(2,1)S(1)}, u32[]{:S(2)}, u32[]{:S(2)}) %collective-permute-start.3) | collective-permute-done | bytes 737312 | tf_op jit(solution)/shard_map/ppermute | solution.py:353
  53.9 1.1 %shard_map.30 = f32[8,64,128]{2,1,0:T(8,128)S(1)} custom-call(bf16[45,64,128]{2,1,0:T(8,128)(2,1)S(1)} %shard_map.29.own_ref.y_ref, bf16[45,64,128]{2,1,0:T(8,128)(2,1)S(1)} %collective-permute-done.3.other_ref), custom_call_target="tpu_custom_call" | custom-call | flops 1048576 | bytes 1048576 | tf_op jit(solution)/shard_map/pallas_call | solution.py:369
  55.0 13.8 %all_to_all.10 = f32[8,64,128]{2,1,0:T(8,128)S(1)} all-to-all(f32[8,64,128]{2,1,0:T(8,128)S(1)} %shard_map.30), channel_id=1, replica_groups=mesh['tm'=4,'lat'=4,'lon'=2] {'lat','lon'}, dimensions={0} | all-to-all | bytes 524288 | tf_op jit(solution)/shard_map/all_to_all | solution.py:357
  68.8 0.1 collective-permute-start.4
  68.9 1.2 %collective-permute-done.4.gp_ref = f32[64,128]{1,0:T(8,128)S(1)} collective-permute-done((f32[64,128]{1,0:T(8,128)S(1)}, f32[64,128]{1,0:T(8,128)S(1)}, u32[]{:S(2)}, u32[]{:S(2)}) %collective-permute-start.4) | collective-permute-done | bytes 32800 | tf_op jit(solution)/shard_map/ppermute | solution.py:353
  70.1 7.0 %shard_map.31 = (bf16[45,32,128]{2,1,0:T(8,128)(2,1)S(1)}, f32[32,32]{1,0:T(8,128)S(1)}, f32[64,32]{1,0:T(8,128)S(1)}) custom-call(f32[64,128]{1,0:T(8,128)S(1)} %reduce_sum.9.g_ref, f32[64,128]{1,0:T(8,128)S(1)} %collective-permute-done.4.gp_ref, bf16[45,64,128]{2,1,0:T(8,128)(2,1)S(1)} %shard_map.29.own_ref.y_ref, ...), custom_call_target="tpu_custom_call" | custom-call | flops 1048576 | bytes 1048576 | tf_op jit(solution)/shard_map/pallas_call | solution.py:372
  77.1 1.6 %collective-permute-start.5 = (bf16[45,32,128]{2,1,0:T(8,128)(2,1)S(1)}, bf16[45,32,128]{2,1,0:T(8,128)(2,1)S(1)}, u32[]{:S(2)}, u32[]{:S(2)}) collective-permute-start(bf16[45,32,128]{2,1,0:T(8,128)(2,1)S(1)} %get-tuple-element.14.own_ref), channel_id=1, source_target_pairs={{0,16},{8,24},{16,0},{24,8},{1,17},{9,25},{17,1},{25,9},{2,18},{10... | collective-permute-start | bytes 1105928 | tf_op jit(solution)/shard_map/ppermute | solution.py:353
  78.7 9.1 %collective-permute-done.5.other_ref = bf16[45,32,128]{2,1,0:T(8,128)(2,1)S(1)} collective-permute-done((bf16[45,32,128]{2,1,0:T(8,128)(2,1)S(1)}, bf16[45,32,128]{2,1,0:T(8,128)(2,1)S(1)}, u32[]{:S(2)}, u32[]{:S(2)}) %collective-permute-start.5) | collective-permute-done | bytes 368672 | tf_op jit(solution)/shard_map/ppermute | solution.py:353
  87.8 0.9 shard_map.32
  88.8 10.7 %all_to_all.11.p_ref = f32[8,32,128]{2,1,0:T(8,128)S(1)} all-to-all(f32[8,32,128]{2,1,0:T(8,128)S(1)} %shard_map.32), channel_id=1, replica_groups=mesh['tm'=4,'lat'=4,'lon'=2] {'lat','lon'}, dimensions={0} | all-to-all | bytes 262144 | tf_op jit(solution)/shard_map/all_to_all | solution.py:357
  99.5 4.2 %shard_map.33 = bf16[45,64,128]{2,1,0:T(8,128)(2,1)} custom-call(f32[8,32,128]{2,1,0:T(8,128)S(1)} %all_to_all.11.p_ref, f32[32,32]{1,0:T(8,128)S(1)} %get-tuple-element.15.h_ref, f32[64,32]{1,0:T(8,128)S(1)} %get-tuple-element.16.c_ref, bf16[45,32,128]{2,1,0:T(8,128)(2,1)S(1)} %get-tuple-element.14.own_ref, ...), custom_call_target="tpu_custom_call" | custom-call | flops 1048576 | bytes 1048576 | tf_op jit(solution)/shard_map/pallas_call | solution.py:382
  (4 shorter events, 0.0 us)
Async XLA Ops:
  0.0 1.1 %copy-start = (bf16[64,45,128]{2,0,1:T(8,128)(2,1)S(1)}, bf16[64,45,128]{2,0,1:T(8,128)(2,1)}, u32[]{:S(2)}) copy-start(bf16[64,45,128]{2,0,1:T(8,128)(2,1)} %param.2) | copy-start | bytes 2211844
  1.1 0.7 copy-start.1
  2.4 5.2 %collective-permute-start = (bf16[3,80,128]{2,1,0:T(8,128)(2,1)S(1)}, bf16[3,80,128]{2,1,0:T(8,128)(2,1)S(1)}, u32[]{:S(2)}, u32[]{:S(2)}) collective-permute-start(bf16[3,80,128]{2,1,0:T(8,128)(2,1)S(1)} %get-tuple-element.11), channel_id=1, source_target_pairs={{0,1},{1,0},{2,3},{3,2},{4,5},{5,4},{6,7},{7,6},{8,9},{9,8},{10,11... | collective-permute-start | bytes 184328 | tf_op jit(solution)/shard_map/ppermute | solution.py:73
  7.6 6.3 %collective-permute-start.1 = (bf16[5,80,128]{2,1,0:T(8,128)(2,1)S(1)}, bf16[5,80,128]{2,1,0:T(8,128)(2,1)S(1)}, u32[]{:S(2)}, u32[]{:S(2)}) collective-permute-start(bf16[5,80,128]{2,1,0:T(8,128)(2,1)S(1)} %pad_maximum_fusion), channel_id=1, source_target_pairs={{0,2},{2,4},{4,6},{1,3},{3,5},{5,7},{8,10},{10,12},{12,14},{9,11},... | collective-permute-start | bytes 307208 | tf_op jit(solution)/shard_map/ppermute | solution.py:80
  11.6 6.6 %collective-permute-start.2 = (bf16[5,80,128]{2,1,0:T(8,128)(2,1)S(1)}, bf16[5,80,128]{2,1,0:T(8,128)(2,1)S(1)}, u32[]{:S(2)}, u32[]{:S(2)}) collective-permute-start(bf16[5,80,128]{2,1,0:T(8,128)(2,1)S(1)} %pad_maximum_fusion.1), channel_id=1, source_target_pairs={{2,0},{4,2},{6,4},{3,1},{5,3},{7,5},{10,8},{12,10},{14,12},{11,9},... | collective-permute-start | bytes 307208 | tf_op jit(solution)/shard_map/ppermute | solution.py:81
  51.6 2.3 %collective-permute-start.3 = (bf16[45,64,128]{2,1,0:T(8,128)(2,1)S(1)}, bf16[45,64,128]{2,1,0:T(8,128)(2,1)S(1)}, u32[]{:S(2)}, u32[]{:S(2)}) collective-permute-start(bf16[45,64,128]{2,1,0:T(8,128)(2,1)S(1)} %shard_map.29.own_ref.y_ref), channel_id=1, source_target_pairs={{0,8},{8,0},{16,24},{24,16},{1,9},{9,1},{17,25},{25,17},{2,10},{10... | collective-permute-start | bytes 2211848 | tf_op jit(solution)/shard_map/ppermute | solution.py:353
  68.8 1.3 %collective-permute-start.4 = (f32[64,128]{1,0:T(8,128)S(1)}, f32[64,128]{1,0:T(8,128)S(1)}, u32[]{:S(2)}, u32[]{:S(2)}) collective-permute-start(f32[64,128]{1,0:T(8,128)S(1)} %reduce_sum.9.g_ref), channel_id=1, source_target_pairs={{0,8},{8,0},{16,24},{24,16},{1,9},{9,1},{17,25},{25,17},{2,10},{10... | collective-permute-start | bytes 98312 | tf_op jit(solution)/shard_map/ppermute | solution.py:353
  77.1 10.7 %collective-permute-start.5 = (bf16[45,32,128]{2,1,0:T(8,128)(2,1)S(1)}, bf16[45,32,128]{2,1,0:T(8,128)(2,1)S(1)}, u32[]{:S(2)}, u32[]{:S(2)}) collective-permute-start(bf16[45,32,128]{2,1,0:T(8,128)(2,1)S(1)} %get-tuple-element.14.own_ref), channel_id=1, source_target_pairs={{0,16},{8,24},{16,0},{24,8},{1,17},{9,25},{17,1},{25,9},{2,18},{10... | collective-permute-start | bytes 1105928 | tf_op jit(solution)/shard_map/ppermute | solution.py:353

commit v2 on v1

--- a/solution.py
+++ b/solution.py
@@ -12,6 +12,7 @@
 PASSES = 4
 LANES = 128
 MSG = 80
+BATCH = 60
 SEG = 32
 exact = lax.Precision.HIGHEST
 VMEM = pltpu.VMEM
@@ -150,8 +151,10 @@
         current, above = carry
         below = field[e + 1]
         south = south_c[pl.ds(e, 1), :] * (below - current)
-        east = east_c[pl.ds(e, 1), :] * (roll(current, -1) - current)
-        fresh = current + ((south - above) + (east - roll(east, 1)))
+        east_face = east_c[pl.ds(e, 1), :]
+        east = east_face * (roll(current, -1) - current)
+        west = roll(east_face, 1) * (current - roll(current, 1))
+        fresh = current + ((south - above) + (east - west))
         return fresh, (below, south)
 
     def entry(field, e, south_c):
@@ -161,7 +164,7 @@
     for step in range(PASSES):
         final = step == PASSES - 1
 
-        def body(e, carry):
+        def one(e, carry):
             main, edge = carry
             fresh, main = updated(u, e, main, cs, ce)
             fresh_edge, edge = updated(s, e, edge, ss, se)
@@ -183,8 +186,15 @@
                 y_ref[i] = merged.astype(jnp.bfloat16)
             return main, edge
 
-        start = step + 1
-        lax.fori_loop(start, ext - 1 - step, body, (entry(u, start, cs), entry(s, start, ss)))
+        start, stop = (PASSES, ext - PASSES) if final else (1, ext - 1)
+        batch = max(b for b in range(1, BATCH + 1) if (stop - start) % b == 0)
+
+        def body(t, carry):
+            for r in range(batch):
+                carry = one(start + t * batch + r, carry)
+            return carry
+
+        lax.fori_loop(0, (stop - start) // batch, body, (entry(u, start, cs), entry(s, start, ss)))
         if not final:
 
             @pl.when(lat == 0)

time: 104 us -> 79.9 us (0.77)
  Pallas kernels: 47.1 us -> 23 us
    pallas_call x1, Pallas kernels: 33.4 us -> 9.35 us  [smooth(): kernel_call(smooth_body, jax.ShapeDtypeStruct((rows, snaps, width), jnp.b...]
where the time goes in v2:
time: 79.9 us; the launch traced here: 79.6 us
  blocking collectives  24.5 us (31%)
  Pallas kernels  23 us (29%)
  waiting for transfers between devices  20 us (25%)
  starting transfers between devices  10 us (13%)
  local copies, waits for them, and re-layouts  1.86 us (2%)
    all_to_all x2, blocking collectives, gathered(): return lax.all_to_all(parts, ('lat', 'lon'), 0, 0, tiled=True)  24.5 us
    ppermute x3, waiting for transfers between devices, exchanged(): lax.ppermute(block, 'tm', [(i, i ^ 1 << level) for i in range(count)])  12.5 us
    pallas_call x1, Pallas kernels, smooth(): kernel_call(smooth_body, jax.ShapeDtypeStruct((rows, snaps, width), jnp.b...  9.35 us
    pallas_call x1, Pallas kernels, shards(): kernel_call(leaf_body, (b16(rows, RANK, width),) + small)  7.03 us
    ppermute x1, waiting for transfers between devices, halo_exchange(): from_south = lax.ppermute(jnp.concatenate([north, side[:1]]), 'lat', down)  4.35 us
    pallas_call x1, Pallas kernels, shards(): kernel_call(functools.partial(project_body, levels - 1), b16(rows, snaps,...  4.15 us
    ppermute x1, starting transfers between devices, halo_exchange(): lax.ppermute(jnp.concatenate([south, side[last:last + 1]]), 'lat', up)  4.02 us
    ppermute x1, starting transfers between devices, halo_exchange(): side = lax.ppermute(packed, 'lon', forward)  3 us
  transfers between devices with their start and end apart: 6, of which 6 were waited for; matrix products, arithmetic and copies ran while one was open for 0% of the time, Pallas kernels for 0%

profile of v2, /device:TPU:0, one launch (start us, length us, event | category | flops | bytes accessed | tf_op | source)
XLA Modules:
  0.0 79.6 jit_solution(1142867106228257049)
XLA Ops:
  0.0 0.0 copy-start
  0.0 1.1 %copy-done = bf16[64,45,128]{2,0,1:T(8,128)(2,1)S(1)} copy-done((bf16[64,45,128]{2,0,1:T(8,128)(2,1)S(1)}, bf16[64,45,128]{2,0,1:T(8,128)(2,1)}, u32[]{:S(2)}) %copy-start) | copy-done | bytes 737304
  1.1 0.0 copy-start.1
  1.1 0.7 copy-done.1
  1.9 0.5 shard_map.28
  2.4 3.0 %collective-permute-start = (bf16[3,80,128]{2,1,0:T(8,128)(2,1)S(1)}, bf16[3,80,128]{2,1,0:T(8,128)(2,1)S(1)}, u32[]{:S(2)}, u32[]{:S(2)}) collective-permute-start(bf16[3,80,128]{2,1,0:T(8,128)(2,1)S(1)} %get-tuple-element.11), channel_id=1, source_target_pairs={{0,1},{1,0},{2,3},{3,2},{4,5},{5,4},{6,7},{7,6},{8,9},{9,8},{10,11... | collective-permute-start | bytes 184328 | tf_op jit(solution)/shard_map/ppermute | solution.py:74
  5.4 2.2 %collective-permute-done.side_ref = bf16[3,80,128]{2,1,0:T(8,128)(2,1)S(1)} collective-permute-done((bf16[3,80,128]{2,1,0:T(8,128)(2,1)S(1)}, bf16[3,80,128]{2,1,0:T(8,128)(2,1)S(1)}, u32[]{:S(2)}, u32[]{:S(2)}) %collective-permute-start) | collective-permute-done | bytes 61472 | tf_op jit(solution)/shard_map/ppermute | solution.py:74
  7.6 4.0 %collective-permute-start.1 = (bf16[5,80,128]{2,1,0:T(8,128)(2,1)S(1)}, bf16[5,80,128]{2,1,0:T(8,128)(2,1)S(1)}, u32[]{:S(2)}, u32[]{:S(2)}) collective-permute-start(bf16[5,80,128]{2,1,0:T(8,128)(2,1)S(1)} %pad_maximum_fusion), channel_id=1, source_target_pairs={{0,2},{2,4},{4,6},{1,3},{3,5},{5,7},{8,10},{10,12},{12,14},{9,11},... | collective-permute-start | bytes 307208 | tf_op jit(solution)/shard_map/ppermute | solution.py:81
  11.6 1.3 %collective-permute-start.2 = (bf16[5,80,128]{2,1,0:T(8,128)(2,1)S(1)}, bf16[5,80,128]{2,1,0:T(8,128)(2,1)S(1)}, u32[]{:S(2)}, u32[]{:S(2)}) collective-permute-start(bf16[5,80,128]{2,1,0:T(8,128)(2,1)S(1)} %pad_maximum_fusion.1), channel_id=1, source_target_pairs={{2,0},{4,2},{6,4},{3,1},{5,3},{7,5},{10,8},{12,10},{14,12},{11,9},... | collective-permute-start | bytes 307208 | tf_op jit(solution)/shard_map/ppermute | solution.py:82
  12.9 0.9 %collective-permute-done.1.north_ref = bf16[5,80,128]{2,1,0:T(8,128)(2,1)S(1)} collective-permute-done((bf16[5,80,128]{2,1,0:T(8,128)(2,1)S(1)}, bf16[5,80,128]{2,1,0:T(8,128)(2,1)S(1)}, u32[]{:S(2)}, u32[]{:S(2)}) %collective-permute-start.1) | collective-permute-done | bytes 102432 | tf_op jit(solution)/shard_map/ppermute | solution.py:81
  13.9 4.3 %collective-permute-done.2.south_ref = bf16[5,80,128]{2,1,0:T(8,128)(2,1)S(1)} collective-permute-done((bf16[5,80,128]{2,1,0:T(8,128)(2,1)S(1)}, bf16[5,80,128]{2,1,0:T(8,128)(2,1)S(1)}, u32[]{:S(2)}, u32[]{:S(2)}) %collective-permute-start.2) | collective-permute-done | bytes 102432 | tf_op jit(solution)/shard_map/ppermute | solution.py:82
  18.2 9.3 %shard_map.29.own_ref.y_ref = bf16[45,64,128]{2,1,0:T(8,128)(2,1)S(1)} custom-call(bf16[45,64,128]{2,1,0:T(8,128)(2,1)S(1)} %bitcast.3, f32[45,128]{1,0:T(8,128)S(1)} %copy-done.1, bf16[3,80,128]{2,1,0:T(8,128)(2,1)S(1)} %collective-permute-done.side_ref, bf16[5,80,128]{2,1,0:T(8,128)(2,1)S(1)} %collective-permute-done.1.north_ref, ...), custom_call_target="tpu_custom_call" | custom-call | flops 1048576 | bytes 1048576 | tf_op jit(solution)/shard_map/pallas_call | solution.py:217
  27.6 0.1 collective-permute-start.3
  27.6 2.2 %collective-permute-done.3.other_ref = bf16[45,64,128]{2,1,0:T(8,128)(2,1)S(1)} collective-permute-done((bf16[45,64,128]{2,1,0:T(8,128)(2,1)S(1)}, bf16[45,64,128]{2,1,0:T(8,128)(2,1)S(1)}, u32[]{:S(2)}, u32[]{:S(2)}) %collective-permute-start.3) | collective-permute-done | bytes 737312 | tf_op jit(solution)/shard_map/ppermute | solution.py:363
  29.8 1.1 %shard_map.30 = f32[8,64,128]{2,1,0:T(8,128)S(1)} custom-call(bf16[45,64,128]{2,1,0:T(8,128)(2,1)S(1)} %shard_map.29.own_ref.y_ref, bf16[45,64,128]{2,1,0:T(8,128)(2,1)S(1)} %collective-permute-done.3.other_ref), custom_call_target="tpu_custom_call" | custom-call | flops 1048576 | bytes 1048576 | tf_op jit(solution)/shard_map/pallas_call | solution.py:379
  30.9 13.8 %all_to_all.10 = f32[8,64,128]{2,1,0:T(8,128)S(1)} all-to-all(f32[8,64,128]{2,1,0:T(8,128)S(1)} %shard_map.30), channel_id=1, replica_groups=mesh['tm'=4,'lat'=4,'lon'=2] {'lat','lon'}, dimensions={0} | all-to-all | bytes 524288 | tf_op jit(solution)/shard_map/all_to_all | solution.py:367
  44.8 0.1 collective-permute-start.4
  44.8 1.2 %collective-permute-done.4.gp_ref = f32[64,128]{1,0:T(8,128)S(1)} collective-permute-done((f32[64,128]{1,0:T(8,128)S(1)}, f32[64,128]{1,0:T(8,128)S(1)}, u32[]{:S(2)}, u32[]{:S(2)}) %collective-permute-start.4) | collective-permute-done | bytes 32800 | tf_op jit(solution)/shard_map/ppermute | solution.py:363
  46.0 7.0 %shard_map.31 = (bf16[45,32,128]{2,1,0:T(8,128)(2,1)S(1)}, f32[32,32]{1,0:T(8,128)S(1)}, f32[64,32]{1,0:T(8,128)S(1)}) custom-call(f32[64,128]{1,0:T(8,128)S(1)} %reduce_sum.9.g_ref, f32[64,128]{1,0:T(8,128)S(1)} %collective-permute-done.4.gp_ref, bf16[45,64,128]{2,1,0:T(8,128)(2,1)S(1)} %shard_map.29.own_ref.y_ref, ...), custom_call_target="tpu_custom_call" | custom-call | flops 1048576 | bytes 1048576 | tf_op jit(solution)/shard_map/pallas_call | solution.py:382
  53.1 1.6 %collective-permute-start.5 = (bf16[45,32,128]{2,1,0:T(8,128)(2,1)S(1)}, bf16[45,32,128]{2,1,0:T(8,128)(2,1)S(1)}, u32[]{:S(2)}, u32[]{:S(2)}) collective-permute-start(bf16[45,32,128]{2,1,0:T(8,128)(2,1)S(1)} %get-tuple-element.14.own_ref), channel_id=1, source_target_pairs={{0,16},{8,24},{16,0},{24,8},{1,17},{9,25},{17,1},{25,9},{2,18},{10... | collective-permute-start | bytes 1105928 | tf_op jit(solution)/shard_map/ppermute | solution.py:363
  54.6 9.1 %collective-permute-done.5.other_ref = bf16[45,32,128]{2,1,0:T(8,128)(2,1)S(1)} collective-permute-done((bf16[45,32,128]{2,1,0:T(8,128)(2,1)S(1)}, bf16[45,32,128]{2,1,0:T(8,128)(2,1)S(1)}, u32[]{:S(2)}, u32[]{:S(2)}) %collective-permute-start.5) | collective-permute-done | bytes 368672 | tf_op jit(solution)/shard_map/ppermute | solution.py:363
  63.8 0.9 %shard_map.32 = f32[8,32,128]{2,1,0:T(8,128)S(1)} custom-call(bf16[45,32,128]{2,1,0:T(8,128)(2,1)S(1)} %collective-permute-done.5.other_ref, bf16[45,64,128]{2,1,0:T(8,128)(2,1)S(1)} %shard_map.29.own_ref.y_ref, bf16[45,32,128]{2,1,0:T(8,128)(2,1)S(1)} %get-tuple-element.14.own_ref), custom_call_target="tpu_custom_call" | custom-call | flops 1048576 | bytes 1048576 | tf_op jit(solution)/shard_map/pallas_call | solution.py:387
  64.7 10.7 %all_to_all.11.p_ref = f32[8,32,128]{2,1,0:T(8,128)S(1)} all-to-all(f32[8,32,128]{2,1,0:T(8,128)S(1)} %shard_map.32), channel_id=1, replica_groups=mesh['tm'=4,'lat'=4,'lon'=2] {'lat','lon'}, dimensions={0} | all-to-all | bytes 262144 | tf_op jit(solution)/shard_map/all_to_all | solution.py:367
  75.4 4.2 %shard_map.33 = bf16[45,64,128]{2,1,0:T(8,128)(2,1)} custom-call(f32[8,32,128]{2,1,0:T(8,128)S(1)} %all_to_all.11.p_ref, f32[32,32]{1,0:T(8,128)S(1)} %get-tuple-element.15.h_ref, f32[64,32]{1,0:T(8,128)S(1)} %get-tuple-element.16.c_ref, bf16[45,32,128]{2,1,0:T(8,128)(2,1)S(1)} %get-tuple-element.14.own_ref, ...), custom_call_target="tpu_custom_call" | custom-call | flops 1048576 | bytes 1048576 | tf_op jit(solution)/shard_map/pallas_call | solution.py:392
  (4 shorter events, 0.0 us)
Async XLA Ops:
  0.0 1.1 %copy-start = (bf16[64,45,128]{2,0,1:T(8,128)(2,1)S(1)}, bf16[64,45,128]{2,0,1:T(8,128)(2,1)}, u32[]{:S(2)}) copy-start(bf16[64,45,128]{2,0,1:T(8,128)(2,1)} %param.2) | copy-start | bytes 2211844
  1.1 0.7 copy-start.1
  2.4 5.2 %collective-permute-start = (bf16[3,80,128]{2,1,0:T(8,128)(2,1)S(1)}, bf16[3,80,128]{2,1,0:T(8,128)(2,1)S(1)}, u32[]{:S(2)}, u32[]{:S(2)}) collective-permute-start(bf16[3,80,128]{2,1,0:T(8,128)(2,1)S(1)} %get-tuple-element.11), channel_id=1, source_target_pairs={{0,1},{1,0},{2,3},{3,2},{4,5},{5,4},{6,7},{7,6},{8,9},{9,8},{10,11... | collective-permute-start | bytes 184328 | tf_op jit(solution)/shard_map/ppermute | solution.py:74
  7.6 6.3 %collective-permute-start.1 = (bf16[5,80,128]{2,1,0:T(8,128)(2,1)S(1)}, bf16[5,80,128]{2,1,0:T(8,128)(2,1)S(1)}, u32[]{:S(2)}, u32[]{:S(2)}) collective-permute-start(bf16[5,80,128]{2,1,0:T(8,128)(2,1)S(1)} %pad_maximum_fusion), channel_id=1, source_target_pairs={{0,2},{2,4},{4,6},{1,3},{3,5},{5,7},{8,10},{10,12},{12,14},{9,11},... | collective-permute-start | bytes 307208 | tf_op jit(solution)/shard_map/ppermute | solution.py:81
  11.6 6.6 %collective-permute-start.2 = (bf16[5,80,128]{2,1,0:T(8,128)(2,1)S(1)}, bf16[5,80,128]{2,1,0:T(8,128)(2,1)S(1)}, u32[]{:S(2)}, u32[]{:S(2)}) collective-permute-start(bf16[5,80,128]{2,1,0:T(8,128)(2,1)S(1)} %pad_maximum_fusion.1), channel_id=1, source_target_pairs={{2,0},{4,2},{6,4},{3,1},{5,3},{7,5},{10,8},{12,10},{14,12},{11,9},... | collective-permute-start | bytes 307208 | tf_op jit(solution)/shard_map/ppermute | solution.py:82
  27.6 2.3 %collective-permute-start.3 = (bf16[45,64,128]{2,1,0:T(8,128)(2,1)S(1)}, bf16[45,64,128]{2,1,0:T(8,128)(2,1)S(1)}, u32[]{:S(2)}, u32[]{:S(2)}) collective-permute-start(bf16[45,64,128]{2,1,0:T(8,128)(2,1)S(1)} %shard_map.29.own_ref.y_ref), channel_id=1, source_target_pairs={{0,8},{8,0},{16,24},{24,16},{1,9},{9,1},{17,25},{25,17},{2,10},{10... | collective-permute-start | bytes 2211848 | tf_op jit(solution)/shard_map/ppermute | solution.py:363
  44.8 1.3 %collective-permute-start.4 = (f32[64,128]{1,0:T(8,128)S(1)}, f32[64,128]{1,0:T(8,128)S(1)}, u32[]{:S(2)}, u32[]{:S(2)}) collective-permute-start(f32[64,128]{1,0:T(8,128)S(1)} %reduce_sum.9.g_ref), channel_id=1, source_target_pairs={{0,8},{8,0},{16,24},{24,16},{1,9},{9,1},{17,25},{25,17},{2,10},{10... | collective-permute-start | bytes 98312 | tf_op jit(solution)/shard_map/ppermute | solution.py:363
  53.1 10.7 %collective-permute-start.5 = (bf16[45,32,128]{2,1,0:T(8,128)(2,1)S(1)}, bf16[45,32,128]{2,1,0:T(8,128)(2,1)S(1)}, u32[]{:S(2)}, u32[]{:S(2)}) collective-permute-start(bf16[45,32,128]{2,1,0:T(8,128)(2,1)S(1)} %get-tuple-element.14.own_ref), channel_id=1, source_target_pairs={{0,16},{8,24},{16,0},{24,8},{1,17},{9,25},{17,1},{25,9},{2,18},{10... | collective-permute-start | bytes 1105928 | tf_op jit(solution)/shard_map/ppermute | solution.py:363

commit v3 on v1

--- a/solution.py
+++ b/solution.py
@@ -11,8 +11,6 @@
 RANK = 32
 PASSES = 4
 LANES = 128
-MSG = 80
-SEG = 32
 exact = lax.Precision.HIGHEST
 VMEM = pltpu.VMEM
 
@@ -40,175 +38,208 @@
     return pltpu.roll(x, shift % LANES, x.ndim - 1)
 
 
-def pack_body(x_ref, d_ref, m_ref, north_ref, south_ref):
-    rows = x_ref.shape[0]
-    snaps = x_ref.shape[1]
-    lane = lane_iota((1, LANES))
-    pad = jnp.zeros((MSG - snaps - 2, LANES), jnp.float32)
-
-    def plane(i):
-        d = d_ref[i : i + 1, :]
-        high = d.astype(jnp.bfloat16).astype(jnp.float32)
-        return jnp.concatenate([x_ref[i].astype(jnp.float32), high, d - high, pad], axis=0)
-
-    for p in range(m_ref.shape[0]):
-        acc = jnp.zeros((MSG, LANES), jnp.float32)
-        for q in range(min(16, rows - 16 * p)):
-            v = plane(16 * p + q)
-            acc = jnp.where((lane >= 8 * q) & (lane < 8 * q + 4), roll(v, 8 * q), acc)
-            acc = jnp.where((lane >= 8 * q + 4) & (lane < 8 * q + 8), roll(v, 8 * q + 8), acc)
-        m_ref[p] = acc.astype(jnp.bfloat16)
-    for r in range(PASSES):
-        north_ref[r] = plane(r).astype(jnp.bfloat16)
-        south_ref[r] = plane(rows - PASSES + r).astype(jnp.bfloat16)
+def eye(n, dtype=jnp.bfloat16):
+    row = lax.broadcasted_iota(jnp.int32, (n, n), 0)
+    return (row == lax.broadcasted_iota(jnp.int32, (n, n), 1)).astype(dtype)
+
+
+def dot_t(a, b):
+    return lax.dot_general(a, b, (((1,), (1,)), ((), ())), preferred_element_type=jnp.float32)
+
+
+def split2(v):
+    high = v.astype(jnp.bfloat16)
+    return high, (v - high.astype(jnp.float32)).astype(jnp.bfloat16)
+
+
+def even_lat():
+    return lax.axis_index("lat") % 2 == 0
+
+
+def pack_body(x_ref, d_ref, m_ref, a_ref, b_ref):
+    rows, snaps, width = x_ref.shape
+    half = -(-rows // 2)
+    row = lax.broadcasted_iota(jnp.int32, (16, width), 0)
+    lane = lane_iota((16, width))
+    column = jnp.where(row % 8 < PASSES, row % 8, width - 8 + row % 8)
+    pick = [((lane == column) & (row // 8 == k)).astype(jnp.bfloat16) for k in range(2)]
+
+    def tile(t):
+        return jnp.concatenate([x_ref[t], x_ref[t + rows - half]], axis=0)
+
+    for t in range(0, half, 2):
+        out = dot_t(pick[0], tile(t))
+        if t + 1 < half:
+            out = out + dot_t(pick[1], tile(t + 1))
+        m_ref[8 * t : 8 * t + 16, :] = out.astype(jnp.bfloat16)
+    d = d_ref[...]
+    high, low = split2(jnp.concatenate([d, jnp.zeros((width - rows, width), jnp.float32)], axis=0))
+    end = m_ref.shape[0]
+    m_ref[end - 16 :, :] = (dot_t(pick[0], high) + dot_t(pick[1], low)).astype(jnp.bfloat16)
+
+    even = even_lat()
+    pad = jnp.zeros((8, width), jnp.float32)
+    edge = lambda lo: [v.astype(jnp.float32) for v in split2(d[lo : lo + PASSES])]
+    first, final = edge(0), edge(rows - PASSES)
+    for ref, south in ((a_ref, even), (b_ref, jnp.logical_not(even))):
+        start = jnp.where(south, rows - PASSES, 0)
+        for r in range(PASSES):
+            ref[r * snaps : (r + 1) * snaps, :] = x_ref[start + r]
+        term = [jnp.where(south, f, g) for f, g in zip(final, first)]
+        ref[PASSES * snaps :, :] = jnp.concatenate(term + [pad], axis=0).astype(jnp.bfloat16)
 
 
 def halo_exchange(x, d):
-    rows = x.shape[0]
-    planes = -(-rows // 16)
-    shape = lambda n: jax.ShapeDtypeStruct((n, MSG, LANES), jnp.bfloat16)
-    packed, north, south = kernel_call(pack_body, (shape(planes), shape(PASSES), shape(PASSES)))(x, d)
+    rows, snaps, width = x.shape
+    half = -(-rows // 2)
+    tiles = 16 * (-(-half // 2))
+    shape = lambda n: jax.ShapeDtypeStruct((n, width), jnp.bfloat16)
+    edge = PASSES * snaps + 16
+    packed, a, b = kernel_call(pack_body, (shape(tiles + 16), shape(edge), shape(edge)))(x, d)
     lons, lats = lax.axis_size("lon"), lax.axis_size("lat")
     forward = [(i, (i + 1) % lons) for i in range(lons)]
     side = lax.ppermute(packed, "lon", forward)
     if lons > 2:
-        from_east = lax.ppermute(packed, "lon", [(b, a) for a, b in forward])
-        side = jnp.where(lane_iota((1, 1, LANES)) % 8 < 4, from_east, side)
-    up = [(i, i + 1) for i in range(lats - 1)]
-    down = [(b, a) for a, b in up]
-    last = (rows - PASSES) // 16
-    from_north = lax.ppermute(jnp.concatenate([south, side[last : last + 1]]), "lat", up)
-    from_south = lax.ppermute(jnp.concatenate([north, side[:1]]), "lat", down)
-    return side, from_north, from_south
-
-
-def smooth_body(x_ref, d_ref, side_ref, north_ref, south_ref, y_ref, u, s, dm, ds, ce, cs, se, ss, scale):
-    rows, snaps, _ = x_ref.shape
-    lats = lax.axis_size("lat")
-    lat = lax.axis_index("lat")
-    ext = rows + 2 * PASSES
+        from_east = lax.ppermute(packed, "lon", [(j, i) for i, j in forward])
+        side = jnp.where(lax.broadcasted_iota(jnp.int32, side.shape, 0) % 8 < PASSES, from_east, side)
+    even = even_lat()
+    corner = 8 * PASSES
+    north_corner, south_corner = side[:corner], side[8 * (half - PASSES) : 8 * half]
+
+    def swapped(base, south, start):
+        message = jnp.concatenate([base, jnp.where(south, south_corner, north_corner), side[tiles:]])
+        pairs = [(i, i + 1) for i in range(start, lats - 1, 2)]
+        return lax.ppermute(message, "lat", pairs + [(j, i) for i, j in pairs])
+
+    return side, swapped(a, even, 0), swapped(b, jnp.logical_not(even), 1)
+
+
+PADDED = 160
+
+
+def smooth_body(x_ref, d_ref, side_ref, a_ref, b_ref, y_ref, u0, u1, ce, cs, dn, dt):
+    rows, snaps, width = x_ref.shape
+    half = -(-rows // 2)
+    shift = rows - half
+    count = half + 2 * PASSES
+    lats, lat = lax.axis_size("lat"), lax.axis_index("lat")
+    even = even_lat()
     lane = lane_iota((1, LANES))
-    groups = snaps // 8
-    last_q = (rows - PASSES) % 16
-
-    def halo(e, lo, hi):
-        if e < PASSES:
-            ref, p, q = north_ref, PASSES, last_q + e
-        elif e < rows + PASSES:
-            ref, p, q = side_ref, (e - PASSES) // 16, (e - PASSES) % 16
+    left = lane < snaps
+    own = 16
+    east = own + width
+    unit = eye(width)
+    edge = PASSES * snaps
+    corner = edge + 16
+    tail = corner + 8 * PASSES
+    tiles = side_ref.shape[0] - 16
+
+    def picked(lo, hi):
+        a, b = a_ref[lo:hi, :], b_ref[lo:hi, :]
+        return jnp.where(even, b, a), jnp.where(even, a, b)
+
+    north, south = picked(0, edge)
+    north_corner, south_corner = (v.astype(jnp.float32) for v in picked(corner, tail))
+    north_d, south_d = (v.astype(jnp.float32) for v in picked(edge, corner))
+    north_t, south_t = (v.astype(jnp.float32) for v in picked(tail, tail + 16))
+    side = lambda t: side_ref[16 * (t // 2) : 16 * (t // 2) + 16, :].astype(jnp.float32)[
+        8 * (t % 2) : 8 * (t % 2) + 8
+    ]
+
+    for k in range(count):
+        t = k - PASSES
+        first = north[k * snaps : (k + 1) * snaps] if t < 0 else x_ref[t]
+        r = t + shift
+        second = x_ref[r] if r < rows else south[(r - rows) * snaps : (r - rows + 1) * snaps]
+        u0[k, own:east, :] = dot_t(unit, jnp.concatenate([first, second], axis=0))
+        if t < 0:
+            halo = roll(jnp.where(left, side(r), north_corner[8 * k : 8 * k + 8]), snaps)
+        elif t >= half:
+            j = t - half
+            halo = roll(jnp.where(left, south_corner[8 * j : 8 * j + 8], side(t - shift)), snaps)
         else:
-            ref, p, q = south_ref, PASSES, e - rows - PASSES
-        return ref[p, lo:hi, :], q
-
-    def in_strip(shape_lane, own_high, own_low, edge):
-        at = shape_lane % SEG
-        return jnp.where(at < 12, own_high, jnp.where(at < 20, edge, own_low))
-
-    u[PASSES : PASSES + rows] = x_ref[...].astype(jnp.float32)
-    dm[PASSES : PASSES + rows, :] = d_ref[...]
-    dm[ext:, :] = jnp.zeros((dm.shape[0] - ext, LANES), jnp.float32)
-    ds[ext:, :] = jnp.zeros((dm.shape[0] - ext, LANES), jnp.float32)
-    for r in range(PASSES):
-        for e, ref in ((r, north_ref), (rows + PASSES + r, south_ref)):
-            u[e] = ref[r, :snaps, :].astype(jnp.float32)
-            term = ref[r, snaps : snaps + 16, :].astype(jnp.float32)
-            dm[e : e + 1, :] = term[0:1] + term[1:2]
-    for e in range(ext):
-        piece, q = halo(e, snaps, snaps + 16)
-        piece = piece.astype(jnp.float32)
-        ds[e : e + 1, :] = roll(piece[0:1] + piece[1:2], 12 - 8 * q)
-        piece, q = halo(e, 0, snaps)
-        piece = piece.astype(jnp.float32)
-        for h in range(groups // 4):
-            acc = None
-            for g in range(4):
-                at = 8 * (4 * h + g)
-                own = u[e, at : at + 8, :]
-                part = in_strip(
-                    lane,
-                    roll(own, 12 + SEG * g),
-                    roll(own, 20 + SEG * g),
-                    roll(piece[at : at + 8], 12 + SEG * g - 8 * q),
-                )
-                acc = part if g == 0 else jnp.where(lane >= SEG * g, part, acc)
-            s[e, 8 * h : 8 * h + 8, :] = acc
-    d = dm[...]
-    first = in_strip(lane, roll(d, 12), roll(d, 20), ds[...])
-    strip = first
-    for g in range(1, 4):
-        strip = jnp.where(lane >= SEG * g, roll(first, SEG * g), strip)
-    ce[...] = 0.5 * (d + roll(d, -1))
-    se[...] = 0.5 * (strip + roll(strip, -1))
-    ds[...] = strip
-    cs[0 : ext - 1, :] = 0.5 * (dm[0 : ext - 1, :] + dm[1:ext, :])
-    ss[0 : ext - 1, :] = 0.5 * (ds[0 : ext - 1, :] + ds[1:ext, :])
-    row = lax.broadcasted_iota(jnp.int32, scale.shape, 0) + lat * rows
-    angle = (row.astype(jnp.float32) + 0.5) * math.pi / (rows * lats) - math.pi / 2
-    scale[...] = jnp.sqrt(jnp.maximum(jnp.cos(angle), 0.0))
-
-    def updated(field, e, carry, south_c, east_c):
-        current, above = carry
-        below = field[e + 1]
-        south = south_c[pl.ds(e, 1), :] * (below - current)
-        east = east_c[pl.ds(e, 1), :] * (roll(current, -1) - current)
-        fresh = current + ((south - above) + (east - roll(east, 1)))
-        return fresh, (below, south)
-
-    def entry(field, e, south_c):
-        current = field[e]
-        return current, south_c[e : e + 1, :] * (current - field[e - 1])
-
+            halo = side(t)
+        u0[k, own - 8 : own, :] = halo
+        u0[k, east : east + 8, :] = halo
+
+    dn[...] = jnp.zeros(dn.shape, jnp.float32)
+    dn[PASSES : PASSES + rows, :] = d_ref[...]
+    dn[0:PASSES, :] = north_d[0:PASSES] + north_d[PASSES : 2 * PASSES]
+    dn[PASSES + rows : 2 * PASSES + rows, :] = south_d[0:PASSES] + south_d[PASSES : 2 * PASSES]
+    dt[own:east, :] = dn[...].T
+    side_d = side_ref[tiles:, :].astype(jnp.float32)
+    fold = lambda v: v[0:8] + v[8:16]
+    halo = jnp.where(
+        lane < PASSES,
+        roll(fold(north_t), PASSES - rows),
+        jnp.where(lane < PASSES + rows, roll(fold(side_d), PASSES), roll(fold(south_t), PASSES + rows)),
+    )
+    dt[0 : own - 8, :] = jnp.zeros((own - 8, LANES), jnp.float32)
+    dt[own - 8 : own, :] = halo
+    dt[east : east + 8, :] = halo
+    dt[east + 8 :, :] = jnp.zeros((PADDED - east - 8, LANES), jnp.float32)
+    low, high = own - 8, east + 8
+    here = dt[low:high, :]
+    faces = jnp.concatenate([here + dt[low + 1 : high + 1, :], here + roll(here, -1)], axis=0) * 0.5
+    f_high, f_low = split2(faces)
+    terms = jnp.where(lane < LANES // 2, f_high.astype(jnp.float32), roll(f_low.astype(jnp.float32), LANES // 2))
+    terms = terms.astype(jnp.bfloat16)
+    source = lax.broadcasted_iota(jnp.int32, (LANES, LANES), 0) % (LANES // 2)
+    offset = jnp.where(lane_iota((LANES, LANES)) < snaps, 0, shift)
+    relative = source - offset
+    for k in range(count):
+        spread = jnp.dot(
+            terms, (relative == k).astype(jnp.bfloat16), preferred_element_type=jnp.float32
+        )
+        ce[k, low:high, :] = spread[: high - low]
+        cs[k, low:high, :] = spread[high - low :]
+
+    buffers = (u0, u1)
     for step in range(PASSES):
+        src, dst = buffers[step % 2], buffers[(step + 1) % 2]
         final = step == PASSES - 1
-
-        def body(e, carry):
-            main, edge = carry
-            fresh, main = updated(u, e, main, cs, ce)
-            fresh_edge, edge = updated(s, e, edge, ss, se)
-            if not final:
-                u[e] = fresh
-                s[e] = fresh_edge
-            else:
-                parts = []
-                for g in range(groups):
-                    strip_part = fresh_edge[8 * (g // 4) : 8 * (g // 4) + 8]
-                    base = SEG * (g % 4)
-                    low = roll(strip_part, -(20 + base))
-                    high = roll(strip_part, 116 - base)
-                    body_part = fresh[8 * g : 8 * g + 8]
-                    merged = jnp.where(lane < PASSES, low, jnp.where(lane >= LANES - PASSES, high, body_part))
-                    parts.append(merged)
-                i = e - PASSES
-                merged = jnp.concatenate(parts, axis=0) * scale[pl.ds(i, 1), :]
-                y_ref[i] = merged.astype(jnp.bfloat16)
-            return main, edge
-
-        start = step + 1
-        lax.fori_loop(start, ext - 1 - step, body, (entry(u, start, cs), entry(s, start, ss)))
+        start, stop = step + 1, count - 1 - step
+        for r in range(own if final else low, east if final else high, 8):
+            here = slice(r, r + 8)
+            current = src[start, here, :]
+            above = cs[start - 1, here, :] * (current - src[start - 1, here, :])
+            for k in range(start, stop):
+                below = src[k + 1, here, :]
+                southward = cs[k, here, :] * (below - current)
+                eastward = ce[k, here, :] * (src[k, r + 1 : r + 9, :] - current)
+                westward = ce[k, r - 1 : r + 7, :] * (current - src[k, r - 1 : r + 7, :])
+                dst[k, here, :] = current + ((southward - above) + (eastward - westward))
+                current, above = below, southward
         if not final:
 
             @pl.when(lat == 0)
             def _():
-                u[PASSES - 1] = jnp.zeros(u.shape[1:], jnp.float32)
-                s[PASSES - 1] = jnp.zeros(s.shape[1:], jnp.float32)
+                dst[PASSES - 1, low:high, :] = jnp.where(left, 0.0, dst[PASSES - 1, low:high, :])
 
             @pl.when(lat == lats - 1)
             def _():
-                u[rows + PASSES] = jnp.zeros(u.shape[1:], jnp.float32)
-                s[rows + PASSES] = jnp.zeros(s.shape[1:], jnp.float32)
-
-
-def smooth(x, d, side, north, south):
+                dst[PASSES + half, low:high, :] = jnp.where(left, dst[PASSES + half, low:high, :], 0.0)
+
+    tall = -(-half // 8) * 8
+    row = lax.broadcasted_iota(jnp.int32, (tall, LANES), 0) + jnp.where(lane_iota((tall, LANES)) < snaps, 0, shift)
+    angle = ((row + lat * rows).astype(jnp.float32) + 0.5) * math.pi / (rows * lats) - math.pi / 2
+    scale = jnp.sqrt(jnp.maximum(jnp.cos(angle), 0.0))
+    for t in range(half):
+        weighted = (dst[t + PASSES, own:east, :] * scale[t : t + 1]).astype(jnp.bfloat16)
+        both = dot_t(unit, weighted).astype(jnp.bfloat16)
+        y_ref[t] = both[:snaps]
+        y_ref[t + shift] = both[snaps:]
+
+
+def smooth(x, d, side, a, b):
     rows, snaps, width = x.shape
-    ext = rows + 2 * PASSES
-    tall = -(-ext // 8) * 8
-    field = lambda n: VMEM((ext, n, width), jnp.float32)
-    plane = VMEM((tall, width), jnp.float32)
+    count = -(-rows // 2) + 2 * PASSES
+    field = VMEM((count, PADDED, LANES), jnp.float32)
     return kernel_call(
         smooth_body,
         jax.ShapeDtypeStruct((rows, snaps, width), jnp.bfloat16),
-        [field(snaps), field(snaps // 4)] + [plane] * 7,
-    )(x, d, side, north, south)
+        [field] * 4 + [VMEM((width, LANES), jnp.float32), VMEM((PADDED, LANES), jnp.float32)],
+    )(x, d, side, a, b)
 
 
 def mm(a, b):
@@ -260,10 +291,6 @@
 def top_rows(h, upper_first=None):
     zt = power_basis(h, upper_first)
     return whitened(mmt(zt, zt), zt)
-
-
-def dot_t(a, b):
-    return lax.dot_general(a, b, (((1,), (1,)), ((), ())), preferred_element_type=jnp.float32)
 
 
 def pair_gram_body(own_ref, other_ref, o_ref):

time: 104 us -> 73.2 us (0.70)
  Pallas kernels: 47.1 us -> 19.4 us
  waiting for transfers between devices: 20 us -> 17.1 us
    pallas_call x1, Pallas kernels: 33.4 us -> 5.78 us  [smooth(): kernel_call(smooth_body, jax.ShapeDtypeStruct((rows, snaps, width), jnp.b...]
    ppermute x2, waiting for transfers between devices: 5.25 us -> 2.42 us  [swapped(): return lax.ppermute(message, 'lat', pairs + [(j, i) for i, j in pairs])]
  transfers between devices with their start and end apart: 6 -> 6, of which waited for: 6 -> 5; matrix products, arithmetic and copies ran while one was open for 0% -> 0% of each run, Pallas kernels for 0% -> 0%
where the time goes in v3:
time: 73.2 us; the launch traced here: 72.8 us
  blocking collectives  24 us (33%)
  Pallas kernels  19.4 us (27%)
  waiting for transfers between devices  17.1 us (23%)
  starting transfers between devices  10.4 us (14%)
  local copies, waits for them, and re-layouts  1.86 us (3%)
    all_to_all x2, blocking collectives, gathered(): return lax.all_to_all(parts, ('lat', 'lon'), 0, 0, tiled=True)  24 us
    ppermute x3, waiting for transfers between devices, exchanged(): lax.ppermute(block, 'tm', [(i, i ^ 1 << level) for i in range(count)])  12.5 us
    pallas_call x1, Pallas kernels, shards(): kernel_call(leaf_body, (b16(rows, RANK, width),) + small)  7.03 us
    pallas_call x1, Pallas kernels, smooth(): kernel_call(smooth_body, jax.ShapeDtypeStruct((rows, snaps, width), jnp.b...  5.78 us
    ppermute x2, starting transfers between devices, swapped(): return lax.ppermute(message, 'lat', pairs + [(j, i) for i, j in pairs])  5.66 us
    pallas_call x1, Pallas kernels, shards(): kernel_call(functools.partial(project_body, levels - 1), b16(rows, snaps,...  4.15 us
    ppermute x1, starting transfers between devices, halo_exchange(): side = lax.ppermute(packed, 'lon', forward)  2.97 us
    ppermute x2, waiting for transfers between devices, swapped(): return lax.ppermute(message, 'lat', pairs + [(j, i) for i, j in pairs])  2.42 us
  transfers between devices with their start and end apart: 6, of which 5 were waited for; matrix products, arithmetic and copies ran while one was open for 0% of the time, Pallas kernels for 0%

profile of v3, /device:TPU:0, one launch (start us, length us, event | category | flops | bytes accessed | tf_op | source)
XLA Modules:
  0.0 72.8 jit_solution(16773645126453130579)
XLA Ops:
  0.0 0.0 copy-start
  0.0 1.1 %copy-done = bf16[64,45,128]{2,0,1:T(8,128)(2,1)S(1)} copy-done((bf16[64,45,128]{2,0,1:T(8,128)(2,1)S(1)}, bf16[64,45,128]{2,0,1:T(8,128)(2,1)}, u32[]{:S(2)}) %copy-start) | copy-done | bytes 737304
  1.1 0.0 copy-start.2
  1.1 0.7 %copy-done.2 = f32[45,128]{1,0:T(8,128)S(1)} copy-done((f32[45,128]{1,0:T(8,128)S(1)}, f32[45,128]{1,0:T(8,128)}, u32[]{:S(2)}) %copy-start.2) | copy-done | bytes 23064
  1.9 0.0 copy-start.1
  1.9 0.5 shard_map.28
  2.4 3.0 %collective-permute-start = (bf16[208,128]{1,0:T(8,128)(2,1)S(1)}, bf16[208,128]{1,0:T(8,128)(2,1)S(1)}, u32[]{:S(2)}, u32[]{:S(2)}) collective-permute-start(bf16[208,128]{1,0:T(8,128)(2,1)S(1)} %get-tuple-element.11), channel_id=1, source_target_pairs={{0,1},{1,0},{2,3},{3,2},{4,5},{5,4},{6,7},{7,6},{8,9},{9,8},{10,11... | collective-permute-start | bytes 159752 | tf_op jit(solution)/shard_map/ppermute | solution.py:101
  5.3 2.1 %collective-permute-done.side_ref = bf16[208,128]{1,0:T(8,128)(2,1)S(1)} collective-permute-done((bf16[208,128]{1,0:T(8,128)(2,1)S(1)}, bf16[208,128]{1,0:T(8,128)(2,1)S(1)}, u32[]{:S(2)}, u32[]{:S(2)}) %collective-permute-start) | collective-permute-done | bytes 53280 | tf_op jit(solution)/shard_map/ppermute | solution.py:101
  7.5 0.0 copy-start.3
  7.5 0.7 collective-permute-start.2
  8.2 5.0 %collective-permute-start.1 = (bf16[320,128]{1,0:T(8,128)(2,1)S(1)}, bf16[320,128]{1,0:T(8,128)(2,1)S(1)}, u32[]{:S(2)}, u32[]{:S(2)}) collective-permute-start(bf16[320,128]{1,0:T(8,128)(2,1)S(1)} %get-tuple-element.20), channel_id=1, source_target_pairs={{0,2},{4,6},{2,0},{6,4},{1,3},{5,7},{3,1},{7,5},{8,10},{12,14},{10... | collective-permute-start | bytes 245768 | tf_op jit(solution)/shard_map/ppermute | solution.py:112
  13.1 0.0 collective-permute-done.2.b_ref
  13.2 2.4 %collective-permute-done.1.a_ref = bf16[320,128]{1,0:T(8,128)(2,1)S(1)} collective-permute-done((bf16[320,128]{1,0:T(8,128)(2,1)S(1)}, bf16[320,128]{1,0:T(8,128)(2,1)S(1)}, u32[]{:S(2)}, u32[]{:S(2)}) %collective-permute-start.1) | collective-permute-done | bytes 81952 | tf_op jit(solution)/shard_map/ppermute | solution.py:112
  15.6 0.0 copy-done.1
  15.6 0.0 copy-done.3
  15.6 5.8 %shard_map.29.own_ref.y_ref = bf16[45,64,128]{2,1,0:T(8,128)(2,1)S(1)} custom-call(bf16[45,64,128]{2,1,0:T(8,128)(2,1)S(1)} %bitcast.3, f32[45,128]{1,0:T(8,128)S(1)} %copy-done.3, bf16[208,128]{1,0:T(8,128)(2,1)S(1)} %collective-permute-done.side_ref, bf16[320,128]{1,0:T(8,128)(2,1)S(1)} %collective-permute-done.1.a_ref, ...), custom_call_target="tpu_custom_call" | custom-call | flops 1048576 | bytes 1048576 | tf_op jit(solution)/shard_map/pallas_call | solution.py:238
  21.4 0.1 collective-permute-start.3
  21.4 2.2 %collective-permute-done.3.other_ref = bf16[45,64,128]{2,1,0:T(8,128)(2,1)S(1)} collective-permute-done((bf16[45,64,128]{2,1,0:T(8,128)(2,1)S(1)}, bf16[45,64,128]{2,1,0:T(8,128)(2,1)S(1)}, u32[]{:S(2)}, u32[]{:S(2)}) %collective-permute-start.3) | collective-permute-done | bytes 737312 | tf_op jit(solution)/shard_map/ppermute | solution.py:380
  23.6 1.1 %shard_map.30 = f32[8,64,128]{2,1,0:T(8,128)S(1)} custom-call(bf16[45,64,128]{2,1,0:T(8,128)(2,1)S(1)} %shard_map.29.own_ref.y_ref, bf16[45,64,128]{2,1,0:T(8,128)(2,1)S(1)} %collective-permute-done.3.other_ref), custom_call_target="tpu_custom_call" | custom-call | flops 1048576 | bytes 1048576 | tf_op jit(solution)/shard_map/pallas_call | solution.py:396
  24.7 13.2 %all_to_all.10 = f32[8,64,128]{2,1,0:T(8,128)S(1)} all-to-all(f32[8,64,128]{2,1,0:T(8,128)S(1)} %shard_map.30), channel_id=1, replica_groups=mesh['tm'=4,'lat'=4,'lon'=2] {'lat','lon'}, dimensions={0} | all-to-all | bytes 524288 | tf_op jit(solution)/shard_map/all_to_all | solution.py:384
  38.0 0.1 collective-permute-start.4
  38.1 1.2 %collective-permute-done.4.gp_ref = f32[64,128]{1,0:T(8,128)S(1)} collective-permute-done((f32[64,128]{1,0:T(8,128)S(1)}, f32[64,128]{1,0:T(8,128)S(1)}, u32[]{:S(2)}, u32[]{:S(2)}) %collective-permute-start.4) | collective-permute-done | bytes 32800 | tf_op jit(solution)/shard_map/ppermute | solution.py:380
  39.3 7.0 %shard_map.31 = (bf16[45,32,128]{2,1,0:T(8,128)(2,1)S(1)}, f32[32,32]{1,0:T(8,128)S(1)}, f32[64,32]{1,0:T(8,128)S(1)}) custom-call(f32[64,128]{1,0:T(8,128)S(1)} %reduce_sum.9.g_ref, f32[64,128]{1,0:T(8,128)S(1)} %collective-permute-done.4.gp_ref, bf16[45,64,128]{2,1,0:T(8,128)(2,1)S(1)} %shard_map.29.own_ref.y_ref, ...), custom_call_target="tpu_custom_call" | custom-call | flops 1048576 | bytes 1048576 | tf_op jit(solution)/shard_map/pallas_call | solution.py:399
  46.3 1.6 %collective-permute-start.5 = (bf16[45,32,128]{2,1,0:T(8,128)(2,1)S(1)}, bf16[45,32,128]{2,1,0:T(8,128)(2,1)S(1)}, u32[]{:S(2)}, u32[]{:S(2)}) collective-permute-start(bf16[45,32,128]{2,1,0:T(8,128)(2,1)S(1)} %get-tuple-element.14.own_ref), channel_id=1, source_target_pairs={{0,16},{8,24},{16,0},{24,8},{1,17},{9,25},{17,1},{25,9},{2,18},{10... | collective-permute-start | bytes 1105928 | tf_op jit(solution)/shard_map/ppermute | solution.py:380
  47.9 9.1 %collective-permute-done.5.other_ref = bf16[45,32,128]{2,1,0:T(8,128)(2,1)S(1)} collective-permute-done((bf16[45,32,128]{2,1,0:T(8,128)(2,1)S(1)}, bf16[45,32,128]{2,1,0:T(8,128)(2,1)S(1)}, u32[]{:S(2)}, u32[]{:S(2)}) %collective-permute-start.5) | collective-permute-done | bytes 368672 | tf_op jit(solution)/shard_map/ppermute | solution.py:380
  57.0 0.9 %shard_map.32 = f32[8,32,128]{2,1,0:T(8,128)S(1)} custom-call(bf16[45,32,128]{2,1,0:T(8,128)(2,1)S(1)} %collective-permute-done.5.other_ref, bf16[45,64,128]{2,1,0:T(8,128)(2,1)S(1)} %shard_map.29.own_ref.y_ref, bf16[45,32,128]{2,1,0:T(8,128)(2,1)S(1)} %get-tuple-element.14.own_ref), custom_call_target="tpu_custom_call" | custom-call | flops 1048576 | bytes 1048576 | tf_op jit(solution)/shard_map/pallas_call | solution.py:404
  57.9 10.7 %all_to_all.11.p_ref = f32[8,32,128]{2,1,0:T(8,128)S(1)} all-to-all(f32[8,32,128]{2,1,0:T(8,128)S(1)} %shard_map.32), channel_id=1, replica_groups=mesh['tm'=4,'lat'=4,'lon'=2] {'lat','lon'}, dimensions={0} | all-to-all | bytes 262144 | tf_op jit(solution)/shard_map/all_to_all | solution.py:384
  68.7 4.2 %shard_map.33 = bf16[45,64,128]{2,1,0:T(8,128)(2,1)} custom-call(f32[8,32,128]{2,1,0:T(8,128)S(1)} %all_to_all.11.p_ref, f32[32,32]{1,0:T(8,128)S(1)} %get-tuple-element.15.h_ref, f32[64,32]{1,0:T(8,128)S(1)} %get-tuple-element.16.c_ref, bf16[45,32,128]{2,1,0:T(8,128)(2,1)S(1)} %get-tuple-element.14.own_ref, ...), custom_call_target="tpu_custom_call" | custom-call | flops 1048576 | bytes 1048576 | tf_op jit(solution)/shard_map/pallas_call | solution.py:409
  (4 shorter events, 0.0 us)
Async XLA Ops:
  0.0 1.1 %copy-start = (bf16[64,45,128]{2,0,1:T(8,128)(2,1)S(1)}, bf16[64,45,128]{2,0,1:T(8,128)(2,1)}, u32[]{:S(2)}) copy-start(bf16[64,45,128]{2,0,1:T(8,128)(2,1)} %param.2) | copy-start | bytes 2211844
  1.1 0.7 %copy-start.2 = (f32[45,128]{1,0:T(8,128)S(1)}, f32[45,128]{1,0:T(8,128)}, u32[]{:S(2)}) copy-start(f32[45,128]{1,0:T(8,128)} %d_ref.3) | copy-start | bytes 69124
  1.9 13.7 %copy-start.1 = (bf16[64,45,128]{2,0,1:T(8,128)(2,1)S(1)}, bf16[64,45,128]{2,0,1:T(8,128)(2,1)}, u32[]{:S(2)}) copy-start(bf16[64,45,128]{2,0,1:T(8,128)(2,1)} %param.2) | copy-start | bytes 2211844
  2.4 5.1 %collective-permute-start = (bf16[208,128]{1,0:T(8,128)(2,1)S(1)}, bf16[208,128]{1,0:T(8,128)(2,1)S(1)}, u32[]{:S(2)}, u32[]{:S(2)}) collective-permute-start(bf16[208,128]{1,0:T(8,128)(2,1)S(1)} %get-tuple-element.11), channel_id=1, source_target_pairs={{0,1},{1,0},{2,3},{3,2},{4,5},{5,4},{6,7},{7,6},{8,9},{9,8},{10,11... | collective-permute-start | bytes 159752 | tf_op jit(solution)/shard_map/ppermute | solution.py:101
  7.5 8.1 %copy-start.3 = (f32[45,128]{1,0:T(8,128)S(1)}, f32[45,128]{1,0:T(8,128)}, u32[]{:S(2)}) copy-start(f32[45,128]{1,0:T(8,128)} %d_ref.3) | copy-start | bytes 69124
  7.5 5.7 %collective-permute-start.2 = (bf16[320,128]{1,0:T(8,128)(2,1)S(1)}, bf16[320,128]{1,0:T(8,128)(2,1)S(1)}, u32[]{:S(2)}, u32[]{:S(2)}) collective-permute-start(bf16[320,128]{1,0:T(8,128)(2,1)S(1)} %get-tuple-element.19), channel_id=1, source_target_pairs={{2,4},{4,2},{3,5},{5,3},{10,12},{12,10},{11,13},{13,11},{18,20},{2... | collective-permute-start | bytes 245768 | tf_op jit(solution)/shard_map/ppermute | solution.py:112
  8.2 7.4 %collective-permute-start.1 = (bf16[320,128]{1,0:T(8,128)(2,1)S(1)}, bf16[320,128]{1,0:T(8,128)(2,1)S(1)}, u32[]{:S(2)}, u32[]{:S(2)}) collective-permute-start(bf16[320,128]{1,0:T(8,128)(2,1)S(1)} %get-tuple-element.20), channel_id=1, source_target_pairs={{0,2},{4,6},{2,0},{6,4},{1,3},{5,7},{3,1},{7,5},{8,10},{12,14},{10... | collective-permute-start | bytes 245768 | tf_op jit(solution)/shard_map/ppermute | solution.py:112
  21.4 2.3 %collective-permute-start.3 = (bf16[45,64,128]{2,1,0:T(8,128)(2,1)S(1)}, bf16[45,64,128]{2,1,0:T(8,128)(2,1)S(1)}, u32[]{:S(2)}, u32[]{:S(2)}) collective-permute-start(bf16[45,64,128]{2,1,0:T(8,128)(2,1)S(1)} %shard_map.29.own_ref.y_ref), channel_id=1, source_target_pairs={{0,8},{8,0},{16,24},{24,16},{1,9},{9,1},{17,25},{25,17},{2,10},{10... | collective-permute-start | bytes 2211848 | tf_op jit(solution)/shard_map/ppermute | solution.py:380
  38.0 1.3 %collective-permute-start.4 = (f32[64,128]{1,0:T(8,128)S(1)}, f32[64,128]{1,0:T(8,128)S(1)}, u32[]{:S(2)}, u32[]{:S(2)}) collective-permute-start(f32[64,128]{1,0:T(8,128)S(1)} %reduce_sum.9.g_ref), channel_id=1, source_target_pairs={{0,8},{8,0},{16,24},{24,16},{1,9},{9,1},{17,25},{25,17},{2,10},{10... | collective-permute-start | bytes 98312 | tf_op jit(solution)/shard_map/ppermute | solution.py:380
  46.3 10.7 %collective-permute-start.5 = (bf16[45,32,128]{2,1,0:T(8,128)(2,1)S(1)}, bf16[45,32,128]{2,1,0:T(8,128)(2,1)S(1)}, u32[]{:S(2)}, u32[]{:S(2)}) collective-permute-start(bf16[45,32,128]{2,1,0:T(8,128)(2,1)S(1)} %get-tuple-element.14.own_ref), channel_id=1, source_target_pairs={{0,16},{8,24},{16,0},{24,8},{1,17},{9,25},{17,1},{25,9},{2,18},{10... | collective-permute-start | bytes 1105928 | tf_op jit(solution)/shard_map/ppermute | solution.py:380

commit v4 on v3

--- a/solution.py
+++ b/solution.py
@@ -256,24 +256,25 @@
     n = s.shape[0]
     a = jnp.concatenate([s, zt], axis=1)
     w = a.shape[1]
-    row = lax.broadcasted_iota(jnp.int32, (n, w), 0)
-    diagonal = row == lane_iota((n, w))
-    floor = jnp.broadcast_to(
-        jnp.sum(jnp.where(diagonal, a, 0.0), axis=1, keepdims=True) * 1e-7 + 1e-37, (n, w)
-    )
+    diagonal = lax.broadcasted_iota(jnp.int32, (n, w), 0) == lane_iota((n, w))
+    least = jnp.sum(jnp.where(diagonal, a, 0.0), axis=1, keepdims=True) * 1e-7 + 1e-37
+    floor = jnp.broadcast_to(least, (n, w))
+    done = []
     for k0 in range(0, n, block):
-        cols = [jnp.broadcast_to(a[:, k0 + j : k0 + j + 1], (n, w)) for j in range(block)]
-        for p in range(block):
-            k = k0 + p
-            if k == n - 1:
-                continue
-            inverse = 1.0 / jnp.maximum(cols[p][k : k + 1, :], floor[k : k + 1, :])
-            below = jnp.where(row > k, cols[p], 0.0)
+        tall = n - k0
+        row = lax.broadcasted_iota(jnp.int32, (tall, w), 0)
+        cols = [jnp.broadcast_to(a[:, k0 + j : k0 + j + 1], (tall, w)) for j in range(block)]
+        for p in range(min(block, tall - 1)):
+            inverse = 1.0 / jnp.maximum(cols[p][p : p + 1, :], floor[k0 + p : k0 + p + 1, :])
+            below = jnp.where(row > p, cols[p], 0.0)
             for j in range(p + 1, block):
-                cols[j] = cols[j] - below * (cols[j][k : k + 1, :] * inverse)
-            a = a - below * (a[k : k + 1, :] * inverse)
+                cols[j] = cols[j] - below * (cols[j][p : p + 1, :] * inverse)
+            a = a - below * (a[p : p + 1, :] * inverse)
+        done.append(a[:block])
+        a = a[block:]
+    a = jnp.concatenate(done, axis=0)
     pivots = jnp.sum(jnp.where(diagonal, a, 0.0), axis=1, keepdims=True)
-    return a[:, n:] * lax.rsqrt(jnp.maximum(pivots, floor[:, :1]))
+    return a[:, n:] * lax.rsqrt(jnp.maximum(pivots, least))
 
 
 def power_basis(h, upper_first):
@@ -293,26 +294,68 @@
     return whitened(mmt(zt, zt), zt)
 
 
+def odd(level):
+    return (lax.axis_index("tm") >> level & 1) == 1
+
+
 def pair_gram_body(own_ref, other_ref, o_ref):
+    n = own_ref.shape[1]
     acc = None
     for i in range(own_ref.shape[0]):
-        own = own_ref[i]
-        part = dot_t(own, jnp.concatenate([own, other_ref[i]], axis=0))
+        both = jnp.concatenate([own_ref[i], other_ref[i]], axis=0)
+        part = dot_t(both, both)
         acc = part if acc is None else acc + part
+    cross = jnp.where(odd(0), pltpu.roll(acc[n + n // 2 :], n, 1), acc[: n // 2])[:, n:]
+    tall = o_ref.shape[1]
+    packed = jnp.concatenate(
+        [acc[:tall, :n], jnp.concatenate([acc[tall:n, :n], cross], axis=0)], axis=1
+    )
     for j in range(o_ref.shape[0]):
-        o_ref[j] = acc
-
-
-def odd(level):
-    return (lax.axis_index("tm") >> level & 1) == 1
-
-
-def leaf_body(g_ref, gp_ref, own_ref, other_ref, modes_ref, h_ref, c_ref):
+        o_ref[j] = packed
+
+
+def pair_gram(g, gp, n):
+    tall = g.shape[0]
+    rest = n - tall
+    block = lambda v: jnp.concatenate([v[:, :n], v[:rest, n:]], axis=0)
+    mine, theirs = g[rest:, n:], gp[rest:, n:]
+    upper = odd(0)
+    cross = jnp.concatenate([jnp.where(upper, theirs, mine), jnp.where(upper, mine, theirs)], axis=0)
+    flipped = cross.T
+    return block(g), block(gp), jnp.where(upper, flipped, cross), jnp.where(upper, cross, flipped)
+
+
+def put_modes(w, own_ref, other, modes_ref, part_ref):
+    rows, half = modes_ref.shape[0], part_ref.shape[0]
+    for i in range(rows):
+        stacked = jnp.concatenate([own_ref[i], other(i)], axis=0)
+        modes_ref[i] = jnp.dot(w, stacked, preferred_element_type=jnp.float32).astype(jnp.bfloat16)
+    start = jnp.where(odd(0), rows - half, 0)
+    for i in range(half):
+        part_ref[i] = modes_ref[start + i]
+
+
+def halves(rows, here_ref, there_ref):
+    half = here_ref.shape[0]
+    upper = odd(0)
+
+    def row(i):
+        if i < half:
+            return jnp.where(upper, there_ref[i], here_ref[i])
+        j = i - (rows - half)
+        return jnp.where(upper, here_ref[j], there_ref[j])
+
+    return row
+
+
+def leaf_body(g_ref, gp_ref, own_ref, other_ref, modes_ref, part_ref, h_ref, c_ref):
     n = own_ref.shape[1]
-    own_rows, other_rows = g_ref[...], gp_ref[...]
-    gram = jnp.concatenate([own_rows, pltpu.roll(other_rows, n, 1)], axis=0)
-    q_own = top_rows(own_rows[:, :n])
-    q_other = top_rows(other_rows[:, :n])
+    own, other, cross, flipped = pair_gram(g_ref[...], gp_ref[...], n)
+    q_own = top_rows(own)
+    q_other = top_rows(other)
+    gram = jnp.concatenate(
+        [jnp.concatenate([own, cross], axis=1), jnp.concatenate([flipped, other], axis=1)], axis=0
+    )
     zero = jnp.zeros_like(q_own)
     basis = jnp.concatenate(
         [jnp.concatenate([q_own, zero], axis=1), jnp.concatenate([zero, q_other], axis=1)], axis=0
@@ -323,16 +366,16 @@
     gw = mmt(gram, wf)
     c_ref[...] = gw[:n]
     h_ref[...] = mm(wf, gw)
-    for i in range(own_ref.shape[0]):
-        stacked = jnp.concatenate([own_ref[i], other_ref[i]], axis=0)
-        modes_ref[i] = jnp.dot(w, stacked, preferred_element_type=jnp.float32).astype(jnp.bfloat16)
-
-
-def cross_body(other_ref, y_ref, own_ref, o_ref):
+    put_modes(w, own_ref, lambda i: other_ref[i], modes_ref, part_ref)
+
+
+def cross_body(here_ref, there_ref, y_ref, own_ref, o_ref):
     acc = None
-    for i in range(y_ref.shape[0]):
-        other = other_ref[i]
-        part = dot_t(other, jnp.concatenate([y_ref[i], own_ref[i], other], axis=0))
+    rows = y_ref.shape[0]
+    other = halves(rows, here_ref, there_ref)
+    for i in range(rows):
+        theirs = other(i)
+        part = dot_t(theirs, jnp.concatenate([y_ref[i], own_ref[i], theirs], axis=0))
         acc = part if acc is None else acc + part
     for j in range(o_ref.shape[0]):
         o_ref[j] = acc
@@ -354,24 +397,24 @@
     return gram, coef
 
 
-def merge_body(level, p_ref, h_ref, c_ref, own_ref, other_ref, modes_ref, hn_ref, cn_ref):
+def merge_body(level, p_ref, h_ref, c_ref, own_ref, here_ref, there_ref, modes_ref, part_ref, hn_ref, cn_ref):
     gram, coef = merged_gram(p_ref, h_ref, c_ref, c_ref.shape[0])
     w = top_rows(gram, odd(level)).astype(jnp.bfloat16)
     wf = w.astype(jnp.float32)
     cn_ref[...] = mmt(coef, wf)
     hn_ref[...] = mmt(mm(wf, gram), wf)
-    for i in range(own_ref.shape[0]):
-        stacked = jnp.concatenate([own_ref[i], other_ref[i]], axis=0)
-        modes_ref[i] = jnp.dot(w, stacked, preferred_element_type=jnp.float32).astype(jnp.bfloat16)
-
-
-def project_body(level, p_ref, h_ref, c_ref, own_ref, other_ref, o_ref):
+    put_modes(w, own_ref, halves(own_ref.shape[0], here_ref, there_ref), modes_ref, part_ref)
+
+
+def project_body(level, p_ref, h_ref, c_ref, own_ref, here_ref, there_ref, o_ref):
     gram, coef = merged_gram(p_ref, h_ref, c_ref, c_ref.shape[0])
     zt = power_basis(gram, odd(level))
     r = whitened(mmt(mm(zt, gram), zt), zt)
     weights = mm(mmt(coef, r), r).astype(jnp.bfloat16)
-    for i in range(own_ref.shape[0]):
-        stacked = jnp.concatenate([own_ref[i], other_ref[i]], axis=0)
+    rows = own_ref.shape[0]
+    other = halves(rows, here_ref, there_ref)
+    for i in range(rows):
+        stacked = jnp.concatenate([own_ref[i], other(i)], axis=0)
         o_ref[i] = jnp.dot(weights, stacked, preferred_element_type=jnp.float32).astype(jnp.bfloat16)
 
 
@@ -393,21 +436,25 @@
     x = jnp.transpose(residuals, (1, 0, 2))
     y = smooth(x, diffusivity, *halo_exchange(x, diffusivity))
     other = exchanged(y, 0)
-    parts = gathered(kernel_call(pair_gram_body, f32(tiles, snaps, 2 * snaps))(y, other))
+    parts = gathered(kernel_call(pair_gram_body, f32(tiles, snaps * 3 // 4, 2 * snaps))(y, other))
     gram = jnp.sum(parts, axis=0)
-    small = (f32(RANK, RANK), f32(snaps, RANK))
-    modes, h, c = kernel_call(leaf_body, (b16(rows, RANK, width),) + small)(
-        gram, exchanged(gram, 0), y, other
-    )
+    block = (
+        b16(rows, RANK, width),
+        b16(-(-rows // 2), RANK, width),
+        f32(RANK, RANK),
+        f32(snaps, RANK),
+    )
+    modes, part, h, c = kernel_call(leaf_body, block)(gram, exchanged(gram, 0), y, other)
     for level in range(1, levels):
-        other = exchanged(modes, level)
-        parts = gathered(kernel_call(cross_body, f32(tiles, RANK, snaps + 2 * RANK))(other, y, modes))
+        here = exchanged(part, level)
+        there = exchanged(here, 0)
+        parts = gathered(kernel_call(cross_body, f32(tiles, RANK, snaps + 2 * RANK))(here, there, y, modes))
         if level < levels - 1:
-            modes, h, c = kernel_call(
-                functools.partial(merge_body, level), (b16(rows, RANK, width),) + small
-            )(parts, h, c, modes, other)
+            modes, part, h, c = kernel_call(functools.partial(merge_body, level), block)(
+                parts, h, c, modes, here, there
+            )
     out = kernel_call(functools.partial(project_body, levels - 1), b16(rows, snaps, width))(
-        parts, h, c, modes, other
+        parts, h, c, modes, here, there
     )
     return jnp.transpose(out, (1, 0, 2))
 

time: 73.2 us -> 69.7 us (0.952)
  waiting for transfers between devices: 17.1 us -> 14.6 us
  blocking collectives: 24 us -> 22.6 us
    ppermute x3 -> x4, waiting for transfers between devices: 12.5 us -> 10.1 us  [exchanged(): lax.ppermute(block, 'tm', [(i, i ^ 1 << level) for i in range(count)])]
    all_to_all x2, blocking collectives: 24 us -> 22.6 us  [gathered(): return lax.all_to_all(parts, ('lat', 'lon'), 0, 0, tiled=True)]
    ppermute x3 -> x4, starting transfers between devices: 1.73 us -> 1.73 us  [exchanged(): lax.ppermute(block, 'tm', [(i, i ^ 1 << level) for i in range(count)])]
  transfers between devices with their start and end apart: 6 -> 7, of which waited for: 5 -> 6; matrix products, arithmetic and copies ran while one was open for 0% -> 0% of each run, Pallas kernels for 0% -> 0%
where the time goes in v4:
time: 69.7 us; the launch traced here: 69.3 us
  blocking collectives  22.6 us (32%)
  Pallas kernels  19.8 us (28%)
  waiting for transfers between devices  14.6 us (21%)
  starting transfers between devices  10.4 us (15%)
  local copies, waits for them, and re-layouts  1.86 us (3%)
    all_to_all x2, blocking collectives, gathered(): return lax.all_to_all(parts, ('lat', 'lon'), 0, 0, tiled=True)  22.6 us
    ppermute x4, waiting for transfers between devices, exchanged(): lax.ppermute(block, 'tm', [(i, i ^ 1 << level) for i in range(count)])  10.1 us
    pallas_call x1, Pallas kernels, shards(): kernel_call(leaf_body, block)(gram, exchanged(gram, 0), y, other)  7.16 us
    pallas_call x1, Pallas kernels, smooth(): kernel_call(smooth_body, jax.ShapeDtypeStruct((rows, snaps, width), jnp.b...  5.78 us
    ppermute x2, starting transfers between devices, swapped(): return lax.ppermute(message, 'lat', pairs + [(j, i) for i, j in pairs])  5.66 us
    pallas_call x1, Pallas kernels, shards(): kernel_call(functools.partial(project_body, levels - 1), b16(rows, snaps,...  4.14 us
    ppermute x1, starting transfers between devices, halo_exchange(): side = lax.ppermute(packed, 'lon', forward)  2.97 us
    ppermute x2, waiting for transfers between devices, swapped(): return lax.ppermute(message, 'lat', pairs + [(j, i) for i, j in pairs])  2.42 us
  transfers between devices with their start and end apart: 7, of which 6 were waited for; matrix products, arithmetic and copies ran while one was open for 0% of the time, Pallas kernels for 0%

profile of v4, /device:TPU:0, one launch (start us, length us, event | category | flops | bytes accessed | tf_op | source)
XLA Modules:
  0.0 69.3 jit_solution(13697317512078504705)
XLA Ops:
  0.0 0.0 copy-start
  0.0 1.1 %copy-done = bf16[64,45,128]{2,0,1:T(8,128)(2,1)S(1)} copy-done((bf16[64,45,128]{2,0,1:T(8,128)(2,1)S(1)}, bf16[64,45,128]{2,0,1:T(8,128)(2,1)}, u32[]{:S(2)}) %copy-start) | copy-done | bytes 737304
  1.1 0.0 copy-start.2
  1.1 0.7 %copy-done.2 = f32[45,128]{1,0:T(8,128)S(1)} copy-done((f32[45,128]{1,0:T(8,128)S(1)}, f32[45,128]{1,0:T(8,128)}, u32[]{:S(2)}) %copy-start.2) | copy-done | bytes 23064
  1.9 0.0 copy-start.1
  1.9 0.5 shard_map.28
  2.4 3.0 %collective-permute-start = (bf16[208,128]{1,0:T(8,128)(2,1)S(1)}, bf16[208,128]{1,0:T(8,128)(2,1)S(1)}, u32[]{:S(2)}, u32[]{:S(2)}) collective-permute-start(bf16[208,128]{1,0:T(8,128)(2,1)S(1)} %get-tuple-element.12), channel_id=1, source_target_pairs={{0,1},{1,0},{2,3},{3,2},{4,5},{5,4},{6,7},{7,6},{8,9},{9,8},{10,11... | collective-permute-start | bytes 159752 | tf_op jit(solution)/shard_map/ppermute | solution.py:101
  5.3 2.1 %collective-permute-done.side_ref = bf16[208,128]{1,0:T(8,128)(2,1)S(1)} collective-permute-done((bf16[208,128]{1,0:T(8,128)(2,1)S(1)}, bf16[208,128]{1,0:T(8,128)(2,1)S(1)}, u32[]{:S(2)}, u32[]{:S(2)}) %collective-permute-start) | collective-permute-done | bytes 53280 | tf_op jit(solution)/shard_map/ppermute | solution.py:101
  7.5 0.0 copy-start.3
  7.5 0.7 collective-permute-start.2
  8.2 5.0 %collective-permute-start.1 = (bf16[320,128]{1,0:T(8,128)(2,1)S(1)}, bf16[320,128]{1,0:T(8,128)(2,1)S(1)}, u32[]{:S(2)}, u32[]{:S(2)}) collective-permute-start(bf16[320,128]{1,0:T(8,128)(2,1)S(1)} %get-tuple-element.22), channel_id=1, source_target_pairs={{0,2},{4,6},{2,0},{6,4},{1,3},{5,7},{3,1},{7,5},{8,10},{12,14},{10... | collective-permute-start | bytes 245768 | tf_op jit(solution)/shard_map/ppermute | solution.py:112
  13.1 0.0 collective-permute-done.2.b_ref
  13.2 2.4 %collective-permute-done.1.a_ref = bf16[320,128]{1,0:T(8,128)(2,1)S(1)} collective-permute-done((bf16[320,128]{1,0:T(8,128)(2,1)S(1)}, bf16[320,128]{1,0:T(8,128)(2,1)S(1)}, u32[]{:S(2)}, u32[]{:S(2)}) %collective-permute-start.1) | collective-permute-done | bytes 81952 | tf_op jit(solution)/shard_map/ppermute | solution.py:112
  15.6 0.0 copy-done.1
  15.6 0.0 copy-done.3
  15.6 5.8 %shard_map.29.own_ref.y_ref = bf16[45,64,128]{2,1,0:T(8,128)(2,1)S(1)} custom-call(bf16[45,64,128]{2,1,0:T(8,128)(2,1)S(1)} %bitcast.3, f32[45,128]{1,0:T(8,128)S(1)} %copy-done.3, bf16[208,128]{1,0:T(8,128)(2,1)S(1)} %collective-permute-done.side_ref, bf16[320,128]{1,0:T(8,128)(2,1)S(1)} %collective-permute-done.1.a_ref, ...), custom_call_target="tpu_custom_call" | custom-call | flops 1048576 | bytes 1048576 | tf_op jit(solution)/shard_map/pallas_call | solution.py:238
  21.4 0.1 collective-permute-start.3
  21.4 2.2 %collective-permute-done.3.other_ref = bf16[45,64,128]{2,1,0:T(8,128)(2,1)S(1)} collective-permute-done((bf16[45,64,128]{2,1,0:T(8,128)(2,1)S(1)}, bf16[45,64,128]{2,1,0:T(8,128)(2,1)S(1)}, u32[]{:S(2)}, u32[]{:S(2)}) %collective-permute-start.3) | collective-permute-done | bytes 737312 | tf_op jit(solution)/shard_map/ppermute | solution.py:423
  23.6 1.3 %shard_map.30 = f32[8,48,128]{2,1,0:T(8,128)S(1)} custom-call(bf16[45,64,128]{2,1,0:T(8,128)(2,1)S(1)} %shard_map.29.own_ref.y_ref, bf16[45,64,128]{2,1,0:T(8,128)(2,1)S(1)} %collective-permute-done.3.other_ref), custom_call_target="tpu_custom_call" | custom-call | flops 1048576 | bytes 1048576 | tf_op jit(solution)/shard_map/pallas_call | solution.py:439
  25.0 12.3 %all_to_all.10 = f32[8,48,128]{2,1,0:T(8,128)S(1)} all-to-all(f32[8,48,128]{2,1,0:T(8,128)S(1)} %shard_map.30), channel_id=1, replica_groups=mesh['tm'=4,'lat'=4,'lon'=2] {'lat','lon'}, dimensions={0} | all-to-all | bytes 393216 | tf_op jit(solution)/shard_map/all_to_all | solution.py:427
  37.3 0.1 collective-permute-start.4
  37.3 1.2 %collective-permute-done.4.gp_ref = f32[48,128]{1,0:T(8,128)S(1)} collective-permute-done((f32[48,128]{1,0:T(8,128)S(1)}, f32[48,128]{1,0:T(8,128)S(1)}, u32[]{:S(2)}, u32[]{:S(2)}) %collective-permute-start.4) | collective-permute-done | bytes 24608 | tf_op jit(solution)/shard_map/ppermute | solution.py:423
  38.5 7.2 %shard_map.31 = (bf16[45,32,128]{2,1,0:T(8,128)(2,1)S(1)}, bf16[23,32,128]{2,1,0:T(8,128)(2,1)S(1)}, f32[32,32]{1,0:T(8,128)S(1)}, f32[64,32]{1,0:T(8,128)S(1)}) custom-call(f32[48,128]{1,0:T(8,128)S(1)} %reduce_sum.9.g_ref, f32[48,128]{1,0:T(8,128)S(1)} %collective-permute-done.4.gp_ref, bf16[45,64,128]{2,1,0:T(8,128)(2,1)S(1)} %shard_map.29.own_ref.y_ref, ...), custom_call_target="tpu_custom_call" | custom-call | flops 1048576 | bytes 1048576 | tf_op jit(solution)/shard_map/pallas_call | solution.py:447
  45.7 1.6 %collective-permute-start.5 = (bf16[23,32,128]{2,1,0:T(8,128)(2,1)S(1)}, bf16[23,32,128]{2,1,0:T(8,128)(2,1)S(1)}, u32[]{:S(2)}, u32[]{:S(2)}) collective-permute-start(bf16[23,32,128]{2,1,0:T(8,128)(2,1)S(1)} %get-tuple-element.15), channel_id=1, source_target_pairs={{0,16},{8,24},{16,0},{24,8},{1,17},{9,25},{17,1},{25,9},{2,18},{10... | collective-permute-start | bytes 565256 | tf_op jit(solution)/shard_map/ppermute | solution.py:423
  47.3 5.3 %collective-permute-done.5.here_ref = bf16[23,32,128]{2,1,0:T(8,128)(2,1)S(1)} collective-permute-done((bf16[23,32,128]{2,1,0:T(8,128)(2,1)S(1)}, bf16[23,32,128]{2,1,0:T(8,128)(2,1)S(1)}, u32[]{:S(2)}, u32[]{:S(2)}) %collective-permute-start.5) | collective-permute-done | bytes 188448 | tf_op jit(solution)/shard_map/ppermute | solution.py:423
  52.6 0.0 collective-permute-start.6
  52.6 1.4 %collective-permute-done.6.there_ref = bf16[23,32,128]{2,1,0:T(8,128)(2,1)S(1)} collective-permute-done((bf16[23,32,128]{2,1,0:T(8,128)(2,1)S(1)}, bf16[23,32,128]{2,1,0:T(8,128)(2,1)S(1)}, u32[]{:S(2)}, u32[]{:S(2)}) %collective-permute-start.6) | collective-permute-done | bytes 188448 | tf_op jit(solution)/shard_map/ppermute | solution.py:423
  54.0 0.9 %shard_map.32 = f32[8,32,128]{2,1,0:T(8,128)S(1)} custom-call(bf16[23,32,128]{2,1,0:T(8,128)(2,1)S(1)} %collective-permute-done.5.here_ref, bf16[23,32,128]{2,1,0:T(8,128)(2,1)S(1)} %collective-permute-done.6.there_ref, bf16[45,64,128]{2,1,0:T(8,128)(2,1)S(1)} %shard_map.29.own_ref.y_ref, bf16[45,32,128]{2,1,0:T(8,128)(2,1)S(1)} %get-tuple-element.16.own_ref), custom_call_target="tpu_custom_call" | custom-call | flops 1048576 | bytes 1048576 | tf_op jit(solution)/shard_map/pallas_call | solution.py:451
  54.9 10.3 %all_to_all.11.p_ref = f32[8,32,128]{2,1,0:T(8,128)S(1)} all-to-all(f32[8,32,128]{2,1,0:T(8,128)S(1)} %shard_map.32), channel_id=1, replica_groups=mesh['tm'=4,'lat'=4,'lon'=2] {'lat','lon'}, dimensions={0} | all-to-all | bytes 262144 | tf_op jit(solution)/shard_map/all_to_all | solution.py:427
  65.2 4.1 %shard_map.33 = bf16[45,64,128]{2,1,0:T(8,128)(2,1)} custom-call(f32[8,32,128]{2,1,0:T(8,128)S(1)} %all_to_all.11.p_ref, f32[32,32]{1,0:T(8,128)S(1)} %get-tuple-element.17.h_ref, f32[64,32]{1,0:T(8,128)S(1)} %get-tuple-element.18.c_ref, bf16[45,32,128]{2,1,0:T(8,128)(2,1)S(1)} %get-tuple-element.16.own_ref, ...), custom_call_target="tpu_custom_call" | custom-call | flops 1048576 | bytes 1048576 | tf_op jit(solution)/shard_map/pallas_call | solution.py:456
  (4 shorter events, 0.0 us)
Async XLA Ops:
  0.0 1.1 %copy-start = (bf16[64,45,128]{2,0,1:T(8,128)(2,1)S(1)}, bf16[64,45,128]{2,0,1:T(8,128)(2,1)}, u32[]{:S(2)}) copy-start(bf16[64,45,128]{2,0,1:T(8,128)(2,1)} %param.2) | copy-start | bytes 2211844
  1.1 0.7 %copy-start.2 = (f32[45,128]{1,0:T(8,128)S(1)}, f32[45,128]{1,0:T(8,128)}, u32[]{:S(2)}) copy-start(f32[45,128]{1,0:T(8,128)} %d_ref.3) | copy-start | bytes 69124
  1.9 13.7 %copy-start.1 = (bf16[64,45,128]{2,0,1:T(8,128)(2,1)S(1)}, bf16[64,45,128]{2,0,1:T(8,128)(2,1)}, u32[]{:S(2)}) copy-start(bf16[64,45,128]{2,0,1:T(8,128)(2,1)} %param.2) | copy-start | bytes 2211844
  2.4 5.1 %collective-permute-start = (bf16[208,128]{1,0:T(8,128)(2,1)S(1)}, bf16[208,128]{1,0:T(8,128)(2,1)S(1)}, u32[]{:S(2)}, u32[]{:S(2)}) collective-permute-start(bf16[208,128]{1,0:T(8,128)(2,1)S(1)} %get-tuple-element.12), channel_id=1, source_target_pairs={{0,1},{1,0},{2,3},{3,2},{4,5},{5,4},{6,7},{7,6},{8,9},{9,8},{10,11... | collective-permute-start | bytes 159752 | tf_op jit(solution)/shard_map/ppermute | solution.py:101
  7.5 8.1 %copy-start.3 = (f32[45,128]{1,0:T(8,128)S(1)}, f32[45,128]{1,0:T(8,128)}, u32[]{:S(2)}) copy-start(f32[45,128]{1,0:T(8,128)} %d_ref.3) | copy-start | bytes 69124
  7.5 5.7 %collective-permute-start.2 = (bf16[320,128]{1,0:T(8,128)(2,1)S(1)}, bf16[320,128]{1,0:T(8,128)(2,1)S(1)}, u32[]{:S(2)}, u32[]{:S(2)}) collective-permute-start(bf16[320,128]{1,0:T(8,128)(2,1)S(1)} %get-tuple-element.21), channel_id=1, source_target_pairs={{2,4},{4,2},{3,5},{5,3},{10,12},{12,10},{11,13},{13,11},{18,20},{2... | collective-permute-start | bytes 245768 | tf_op jit(solution)/shard_map/ppermute | solution.py:112
  8.2 7.4 %collective-permute-start.1 = (bf16[320,128]{1,0:T(8,128)(2,1)S(1)}, bf16[320,128]{1,0:T(8,128)(2,1)S(1)}, u32[]{:S(2)}, u32[]{:S(2)}) collective-permute-start(bf16[320,128]{1,0:T(8,128)(2,1)S(1)} %get-tuple-element.22), channel_id=1, source_target_pairs={{0,2},{4,6},{2,0},{6,4},{1,3},{5,7},{3,1},{7,5},{8,10},{12,14},{10... | collective-permute-start | bytes 245768 | tf_op jit(solution)/shard_map/ppermute | solution.py:112
  21.4 2.3 %collective-permute-start.3 = (bf16[45,64,128]{2,1,0:T(8,128)(2,1)S(1)}, bf16[45,64,128]{2,1,0:T(8,128)(2,1)S(1)}, u32[]{:S(2)}, u32[]{:S(2)}) collective-permute-start(bf16[45,64,128]{2,1,0:T(8,128)(2,1)S(1)} %shard_map.29.own_ref.y_ref), channel_id=1, source_target_pairs={{0,8},{8,0},{16,24},{24,16},{1,9},{9,1},{17,25},{25,17},{2,10},{10... | collective-permute-start | bytes 2211848 | tf_op jit(solution)/shard_map/ppermute | solution.py:423
  37.3 1.3 %collective-permute-start.4 = (f32[48,128]{1,0:T(8,128)S(1)}, f32[48,128]{1,0:T(8,128)S(1)}, u32[]{:S(2)}, u32[]{:S(2)}) collective-permute-start(f32[48,128]{1,0:T(8,128)S(1)} %reduce_sum.9.g_ref), channel_id=1, source_target_pairs={{0,8},{8,0},{16,24},{24,16},{1,9},{9,1},{17,25},{25,17},{2,10},{10... | collective-permute-start | bytes 73736 | tf_op jit(solution)/shard_map/ppermute | solution.py:423
  45.7 6.9 %collective-permute-start.5 = (bf16[23,32,128]{2,1,0:T(8,128)(2,1)S(1)}, bf16[23,32,128]{2,1,0:T(8,128)(2,1)S(1)}, u32[]{:S(2)}, u32[]{:S(2)}) collective-permute-start(bf16[23,32,128]{2,1,0:T(8,128)(2,1)S(1)} %get-tuple-element.15), channel_id=1, source_target_pairs={{0,16},{8,24},{16,0},{24,8},{1,17},{9,25},{17,1},{25,9},{2,18},{10... | collective-permute-start | bytes 565256 | tf_op jit(solution)/shard_map/ppermute | solution.py:423
  52.6 1.4 %collective-permute-start.6 = (bf16[23,32,128]{2,1,0:T(8,128)(2,1)S(1)}, bf16[23,32,128]{2,1,0:T(8,128)(2,1)S(1)}, u32[]{:S(2)}, u32[]{:S(2)}) collective-permute-start(bf16[23,32,128]{2,1,0:T(8,128)(2,1)S(1)} %collective-permute-done.5.here_ref), channel_id=1, source_target_pairs={{0,8},{8,0},{16,24},{24,16},{1,9},{9,1},{17,25},{25,17},{2,10},{10... | collective-permute-start | bytes 565256 | tf_op jit(solution)/shard_map/ppermute | solution.py:423

commit v5 on v4

--- a/solution.py
+++ b/solution.py
@@ -50,6 +50,10 @@
 def split2(v):
     high = v.astype(jnp.bfloat16)
     return high, (v - high.astype(jnp.float32)).astype(jnp.bfloat16)
+
+
+def odd(level):
+    return (lax.axis_index("tm") >> level & 1) == 1
 
 
 def even_lat():
@@ -252,50 +256,73 @@
     )
 
 
-def whitened(s, zt, block=16):
-    n = s.shape[0]
-    a = jnp.concatenate([s, zt], axis=1)
-    w = a.shape[1]
-    diagonal = lax.broadcasted_iota(jnp.int32, (n, w), 0) == lane_iota((n, w))
-    least = jnp.sum(jnp.where(diagonal, a, 0.0), axis=1, keepdims=True) * 1e-7 + 1e-37
-    floor = jnp.broadcast_to(least, (n, w))
+def inverse_factors(grams, block=16):
+    n = RANK
+    row = lax.broadcasted_iota(jnp.int32, (n, LANES), 0)
+    lane = lane_iota((n, LANES))
+    diagonal = row == lane % n
+    unit = diagonal.astype(jnp.float32)
+    first = lane // n * n
+    s = jnp.concatenate(list(grams) + [unit[:, :n]] * (LANES // n - len(grams)), axis=1)
+
+    def pivots(m):
+        return jnp.sum(jnp.where(diagonal, m, 0.0), axis=0, keepdims=True)
+
+    least = pivots(s) * 1e-7 + 1e-37
+    inv = unit
     done = []
     for k0 in range(0, n, block):
         tall = n - k0
-        row = lax.broadcasted_iota(jnp.int32, (tall, w), 0)
-        cols = [jnp.broadcast_to(a[:, k0 + j : k0 + j + 1], (tall, w)) for j in range(block)]
+        cols = [jnp.take_along_axis(s, (first + (k0 + j))[:tall], axis=1) for j in range(block)]
+        floor = [jnp.take_along_axis(jnp.broadcast_to(least, (8, LANES)), (first + (k0 + j))[:8], axis=1) for j in range(block)]
         for p in range(min(block, tall - 1)):
-            inverse = 1.0 / jnp.maximum(cols[p][p : p + 1, :], floor[k0 + p : k0 + p + 1, :])
-            below = jnp.where(row > p, cols[p], 0.0)
+            inverse = 1.0 / jnp.maximum(cols[p][p : p + 1], floor[p][0:1])
+            below = jnp.where(row[:tall] > p, cols[p], 0.0)
             for j in range(p + 1, block):
-                cols[j] = cols[j] - below * (cols[j][p : p + 1, :] * inverse)
-            a = a - below * (a[p : p + 1, :] * inverse)
-        done.append(a[:block])
-        a = a[block:]
-    a = jnp.concatenate(done, axis=0)
-    pivots = jnp.sum(jnp.where(diagonal, a, 0.0), axis=1, keepdims=True)
-    return a[:, n:] * lax.rsqrt(jnp.maximum(pivots, least))
-
-
-def power_basis(h, upper_first):
-    n = h.shape[0]
-    eye = lax.broadcasted_iota(jnp.int32, (n, n), 0) == lane_iota((n, n))
-    top = jnp.max(jnp.max(jnp.where(eye, h, 0.0), axis=1, keepdims=True), axis=0, keepdims=True)
-    unit = 1.0 / jnp.maximum(top, 1e-30)
-    h2 = mm(h, h) * (unit * unit)
-    start = h2[:RANK]
-    if upper_first is not None:
-        start = jnp.where(upper_first, h2[RANK:], start)
-    return mm(whitened(mmt(start, start), start), h2)
-
-
-def top_rows(h, upper_first=None):
-    zt = power_basis(h, upper_first)
-    return whitened(mmt(zt, zt), zt)
-
-
-def odd(level):
-    return (lax.axis_index("tm") >> level & 1) == 1
+                cols[j] = cols[j] - below * (cols[j][p : p + 1] * inverse)
+            s = s - below * (s[p : p + 1] * inverse)
+            inv = inv - below * (inv[p : p + 1] * inverse)
+        done.append((s[:block], inv[:block]))
+        s, inv = s[block:], inv[block:]
+    s, inv = (jnp.concatenate(v, axis=0) for v in zip(*done))
+    scale = lax.rsqrt(jnp.maximum(pivots(s), least))
+    out = []
+    for g in range(len(grams)):
+        seg = slice(n * g, n * g + n)
+        rows_scale = jnp.sum(jnp.where(diagonal[:, seg], scale[:, seg], 0.0), axis=1, keepdims=True)
+        out.append(inv[:, seg] * rows_scale)
+    return out
+
+
+def power_bases(hs, upper_first):
+    squares, starts = [], []
+    for h in hs:
+        n = h.shape[0]
+        on = lax.broadcasted_iota(jnp.int32, (n, n), 0) == lane_iota((n, n))
+        top = jnp.max(jnp.max(jnp.where(on, h, 0.0), axis=1, keepdims=True), axis=0, keepdims=True)
+        unit = 1.0 / jnp.maximum(top, 1e-30)
+        h2 = mm(h, h) * (unit * unit)
+        squares.append(h2)
+        starts.append(h2[:RANK] if upper_first is None else jnp.where(upper_first, h2[RANK:], h2[:RANK]))
+    factors = inverse_factors([mmt(z, z) for z in starts])
+    return [mm(mm(f, z), h2) for f, z, h2 in zip(factors, starts, squares)]
+
+
+def top_rows(hs, upper_first=None):
+    zs = power_bases(hs, upper_first)
+    return [mm(f, z) for f, z in zip(inverse_factors([mmt(z, z) for z in zs]), zs)]
+
+
+def diagonal_blocks(a, b):
+    top = jnp.concatenate([a, jnp.zeros((a.shape[0], b.shape[1]), a.dtype)], axis=1)
+    low = jnp.concatenate([jnp.zeros((b.shape[0], a.shape[1]), b.dtype), b], axis=1)
+    return jnp.concatenate([top, low], axis=0)
+
+
+def projection(gram, coef, upper_first):
+    zt = power_bases([gram], upper_first)[0]
+    r = mm(inverse_factors([mmt(mm(zt, gram), zt)])[0], zt)
+    return mm(mmt(coef, r), r)
 
 
 def pair_gram_body(own_ref, other_ref, o_ref):
@@ -325,11 +352,14 @@
     return block(g), block(gp), jnp.where(upper, flipped, cross), jnp.where(upper, cross, flipped)
 
 
-def put_modes(w, own_ref, other, modes_ref, part_ref):
+def put_rows(w, stacked, o_ref):
+    for i in range(o_ref.shape[0]):
+        o_ref[i] = jnp.dot(w, stacked(i), preferred_element_type=jnp.float32).astype(jnp.bfloat16)
+
+
+def put_modes(w, stacked, modes_ref, part_ref):
     rows, half = modes_ref.shape[0], part_ref.shape[0]
-    for i in range(rows):
-        stacked = jnp.concatenate([own_ref[i], other(i)], axis=0)
-        modes_ref[i] = jnp.dot(w, stacked, preferred_element_type=jnp.float32).astype(jnp.bfloat16)
+    put_rows(w, stacked, modes_ref)
     start = jnp.where(odd(0), rows - half, 0)
     for i in range(half):
         part_ref[i] = modes_ref[start + i]
@@ -348,25 +378,64 @@
     return row
 
 
-def leaf_body(g_ref, gp_ref, own_ref, other_ref, modes_ref, part_ref, h_ref, c_ref):
+def far_gram_body(own_ref, other_ref, far_ref, o_ref):
     n = own_ref.shape[1]
+    acc = None
+    for i in range(own_ref.shape[0]):
+        part = dot_t(jnp.concatenate([own_ref[i], other_ref[i]], axis=0), far_ref[i])
+        acc = part if acc is None else acc + part
+    packed = jnp.concatenate([acc[:n], acc[n:]], axis=1)
+    for j in range(o_ref.shape[0]):
+        o_ref[j] = packed
+
+
+def square(a, b, c, d):
+    return jnp.concatenate(
+        [jnp.concatenate([a, b], axis=1), jnp.concatenate([c, d], axis=1)], axis=0
+    )
+
+
+def pair_levels_body(g_ref, gp_ref, wh_ref, c_ref):
+    n = c_ref.shape[0]
     own, other, cross, flipped = pair_gram(g_ref[...], gp_ref[...], n)
-    q_own = top_rows(own)
-    q_other = top_rows(other)
-    gram = jnp.concatenate(
-        [jnp.concatenate([own, cross], axis=1), jnp.concatenate([flipped, other], axis=1)], axis=0
-    )
-    zero = jnp.zeros_like(q_own)
-    basis = jnp.concatenate(
-        [jnp.concatenate([q_own, zero], axis=1), jnp.concatenate([zero, q_other], axis=1)], axis=0
-    )
-    merged = mmt(mm(basis, gram), basis)
-    w = mm(top_rows(merged, odd(0)), basis).astype(jnp.bfloat16)
-    wf = w.astype(jnp.float32)
-    gw = mmt(gram, wf)
-    c_ref[...] = gw[:n]
-    h_ref[...] = mm(wf, gw)
-    put_modes(w, own_ref, lambda i: other_ref[i], modes_ref, part_ref)
+    gram = square(own, cross, flipped, other)
+    basis = diagonal_blocks(*top_rows([own, other]))
+    w = mm(top_rows([mmt(mm(basis, gram), basis)], odd(0))[0], basis)
+    on = mmt(gram, w)
+    c_ref[...] = on[:n]
+    h = mm(w, on)
+    wh_ref[...] = jnp.concatenate(
+        [w, jnp.concatenate([h, jnp.zeros((RANK, LANES - RANK), jnp.float32)], axis=1)], axis=0
+    )
+
+
+def quad_level(wh_ref, c_ref, far_wh_ref, cs_ref, twin_ref):
+    n = c_ref.shape[0]
+    cs, twin = cs_ref[...], twin_ref[...]
+    between = square(cs[:, :n], twin[:, n:], cs[:, n:], twin[:, :n])
+    wa, wb = wh_ref[:RANK, :], far_wh_ref[:RANK, :]
+    on_b = mmt(between, wb)
+    mixed = mm(wa, on_b)
+    gram = square(wh_ref[RANK:, :RANK], mixed, mixed.T, far_wh_ref[RANK:, :RANK])
+    return diagonal_blocks(wa, wb), gram, jnp.concatenate([c_ref[...], on_b[:n]], axis=1)
+
+
+def stack_of(*refs):
+    return lambda i: jnp.concatenate([ref[i] for ref in refs], axis=0)
+
+
+def quad_project_body(wh, c, far_wh, cs, twin, yo, yp, yy, yz, o_ref):
+    w, gram, coef = quad_level(wh, c, far_wh, cs, twin)
+    weights = mm(projection(gram, coef, odd(1)), w).astype(jnp.bfloat16)
+    put_rows(weights, stack_of(yo, yp, yy, yz), o_ref)
+
+
+def quad_modes_body(wh, c, far_wh, cs, twin, yo, yp, yy, yz, modes_ref, part_ref, h_ref, c_ref):
+    w, gram, coef = quad_level(wh, c, far_wh, cs, twin)
+    q = top_rows([gram], odd(1))[0]
+    h_ref[...] = mmt(mm(q, gram), q)
+    c_ref[...] = mmt(coef, q)
+    put_modes(mm(q, w).astype(jnp.bfloat16), stack_of(yo, yp, yy, yz), modes_ref, part_ref)
 
 
 def cross_body(here_ref, there_ref, y_ref, own_ref, o_ref):
@@ -399,23 +468,19 @@
 
 def merge_body(level, p_ref, h_ref, c_ref, own_ref, here_ref, there_ref, modes_ref, part_ref, hn_ref, cn_ref):
     gram, coef = merged_gram(p_ref, h_ref, c_ref, c_ref.shape[0])
-    w = top_rows(gram, odd(level)).astype(jnp.bfloat16)
+    w = top_rows([gram], odd(level))[0].astype(jnp.bfloat16)
     wf = w.astype(jnp.float32)
     cn_ref[...] = mmt(coef, wf)
     hn_ref[...] = mmt(mm(wf, gram), wf)
-    put_modes(w, own_ref, halves(own_ref.shape[0], here_ref, there_ref), modes_ref, part_ref)
+    other = halves(own_ref.shape[0], here_ref, there_ref)
+    put_modes(w, lambda i: jnp.concatenate([own_ref[i], other(i)], axis=0), modes_ref, part_ref)
 
 
 def project_body(level, p_ref, h_ref, c_ref, own_ref, here_ref, there_ref, o_ref):
     gram, coef = merged_gram(p_ref, h_ref, c_ref, c_ref.shape[0])
-    zt = power_basis(gram, odd(level))
-    r = whitened(mmt(mm(zt, gram), zt), zt)
-    weights = mm(mmt(coef, r), r).astype(jnp.bfloat16)
-    rows = own_ref.shape[0]
-    other = halves(rows, here_ref, there_ref)
-    for i in range(rows):
-        stacked = jnp.concatenate([own_ref[i], other(i)], axis=0)
-        o_ref[i] = jnp.dot(weights, stacked, preferred_element_type=jnp.float32).astype(jnp.bfloat16)
+    weights = projection(gram, coef, odd(level)).astype(jnp.bfloat16)
+    other = halves(own_ref.shape[0], here_ref, there_ref)
+    put_rows(weights, lambda i: jnp.concatenate([own_ref[i], other(i)], axis=0), o_ref)
 
 
 def exchanged(block, level):
@@ -435,17 +500,27 @@
     b16 = lambda *shape: jax.ShapeDtypeStruct(shape, jnp.bfloat16)
     x = jnp.transpose(residuals, (1, 0, 2))
     y = smooth(x, diffusivity, *halo_exchange(x, diffusivity))
-    other = exchanged(y, 0)
-    parts = gathered(kernel_call(pair_gram_body, f32(tiles, snaps * 3 // 4, 2 * snaps))(y, other))
-    gram = jnp.sum(parts, axis=0)
+    other, far = exchanged(y, 0), exchanged(y, 1)
+    pair = kernel_call(pair_gram_body, f32(tiles, snaps * 3 // 4, 2 * snaps))(y, other)
+    pair = jnp.sum(gathered(pair), axis=0)
+    cross = kernel_call(far_gram_body, f32(tiles, snaps, 2 * snaps))(y, other, far)
+    cross = jnp.sum(gathered(cross), axis=0)
+    wh, c = kernel_call(
+        pair_levels_body, (f32(2 * RANK, 2 * snaps), f32(snaps, RANK)), flops=1 << 32
+    )(pair, exchanged(pair, 0))
+    operands = (wh, c, exchanged(wh, 1), cross, exchanged(cross, 0))
+    operands += (y, other, far, exchanged(far, 0))
+    if levels == 2:
+        out = kernel_call(quad_project_body, b16(rows, snaps, width))(*operands)
+        return jnp.transpose(out, (1, 0, 2))
     block = (
         b16(rows, RANK, width),
         b16(-(-rows // 2), RANK, width),
         f32(RANK, RANK),
         f32(snaps, RANK),
     )
-    modes, part, h, c = kernel_call(leaf_body, block)(gram, exchanged(gram, 0), y, other)
-    for level in range(1, levels):
+    modes, part, h, c = kernel_call(quad_modes_body, block)(*operands)
+    for level in range(2, levels):
         here = exchanged(part, level)
         there = exchanged(here, 0)
         parts = gathered(kernel_call(cross_body, f32(tiles, RANK, snaps + 2 * RANK))(here, there, y, modes))

time: 69.7 us -> 62.8 us (0.901)
  blocking collectives: 22.6 us -> 0 us
  starting transfers between devices: 10.4 us -> 20.7 us
  waiting for transfers between devices: 14.6 us -> 18.9 us
  Pallas kernels: 19.8 us -> 20.8 us
    all_to_all x2 -> x0, blocking collectives: 22.6 us -> none  [gathered(): return lax.all_to_all(parts, ('lat', 'lon'), 0, 0, tiled=True)]
    all_to_all x0 -> x2, starting transfers between devices: none -> 8.44 us  [gathered(): return lax.all_to_all(parts, ('lat', 'lon'), 0, 0, tiled=True)]
    ppermute x4 -> x6, waiting for transfers between devices: 10.1 us -> 13.8 us  [exchanged(): lax.ppermute(block, 'tm', [(i, i ^ 1 << level) for i in range(count)])]
    ppermute x4 -> x6, starting transfers between devices: 1.73 us -> 3.59 us  [exchanged(): lax.ppermute(block, 'tm', [(i, i ^ 1 << level) for i in range(count)])]
    pallas_call x1, Pallas kernels: 1.3 us -> 2.02 us  [shards(): kernel_call(pair_gram_body, f32(tiles, snaps * 3 // 4, 2 * snaps))(y, other)]
  transfers between devices with their start and end apart: 7 -> 11, of which waited for: 6 -> 7; matrix products, arithmetic and copies ran while one was open for 0% -> 0% of each run, Pallas kernels for 0% -> 15%
where the time goes in v5:
time: 62.8 us; the launch traced here: 62.4 us
  Pallas kernels  20.8 us (33%)
  starting transfers between devices  20.7 us (33%)
  waiting for transfers between devices  18.9 us (30%)
  local copies, waits for them, and re-layouts  1.86 us (3%)
    ppermute x6, waiting for transfers between devices, exchanged(): lax.ppermute(block, 'tm', [(i, i ^ 1 << level) for i in range(count)])  13.8 us
    all_to_all x2, starting transfers between devices, gathered(): return lax.all_to_all(parts, ('lat', 'lon'), 0, 0, tiled=True)  8.44 us
    pallas_call x1, Pallas kernels, shards(): kernel_call(pair_levels_body, (f32(2 * RANK, 2 * snaps), f32(snaps, RANK)...  6.17 us
    pallas_call x1, Pallas kernels, smooth(): kernel_call(smooth_body, jax.ShapeDtypeStruct((rows, snaps, width), jnp.b...  5.78 us
    ppermute x2, starting transfers between devices, swapped(): return lax.ppermute(message, 'lat', pairs + [(j, i) for i, j in pairs])  5.66 us
    pallas_call x1, Pallas kernels, shards(): out = kernel_call(quad_project_body, b16(rows, snaps, width))(*operands)  5.06 us
    ppermute x6, starting transfers between devices, exchanged(): lax.ppermute(block, 'tm', [(i, i ^ 1 << level) for i in range(count)])  3.59 us
    ppermute x1, starting transfers between devices, halo_exchange(): side = lax.ppermute(packed, 'lon', forward)  2.97 us
  transfers between devices with their start and end apart: 11, of which 7 were waited for; matrix products, arithmetic and copies ran while one was open for 0% of the time, Pallas kernels for 15%

profile of v5, /device:TPU:0, one launch (start us, length us, event | category | flops | bytes accessed | tf_op | source)
XLA Modules:
  0.0 62.4 jit_solution(6277410185435783481)
XLA Ops:
  0.0 1.1 %copy-done = bf16[64,45,128]{2,0,1:T(8,128)(2,1)S(1)} copy-done((bf16[64,45,128]{2,0,1:T(8,128)(2,1)S(1)}, bf16[64,45,128]{2,0,1:T(8,128)(2,1)}, u32[]{:S(2)}) %copy-start) | copy-done | bytes 737304
  1.1 0.7 %copy-done.2 = f32[45,128]{1,0:T(8,128)S(1)} copy-done((f32[45,128]{1,0:T(8,128)S(1)}, f32[45,128]{1,0:T(8,128)}, u32[]{:S(2)}) %copy-start.2) | copy-done | bytes 23064
  1.9 0.5 shard_map.28
  2.4 3.0 %collective-permute-start = (bf16[208,128]{1,0:T(8,128)(2,1)S(1)}, bf16[208,128]{1,0:T(8,128)(2,1)S(1)}, u32[]{:S(2)}, u32[]{:S(2)}) collective-permute-start(bf16[208,128]{1,0:T(8,128)(2,1)S(1)} %get-tuple-element.10), channel_id=1, source_target_pairs={{0,1},{1,0},{2,3},{3,2},{4,5},{5,4},{6,7},{7,6},{8,9},{9,8},{10,11... | collective-permute-start | bytes 159752 | tf_op jit(solution)/shard_map/ppermute | solution.py:105
  5.3 2.1 %collective-permute-done.side_ref = bf16[208,128]{1,0:T(8,128)(2,1)S(1)} collective-permute-done((bf16[208,128]{1,0:T(8,128)(2,1)S(1)}, bf16[208,128]{1,0:T(8,128)(2,1)S(1)}, u32[]{:S(2)}, u32[]{:S(2)}) %collective-permute-start) | collective-permute-done | bytes 53280 | tf_op jit(solution)/shard_map/ppermute | solution.py:105
  7.5 0.7 %collective-permute-start.2 = (bf16[320,128]{1,0:T(8,128)(2,1)S(1)}, bf16[320,128]{1,0:T(8,128)(2,1)S(1)}, u32[]{:S(2)}, u32[]{:S(2)}) collective-permute-start(bf16[320,128]{1,0:T(8,128)(2,1)S(1)} %get-tuple-element.17), channel_id=1, source_target_pairs={{2,4},{4,2},{3,5},{5,3},{10,12},{12,10},{11,13},{13,11},{18,20},{2... | collective-permute-start | bytes 245768 | tf_op jit(solution)/shard_map/ppermute | solution.py:116
  8.2 5.0 %collective-permute-start.1 = (bf16[320,128]{1,0:T(8,128)(2,1)S(1)}, bf16[320,128]{1,0:T(8,128)(2,1)S(1)}, u32[]{:S(2)}, u32[]{:S(2)}) collective-permute-start(bf16[320,128]{1,0:T(8,128)(2,1)S(1)} %get-tuple-element.18), channel_id=1, source_target_pairs={{0,2},{4,6},{2,0},{6,4},{1,3},{5,7},{3,1},{7,5},{8,10},{12,14},{10... | collective-permute-start | bytes 245768 | tf_op jit(solution)/shard_map/ppermute | solution.py:116
  13.1 0.0 collective-permute-done.2.b_ref
  13.2 2.4 %collective-permute-done.1.a_ref = bf16[320,128]{1,0:T(8,128)(2,1)S(1)} collective-permute-done((bf16[320,128]{1,0:T(8,128)(2,1)S(1)}, bf16[320,128]{1,0:T(8,128)(2,1)S(1)}, u32[]{:S(2)}, u32[]{:S(2)}) %collective-permute-start.1) | collective-permute-done | bytes 81952 | tf_op jit(solution)/shard_map/ppermute | solution.py:116
  15.6 0.0 copy-done.1
  15.6 0.0 copy-done.3
  15.6 5.8 %shard_map.29.own_ref.yo = bf16[45,64,128]{2,1,0:T(8,128)(2,1)S(1)} custom-call(bf16[45,64,128]{2,1,0:T(8,128)(2,1)S(1)} %bitcast.3, f32[45,128]{1,0:T(8,128)S(1)} %copy-done.3, bf16[208,128]{1,0:T(8,128)(2,1)S(1)} %collective-permute-done.side_ref, bf16[320,128]{1,0:T(8,128)(2,1)S(1)} %collective-permute-done.1.a_ref, ...), custom_call_target="tpu_custom_call" | custom-call | flops 1048576 | bytes 1048576 | tf_op jit(solution)/shard_map/pallas_call | solution.py:242
  21.4 0.1 collective-permute-start.3
  21.4 1.6 %collective-permute-start.6 = (bf16[45,64,128]{2,1,0:T(8,128)(2,1)S(1)}, bf16[45,64,128]{2,1,0:T(8,128)(2,1)S(1)}, u32[]{:S(2)}, u32[]{:S(2)}) collective-permute-start(bf16[45,64,128]{2,1,0:T(8,128)(2,1)S(1)} %shard_map.29.own_ref.yo), channel_id=1, source_target_pairs={{0,16},{8,24},{16,0},{24,8},{1,17},{9,25},{17,1},{25,9},{2,18},{10... | collective-permute-start | bytes 2211848 | tf_op jit(solution)/shard_map/ppermute | solution.py:488
  23.0 0.6 collective-permute-done.3.other_ref.yp
  23.6 2.0 %shard_map.30 = f32[8,48,128]{2,1,0:T(8,128)} custom-call(bf16[45,64,128]{2,1,0:T(8,128)(2,1)S(1)} %shard_map.29.own_ref.yo, bf16[45,64,128]{2,1,0:T(8,128)(2,1)S(1)} %collective-permute-done.3.other_ref.yp), custom_call_target="tpu_custom_call" | custom-call | flops 1048576 | bytes 1048576 | tf_op jit(solution)/shard_map/pallas_call | solution.py:504
  25.7 4.2 %all-to-all-start = ((f32[8,48,128]{2,1,0:T(8,128)}), f32[8,48,128]{2,1,0:T(8,128)S(1)}, u32[]{:S(2)}, u32[]{:S(2)}) async-start(f32[8,48,128]{2,1,0:T(8,128)} %shard_map.30), calls=%async_computation | async-start | bytes 393216 | tf_op jit(solution)/shard_map/all_to_all | solution.py:492
  29.9 10.5 %collective-permute-done.6.far_ref.yy = bf16[45,64,128]{2,1,0:T(8,128)(2,1)S(1)} collective-permute-done((bf16[45,64,128]{2,1,0:T(8,128)(2,1)S(1)}, bf16[45,64,128]{2,1,0:T(8,128)(2,1)S(1)}, u32[]{:S(2)}, u32[]{:S(2)}) %collective-permute-start.6) | collective-permute-done | bytes 737312 | tf_op jit(solution)/shard_map/ppermute | solution.py:488
  40.3 0.0 collective-permute-start.8
  40.3 1.3 %shard_map.32 = f32[8,64,128]{2,1,0:T(8,128)} custom-call(bf16[45,64,128]{2,1,0:T(8,128)(2,1)S(1)} %shard_map.29.own_ref.yo, bf16[45,64,128]{2,1,0:T(8,128)(2,1)S(1)} %collective-permute-done.3.other_ref.yp, bf16[45,64,128]{2,1,0:T(8,128)(2,1)S(1)} %collective-permute-done.6.far_ref.yy), custom_call_target="tpu_custom_call" | custom-call | flops 1048576 | bytes 1048576 | tf_op jit(solution)/shard_map/pallas_call | solution.py:506
  41.7 0.0 all-to-all-done
  41.7 4.2 %all-to-all-start.1 = ((f32[8,64,128]{2,1,0:T(8,128)}), f32[8,64,128]{2,1,0:T(8,128)S(1)}, u32[]{:S(2)}, u32[]{:S(2)}) async-start(f32[8,64,128]{2,1,0:T(8,128)} %shard_map.32), calls=%async_computation.1 | async-start | bytes 524288 | tf_op jit(solution)/shard_map/all_to_all | solution.py:492
  45.9 0.3 collective-permute-start.4
  46.2 1.0 %collective-permute-done.4.gp_ref = f32[48,128]{1,0:T(8,128)S(1)} collective-permute-done((f32[48,128]{1,0:T(8,128)S(1)}, f32[48,128]{1,0:T(8,128)S(1)}, u32[]{:S(2)}, u32[]{:S(2)}) %collective-permute-start.4) | collective-permute-done | bytes 24608 | tf_op jit(solution)/shard_map/ppermute | solution.py:488
  47.2 6.2 %shard_map.31 = (f32[64,128]{1,0:T(8,128)S(1)}, f32[64,32]{1,0:T(8,128)S(1)}) custom-call(f32[48,128]{1,0:T(8,128)S(1)} %reduce_sum.18.g_ref, f32[48,128]{1,0:T(8,128)S(1)} %collective-permute-done.4.gp_ref), custom_call_target="tpu_custom_call" | custom-call | flops 4294967296 | bytes 1048576 | tf_op jit(solution)/shard_map/pallas_call | solution.py:508
  53.3 1.6 %collective-permute-start.5 = (f32[64,128]{1,0:T(8,128)S(1)}, f32[64,128]{1,0:T(8,128)S(1)}, u32[]{:S(2)}, u32[]{:S(2)}) collective-permute-start(f32[64,128]{1,0:T(8,128)S(1)} %get-tuple-element.13.wh), channel_id=1, source_target_pairs={{0,16},{8,24},{16,0},{24,8},{1,17},{9,25},{17,1},{25,9},{2,18},{10... | collective-permute-start | bytes 98312 | tf_op jit(solution)/shard_map/ppermute | solution.py:488
  54.9 0.6 all-to-all-done.1
  55.5 0.1 collective-permute-start.7
  55.6 1.7 %collective-permute-done.5.far_wh = f32[64,128]{1,0:T(8,128)S(1)} collective-permute-done((f32[64,128]{1,0:T(8,128)S(1)}, f32[64,128]{1,0:T(8,128)S(1)}, u32[]{:S(2)}, u32[]{:S(2)}) %collective-permute-start.5) | collective-permute-done | bytes 32800 | tf_op jit(solution)/shard_map/ppermute | solution.py:488
  57.3 0.0 collective-permute-done.7.twin
  57.3 0.0 collective-permute-done.8.yz
  57.3 5.1 %shard_map.33 = bf16[45,64,128]{2,1,0:T(8,128)(2,1)} custom-call(f32[64,128]{1,0:T(8,128)S(1)} %get-tuple-element.13.wh, f32[64,32]{1,0:T(8,128)S(1)} %get-tuple-element.14.c, f32[64,128]{1,0:T(8,128)S(1)} %collective-permute-done.5.far_wh, f32[64,128]{1,0:T(8,128)S(1)} %reduce_sum.19.cs, f32[64,128]{1,0:T(8,128)S(1)} %collective-permute-done.7.twin, ...), custom_call_target="tpu_custom_call" | custom-call | flops 1048576 | bytes 1048576 | tf_op jit(solution)/shard_map/pallas_call | solution.py:514
  (9 shorter events, 0.1 us)
Async XLA Ops:
  0.0 1.1 %copy-start = (bf16[64,45,128]{2,0,1:T(8,128)(2,1)S(1)}, bf16[64,45,128]{2,0,1:T(8,128)(2,1)}, u32[]{:S(2)}) copy-start(bf16[64,45,128]{2,0,1:T(8,128)(2,1)} %param.2) | copy-start | bytes 2211844
  1.1 0.7 %copy-start.2 = (f32[45,128]{1,0:T(8,128)S(1)}, f32[45,128]{1,0:T(8,128)}, u32[]{:S(2)}) copy-start(f32[45,128]{1,0:T(8,128)} %d_ref.3) | copy-start | bytes 69124
  1.9 13.7 %copy-start.1 = (bf16[64,45,128]{2,0,1:T(8,128)(2,1)S(1)}, bf16[64,45,128]{2,0,1:T(8,128)(2,1)}, u32[]{:S(2)}) copy-start(bf16[64,45,128]{2,0,1:T(8,128)(2,1)} %param.2) | copy-start | bytes 2211844
  2.4 5.1 %collective-permute-start = (bf16[208,128]{1,0:T(8,128)(2,1)S(1)}, bf16[208,128]{1,0:T(8,128)(2,1)S(1)}, u32[]{:S(2)}, u32[]{:S(2)}) collective-permute-start(bf16[208,128]{1,0:T(8,128)(2,1)S(1)} %get-tuple-element.10), channel_id=1, source_target_pairs={{0,1},{1,0},{2,3},{3,2},{4,5},{5,4},{6,7},{7,6},{8,9},{9,8},{10,11... | collective-permute-start | bytes 159752 | tf_op jit(solution)/shard_map/ppermute | solution.py:105
  7.5 8.1 %copy-start.3 = (f32[45,128]{1,0:T(8,128)S(1)}, f32[45,128]{1,0:T(8,128)}, u32[]{:S(2)}) copy-start(f32[45,128]{1,0:T(8,128)} %d_ref.3) | copy-start | bytes 69124
  7.5 5.7 %collective-permute-start.2 = (bf16[320,128]{1,0:T(8,128)(2,1)S(1)}, bf16[320,128]{1,0:T(8,128)(2,1)S(1)}, u32[]{:S(2)}, u32[]{:S(2)}) collective-permute-start(bf16[320,128]{1,0:T(8,128)(2,1)S(1)} %get-tuple-element.17), channel_id=1, source_target_pairs={{2,4},{4,2},{3,5},{5,3},{10,12},{12,10},{11,13},{13,11},{18,20},{2... | collective-permute-start | bytes 245768 | tf_op jit(solution)/shard_map/ppermute | solution.py:116
  8.2 7.4 %collective-permute-start.1 = (bf16[320,128]{1,0:T(8,128)(2,1)S(1)}, bf16[320,128]{1,0:T(8,128)(2,1)S(1)}, u32[]{:S(2)}, u32[]{:S(2)}) collective-permute-start(bf16[320,128]{1,0:T(8,128)(2,1)S(1)} %get-tuple-element.18), channel_id=1, source_target_pairs={{0,2},{4,6},{2,0},{6,4},{1,3},{5,7},{3,1},{7,5},{8,10},{12,14},{10... | collective-permute-start | bytes 245768 | tf_op jit(solution)/shard_map/ppermute | solution.py:116
  21.4 2.3 %collective-permute-start.3 = (bf16[45,64,128]{2,1,0:T(8,128)(2,1)S(1)}, bf16[45,64,128]{2,1,0:T(8,128)(2,1)S(1)}, u32[]{:S(2)}, u32[]{:S(2)}) collective-permute-start(bf16[45,64,128]{2,1,0:T(8,128)(2,1)S(1)} %shard_map.29.own_ref.yo), channel_id=1, source_target_pairs={{0,8},{8,0},{16,24},{24,16},{1,9},{9,1},{17,25},{25,17},{2,10},{10... | collective-permute-start | bytes 2211848 | tf_op jit(solution)/shard_map/ppermute | solution.py:488
  21.4 18.9 %collective-permute-start.6 = (bf16[45,64,128]{2,1,0:T(8,128)(2,1)S(1)}, bf16[45,64,128]{2,1,0:T(8,128)(2,1)S(1)}, u32[]{:S(2)}, u32[]{:S(2)}) collective-permute-start(bf16[45,64,128]{2,1,0:T(8,128)(2,1)S(1)} %shard_map.29.own_ref.yo), channel_id=1, source_target_pairs={{0,16},{8,24},{16,0},{24,8},{1,17},{9,25},{17,1},{25,9},{2,18},{10... | collective-permute-start | bytes 2211848 | tf_op jit(solution)/shard_map/ppermute | solution.py:488
  25.7 16.0 %all-to-all-start = ((f32[8,48,128]{2,1,0:T(8,128)}), f32[8,48,128]{2,1,0:T(8,128)S(1)}, u32[]{:S(2)}, u32[]{:S(2)}) async-start(f32[8,48,128]{2,1,0:T(8,128)} %shard_map.30), calls=%async_computation | async-start | bytes 393216 | tf_op jit(solution)/shard_map/all_to_all | solution.py:492
  40.3 17.0 %collective-permute-start.8 = (bf16[45,64,128]{2,1,0:T(8,128)(2,1)S(1)}, bf16[45,64,128]{2,1,0:T(8,128)(2,1)S(1)}, u32[]{:S(2)}, u32[]{:S(2)}) collective-permute-start(bf16[45,64,128]{2,1,0:T(8,128)(2,1)S(1)} %collective-permute-done.6.far_ref.yy), channel_id=1, source_target_pairs={{0,8},{8,0},{16,24},{24,16},{1,9},{9,1},{17,25},{25,17},{2,10},{10... | collective-permute-start | bytes 2211848 | tf_op jit(solution)/shard_map/ppermute | solution.py:488
  41.7 13.8 %all-to-all-start.1 = ((f32[8,64,128]{2,1,0:T(8,128)}), f32[8,64,128]{2,1,0:T(8,128)S(1)}, u32[]{:S(2)}, u32[]{:S(2)}) async-start(f32[8,64,128]{2,1,0:T(8,128)} %shard_map.32), calls=%async_computation.1 | async-start | bytes 524288 | tf_op jit(solution)/shard_map/all_to_all | solution.py:492
  45.9 1.3 %collective-permute-start.4 = (f32[48,128]{1,0:T(8,128)S(1)}, f32[48,128]{1,0:T(8,128)S(1)}, u32[]{:S(2)}, u32[]{:S(2)}) collective-permute-start(f32[48,128]{1,0:T(8,128)S(1)} %reduce_sum.18.g_ref), channel_id=1, source_target_pairs={{0,8},{8,0},{16,24},{24,16},{1,9},{9,1},{17,25},{25,17},{2,10},{10... | collective-permute-start | bytes 73736 | tf_op jit(solution)/shard_map/ppermute | solution.py:488
  53.3 4.0 %collective-permute-start.5 = (f32[64,128]{1,0:T(8,128)S(1)}, f32[64,128]{1,0:T(8,128)S(1)}, u32[]{:S(2)}, u32[]{:S(2)}) collective-permute-start(f32[64,128]{1,0:T(8,128)S(1)} %get-tuple-element.13.wh), channel_id=1, source_target_pairs={{0,16},{8,24},{16,0},{24,8},{1,17},{9,25},{17,1},{25,9},{2,18},{10... | collective-permute-start | bytes 98312 | tf_op jit(solution)/shard_map/ppermute | solution.py:488
  55.5 1.8 %collective-permute-start.7 = (f32[64,128]{1,0:T(8,128)S(1)}, f32[64,128]{1,0:T(8,128)S(1)}, u32[]{:S(2)}, u32[]{:S(2)}) collective-permute-start(f32[64,128]{1,0:T(8,128)S(1)} %reduce_sum.19.cs), channel_id=1, source_target_pairs={{0,8},{8,0},{16,24},{24,16},{1,9},{9,1},{17,25},{25,17},{2,10},{10... | collective-permute-start | bytes 98312 | tf_op jit(solution)/shard_map/ppermute | solution.py:488

commit v6 on v5

--- a/solution.py
+++ b/solution.py
@@ -19,13 +19,14 @@
     return pl.BlockSpec(memory_space=VMEM)
 
 
-def kernel_call(body, outs, scratch=(), flops=1 << 20):
+def kernel_call(body, outs, scratch=(), flops=1 << 20, specs=None, vmem=48 << 20):
     return pl.pallas_call(
         body,
         out_shape=outs,
+        **({} if specs is None else {"in_specs": specs}),
         out_specs=jax.tree.map(lambda _: whole(), outs),
         scratch_shapes=list(scratch),
-        compiler_params=pltpu.CompilerParams(vmem_limit_bytes=48 << 20),
+        compiler_params=pltpu.CompilerParams(vmem_limit_bytes=vmem),
         cost_estimate=pl.CostEstimate(flops=flops, bytes_accessed=1 << 20, transcendentals=0),
     )
 
@@ -60,62 +61,110 @@
     return lax.axis_index("lat") % 2 == 0
 
 
-def pack_body(x_ref, d_ref, m_ref, a_ref, b_ref):
+def edge_body(x_hbm, d_hbm, a_ref, b_ref, d_ref, sems):
+    rows, snaps, width = x_hbm.shape
+    even = even_lat()
+    flags = ((a_ref, even), (b_ref, jnp.logical_not(even)))
+    copies = [pltpu.make_async_copy(d_hbm, d_ref, sems.at[0])]
+    for ref, south in flags:
+        start = jnp.where(south, rows - PASSES, 0)
+        for r in range(PASSES):
+            copies.append(
+                pltpu.make_async_copy(
+                    x_hbm.at[start + r], ref.at[pl.ds(r * snaps, snaps)], sems.at[len(copies)]
+                )
+            )
+    for copy in copies:
+        copy.start()
+    copies[0].wait()
+    pad = jnp.zeros((8, width), jnp.float32)
+    edge = lambda lo: [v.astype(jnp.float32) for v in split2(d_ref[lo : lo + PASSES, :])]
+    first, final = edge(0), edge(rows - PASSES)
+    for ref, south in flags:
+        term = [jnp.where(south, f, g) for f, g in zip(final, first)]
+        ref[PASSES * snaps :, :] = jnp.concatenate(term + [pad], axis=0).astype(jnp.bfloat16)
+    for copy in copies[1:]:
+        copy.wait()
+
+
+def by_side(a_ref, b_ref):
+    even = even_lat()
+
+    def picked(lo, hi):
+        a, b = a_ref[lo:hi, :], b_ref[lo:hi, :]
+        return jnp.where(even, b, a), jnp.where(even, a, b)
+
+    return picked
+
+
+def tile_rows(x_ref, north, south, t):
+    rows, snaps, _ = x_ref.shape
+    first = north[(t + PASSES) * snaps : (t + PASSES + 1) * snaps] if t < 0 else x_ref[t]
+    r = t + rows // 2
+    second = x_ref[r] if r < rows else south[(r - rows) * snaps : (r - rows + 1) * snaps]
+    return jnp.concatenate([first, second], axis=0)
+
+
+def extend_rows(dn, d_ref, north_d, south_d):
+    rows = d_ref.shape[0]
+    dn[...] = jnp.zeros(dn.shape, jnp.float32)
+    dn[PASSES : PASSES + rows, :] = d_ref[...]
+    dn[0:PASSES, :] = north_d[0:PASSES] + north_d[PASSES : 2 * PASSES]
+    dn[PASSES + rows : 2 * PASSES + rows, :] = south_d[0:PASSES] + south_d[PASSES : 2 * PASSES]
+
+
+def pack_body(x_ref, d_ref, b_ref, a_ref, m_ref, dn):
     rows, snaps, width = x_ref.shape
     half = -(-rows // 2)
+    count = half + 2 * PASSES
+    edge = PASSES * snaps
     row = lax.broadcasted_iota(jnp.int32, (16, width), 0)
     lane = lane_iota((16, width))
     column = jnp.where(row % 8 < PASSES, row % 8, width - 8 + row % 8)
     pick = [((lane == column) & (row // 8 == k)).astype(jnp.bfloat16) for k in range(2)]
-
-    def tile(t):
-        return jnp.concatenate([x_ref[t], x_ref[t + rows - half]], axis=0)
-
-    for t in range(0, half, 2):
-        out = dot_t(pick[0], tile(t))
-        if t + 1 < half:
-            out = out + dot_t(pick[1], tile(t + 1))
-        m_ref[8 * t : 8 * t + 16, :] = out.astype(jnp.bfloat16)
-    d = d_ref[...]
-    high, low = split2(jnp.concatenate([d, jnp.zeros((width - rows, width), jnp.float32)], axis=0))
+    picked = by_side(a_ref, b_ref)
+    north, south = picked(0, edge)
+    north_d, south_d = (v.astype(jnp.float32) for v in picked(edge, edge + 16))
+    for k in range(0, count, 2):
+        out = dot_t(pick[0], tile_rows(x_ref, north, south, k - PASSES))
+        if k + 1 < count:
+            out = out + dot_t(pick[1], tile_rows(x_ref, north, south, k + 1 - PASSES))
+        m_ref[8 * k : 8 * k + 16, :] = out.astype(jnp.bfloat16)
+    extend_rows(dn, d_ref, north_d, south_d)
+    high, low = split2(dn[...])
     end = m_ref.shape[0]
     m_ref[end - 16 :, :] = (dot_t(pick[0], high) + dot_t(pick[1], low)).astype(jnp.bfloat16)
 
-    even = even_lat()
-    pad = jnp.zeros((8, width), jnp.float32)
-    edge = lambda lo: [v.astype(jnp.float32) for v in split2(d[lo : lo + PASSES])]
-    first, final = edge(0), edge(rows - PASSES)
-    for ref, south in ((a_ref, even), (b_ref, jnp.logical_not(even))):
-        start = jnp.where(south, rows - PASSES, 0)
-        for r in range(PASSES):
-            ref[r * snaps : (r + 1) * snaps, :] = x_ref[start + r]
-        term = [jnp.where(south, f, g) for f, g in zip(final, first)]
-        ref[PASSES * snaps :, :] = jnp.concatenate(term + [pad], axis=0).astype(jnp.bfloat16)
-
 
 def halo_exchange(x, d):
     rows, snaps, width = x.shape
-    half = -(-rows // 2)
-    tiles = 16 * (-(-half // 2))
+    count = -(-rows // 2) + 2 * PASSES
     shape = lambda n: jax.ShapeDtypeStruct((n, width), jnp.bfloat16)
     edge = PASSES * snaps + 16
-    packed, a, b = kernel_call(pack_body, (shape(tiles + 16), shape(edge), shape(edge)))(x, d)
+    hbm = pl.BlockSpec(memory_space=pltpu.HBM)
+    a, b = kernel_call(
+        edge_body,
+        (shape(edge), shape(edge)),
+        [VMEM(d.shape, d.dtype), pltpu.SemaphoreType.DMA((2 * PASSES + 1,))],
+        specs=[hbm, hbm],
+        vmem=60 << 20,
+    )(x, d)
     lons, lats = lax.axis_size("lon"), lax.axis_size("lat")
+
+    def swapped(message, start):
+        pairs = [(i, i + 1) for i in range(start, lats - 1, 2)]
+        return lax.ppermute(message, "lat", pairs + [(j, i) for i, j in pairs])
+
+    a, b = swapped(a, 0), swapped(b, 1)
+    packed = kernel_call(
+        pack_body, shape(16 * (-(-count // 2)) + 16), [VMEM((width, LANES), jnp.float32)]
+    )(x, d, b, a)
     forward = [(i, (i + 1) % lons) for i in range(lons)]
     side = lax.ppermute(packed, "lon", forward)
     if lons > 2:
         from_east = lax.ppermute(packed, "lon", [(j, i) for i, j in forward])
         side = jnp.where(lax.broadcasted_iota(jnp.int32, side.shape, 0) % 8 < PASSES, from_east, side)
-    even = even_lat()
-    corner = 8 * PASSES
-    north_corner, south_corner = side[:corner], side[8 * (half - PASSES) : 8 * half]
-
-    def swapped(base, south, start):
-        message = jnp.concatenate([base, jnp.where(south, south_corner, north_corner), side[tiles:]])
-        pairs = [(i, i + 1) for i in range(start, lats - 1, 2)]
-        return lax.ppermute(message, "lat", pairs + [(j, i) for i, j in pairs])
-
-    return side, swapped(a, even, 0), swapped(b, jnp.logical_not(even), 1)
+    return side, a, b
 
 
 PADDED = 160
@@ -127,57 +176,27 @@
     shift = rows - half
     count = half + 2 * PASSES
     lats, lat = lax.axis_size("lat"), lax.axis_index("lat")
-    even = even_lat()
     lane = lane_iota((1, LANES))
     left = lane < snaps
     own = 16
     east = own + width
     unit = eye(width)
     edge = PASSES * snaps
-    corner = edge + 16
-    tail = corner + 8 * PASSES
-    tiles = side_ref.shape[0] - 16
-
-    def picked(lo, hi):
-        a, b = a_ref[lo:hi, :], b_ref[lo:hi, :]
-        return jnp.where(even, b, a), jnp.where(even, a, b)
-
+    picked = by_side(a_ref, b_ref)
     north, south = picked(0, edge)
-    north_corner, south_corner = (v.astype(jnp.float32) for v in picked(corner, tail))
-    north_d, south_d = (v.astype(jnp.float32) for v in picked(edge, corner))
-    north_t, south_t = (v.astype(jnp.float32) for v in picked(tail, tail + 16))
-    side = lambda t: side_ref[16 * (t // 2) : 16 * (t // 2) + 16, :].astype(jnp.float32)[
-        8 * (t % 2) : 8 * (t % 2) + 8
-    ]
+    north_d, south_d = (v.astype(jnp.float32) for v in picked(edge, edge + 16))
 
     for k in range(count):
-        t = k - PASSES
-        first = north[k * snaps : (k + 1) * snaps] if t < 0 else x_ref[t]
-        r = t + shift
-        second = x_ref[r] if r < rows else south[(r - rows) * snaps : (r - rows + 1) * snaps]
-        u0[k, own:east, :] = dot_t(unit, jnp.concatenate([first, second], axis=0))
-        if t < 0:
-            halo = roll(jnp.where(left, side(r), north_corner[8 * k : 8 * k + 8]), snaps)
-        elif t >= half:
-            j = t - half
-            halo = roll(jnp.where(left, south_corner[8 * j : 8 * j + 8], side(t - shift)), snaps)
-        else:
-            halo = side(t)
+        u0[k, own:east, :] = dot_t(unit, tile_rows(x_ref, north, south, k - PASSES))
+        pair = side_ref[16 * (k // 2) : 16 * (k // 2) + 16, :].astype(jnp.float32)
+        halo = pair[8 * (k % 2) : 8 * (k % 2) + 8]
         u0[k, own - 8 : own, :] = halo
         u0[k, east : east + 8, :] = halo
 
-    dn[...] = jnp.zeros(dn.shape, jnp.float32)
-    dn[PASSES : PASSES + rows, :] = d_ref[...]
-    dn[0:PASSES, :] = north_d[0:PASSES] + north_d[PASSES : 2 * PASSES]
-    dn[PASSES + rows : 2 * PASSES + rows, :] = south_d[0:PASSES] + south_d[PASSES : 2 * PASSES]
+    extend_rows(dn, d_ref, north_d, south_d)
     dt[own:east, :] = dn[...].T
-    side_d = side_ref[tiles:, :].astype(jnp.float32)
-    fold = lambda v: v[0:8] + v[8:16]
-    halo = jnp.where(
-        lane < PASSES,
-        roll(fold(north_t), PASSES - rows),
-        jnp.where(lane < PASSES + rows, roll(fold(side_d), PASSES), roll(fold(south_t), PASSES + rows)),
-    )
+    side_d = side_ref[side_ref.shape[0] - 16 :, :].astype(jnp.float32)
+    halo = side_d[0:8] + side_d[8:16]
     dt[0 : own - 8, :] = jnp.zeros((own - 8, LANES), jnp.float32)
     dt[own - 8 : own, :] = halo
     dt[east : east + 8, :] = halo
@@ -199,21 +218,34 @@
         cs[k, low:high, :] = spread[high - low :]
 
     buffers = (u0, u1)
+    first_row = lax.broadcasted_iota(jnp.int32, (8, LANES), 0) == 0
     for step in range(PASSES):
         src, dst = buffers[step % 2], buffers[(step + 1) % 2]
         final = step == PASSES - 1
         start, stop = step + 1, count - 1 - step
-        for r in range(own if final else low, east if final else high, 8):
-            here = slice(r, r + 8)
-            current = src[start, here, :]
-            above = cs[start - 1, here, :] * (current - src[start - 1, here, :])
-            for k in range(start, stop):
-                below = src[k + 1, here, :]
-                southward = cs[k, here, :] * (below - current)
-                eastward = ce[k, here, :] * (src[k, r + 1 : r + 9, :] - current)
-                westward = ce[k, r - 1 : r + 7, :] * (current - src[k, r - 1 : r + 7, :])
-                dst[k, here, :] = current + ((southward - above) + (eastward - westward))
-                current, above = below, southward
+        blocks = range(own, east, 8) if final else range(low, high, 8)
+        current = [src[start, r : r + 8, :] for r in blocks]
+        above = [
+            cs[start - 1, r : r + 8, :] * (c - src[start - 1, r : r + 8, :])
+            for r, c in zip(blocks, current)
+        ]
+
+        def eastward(k, r, here):
+            return ce[k, r : r + 8, :] * (src[k, r + 1 : r + 9, :] - here)
+
+        for k in range(start, stop):
+            before = None
+            if final:
+                before = pltpu.roll(eastward(k, low, src[k, low:own, :]), 1, 0)
+            for i, r in enumerate(blocks):
+                here = current[i]
+                east_flux = eastward(k, r, here)
+                turned = pltpu.roll(east_flux, 1, 0)
+                west_flux = turned if before is None else jnp.where(first_row, before, turned)
+                below = src[k + 1, r : r + 8, :]
+                south_flux = cs[k, r : r + 8, :] * (below - here)
+                dst[k, r : r + 8, :] = here + ((south_flux - above[i]) + (east_flux - west_flux))
+                current[i], above[i], before = below, south_flux, turned
         if not final:
 
             @pl.when(lat == 0)
@@ -268,15 +300,14 @@
     def pivots(m):
         return jnp.sum(jnp.where(diagonal, m, 0.0), axis=0, keepdims=True)
 
-    least = pivots(s) * 1e-7 + 1e-37
+    least = jnp.max(pivots(s), axis=1, keepdims=True) * 1e-12 + 1e-37
     inv = unit
     done = []
     for k0 in range(0, n, block):
         tall = n - k0
         cols = [jnp.take_along_axis(s, (first + (k0 + j))[:tall], axis=1) for j in range(block)]
-        floor = [jnp.take_along_axis(jnp.broadcast_to(least, (8, LANES)), (first + (k0 + j))[:8], axis=1) for j in range(block)]
         for p in range(min(block, tall - 1)):
-            inverse = 1.0 / jnp.maximum(cols[p][p : p + 1], floor[p][0:1])
+            inverse = 1.0 / jnp.maximum(cols[p][p : p + 1], least)
             below = jnp.where(row[:tall] > p, cols[p], 0.0)
             for j in range(p + 1, block):
                 cols[j] = cols[j] - below * (cols[j][p : p + 1] * inverse)
@@ -319,10 +350,11 @@
     return jnp.concatenate([top, low], axis=0)
 
 
-def projection(gram, coef, upper_first):
+def projection(gram, coef, upper_first, w=None):
     zt = power_bases([gram], upper_first)[0]
-    r = mm(inverse_factors([mmt(mm(zt, gram), zt)])[0], zt)
-    return mm(mmt(coef, r), r)
+    on, out = mmt(coef, zt), zt if w is None else mm(zt, w)
+    f = inverse_factors([mmt(mm(zt, gram), zt)])[0]
+    return mm(mmt(on, f), mm(f, out))
 
 
 def pair_gram_body(own_ref, other_ref, o_ref):
@@ -400,10 +432,11 @@
     own, other, cross, flipped = pair_gram(g_ref[...], gp_ref[...], n)
     gram = square(own, cross, flipped, other)
     basis = diagonal_blocks(*top_rows([own, other]))
-    w = mm(top_rows([mmt(mm(basis, gram), basis)], odd(0))[0], basis)
-    on = mmt(gram, w)
-    c_ref[...] = on[:n]
-    h = mm(w, on)
+    merged = mmt(mm(basis, gram), basis)
+    q = top_rows([merged], odd(0))[0]
+    h = mmt(mm(q, merged), q)
+    w = mm(q, basis)
+    c_ref[...] = mmt(gram[:n], w)
     wh_ref[...] = jnp.concatenate(
         [w, jnp.concatenate([h, jnp.zeros((RANK, LANES - RANK), jnp.float32)], axis=1)], axis=0
     )
@@ -426,7 +459,7 @@
 
 def quad_project_body(wh, c, far_wh, cs, twin, yo, yp, yy, yz, o_ref):
     w, gram, coef = quad_level(wh, c, far_wh, cs, twin)
-    weights = mm(projection(gram, coef, odd(1)), w).astype(jnp.bfloat16)
+    weights = projection(gram, coef, odd(1), w).astype(jnp.bfloat16)
     put_rows(weights, stack_of(yo, yp, yy, yz), o_ref)
 
 

time: 62.8 us -> 60.8 us (0.968)
  local copies, waits for them, and re-layouts: 1.86 us -> 0.01 us
  waiting for transfers between devices: 18.9 us -> 19.7 us
    unnamed x8 -> x4, local copies, waits for them, and re-layouts: 1.86 us -> 0.01 us
    pallas_call x1 -> x2, Pallas kernels: 0.5 us -> 2.3 us  [the longest x1 1.63 us: halo_exchange(): kernel_call(edge_body, (shape(edge), shape(edge)), [VMEM(d.shape, d.dtype...]
    pallas_call x1, Pallas kernels: 5.78 us -> 4.22 us  [smooth(): kernel_call(smooth_body, jax.ShapeDtypeStruct((rows, snaps, width), jnp.b...]
    ppermute x1, starting transfers between devices: 2.97 us -> 1.53 us  [halo_exchange(): side = lax.ppermute(packed, 'lon', forward)]
    ppermute x2, starting transfers between devices: 5.66 us -> 6.57 us  [swapped(): return lax.ppermute(message, 'lat', pairs + [(j, i) for i, j in pairs])]
    ppermute x1, waiting for transfers between devices: 2.11 us -> 2.82 us  [halo_exchange(): side = lax.ppermute(packed, 'lon', forward)]
where the time goes in v6:
time: 60.8 us; the launch traced here: 60.5 us
  Pallas kernels  20.6 us (34%)
  starting transfers between devices  20.1 us (33%)
  waiting for transfers between devices  19.7 us (32%)
    ppermute x6, waiting for transfers between devices, exchanged(): lax.ppermute(block, 'tm', [(i, i ^ 1 << level) for i in range(count)])  13.6 us
    all_to_all x2, starting transfers between devices, gathered(): return lax.all_to_all(parts, ('lat', 'lon'), 0, 0, tiled=True)  8.42 us
    ppermute x2, starting transfers between devices, swapped(): return lax.ppermute(message, 'lat', pairs + [(j, i) for i, j in pairs])  6.57 us
    pallas_call x1, Pallas kernels, shards(): kernel_call(pair_levels_body, (f32(2 * RANK, 2 * snaps), f32(snaps, RANK)...  6.02 us
    pallas_call x1, Pallas kernels, shards(): out = kernel_call(quad_project_body, b16(rows, snaps, width))(*operands)  4.78 us
    pallas_call x1, Pallas kernels, smooth(): kernel_call(smooth_body, jax.ShapeDtypeStruct((rows, snaps, width), jnp.b...  4.22 us
    ppermute x6, starting transfers between devices, exchanged(): lax.ppermute(block, 'tm', [(i, i ^ 1 << level) for i in range(count)])  3.57 us
    ppermute x1, waiting for transfers between devices, halo_exchange(): side = lax.ppermute(packed, 'lon', forward)  2.82 us
  transfers between devices with their start and end apart: 11, of which 7 were waited for; matrix products, arithmetic and copies ran while one was open for 0% of the time, Pallas kernels for 15%

profile of v6, /device:TPU:0, one launch (start us, length us, event | category | flops | bytes accessed | tf_op | source)
XLA Modules:
  0.0 60.5 jit_solution(10686848633827180757)
XLA Ops:
  0.0 0.0 copy-start
  0.0 1.6 %shard_map.28 = (bf16[272,128]{1,0:T(8,128)(2,1)}, bf16[272,128]{1,0:T(8,128)(2,1)}) custom-call(bf16[45,64,128]{2,1,0:T(8,128)(2,1)} %bitcast.2, f32[45,128]{1,0:T(8,128)} %d_ref.3), custom_call_target="tpu_custom_call" | custom-call | flops 1048576 | bytes 1048576 | tf_op jit(solution)/shard_map/pallas_call | solution.py:145
  1.6 0.7 %collective-permute-start = (bf16[272,128]{1,0:T(8,128)(2,1)}, bf16[272,128]{1,0:T(8,128)(2,1)S(1)}, u32[]{:S(2)}, u32[]{:S(2)}) collective-permute-start(bf16[272,128]{1,0:T(8,128)(2,1)} %get-tuple-element.9), channel_id=1, source_target_pairs={{2,4},{4,2},{3,5},{5,3},{10,12},{12,10},{11,13},{13,11},{18,20},{2... | collective-permute-start | bytes 208904 | tf_op jit(solution)/shard_map/ppermute | solution.py:156
  2.3 5.9 %collective-permute-start.1 = (bf16[272,128]{1,0:T(8,128)(2,1)}, bf16[272,128]{1,0:T(8,128)(2,1)S(1)}, u32[]{:S(2)}, u32[]{:S(2)}) collective-permute-start(bf16[272,128]{1,0:T(8,128)(2,1)} %get-tuple-element.10), channel_id=1, source_target_pairs={{0,2},{4,6},{2,0},{6,4},{1,3},{5,7},{3,1},{7,5},{8,10},{12,14},{10... | collective-permute-start | bytes 208904 | tf_op jit(solution)/shard_map/ppermute | solution.py:156
  8.2 0.0 collective-permute-done.b_ref
  8.2 2.5 %collective-permute-done.1.a_ref = bf16[272,128]{1,0:T(8,128)(2,1)S(1)} collective-permute-done((bf16[272,128]{1,0:T(8,128)(2,1)}, bf16[272,128]{1,0:T(8,128)(2,1)S(1)}, u32[]{:S(2)}, u32[]{:S(2)}) %collective-permute-start.1) | collective-permute-done | bytes 69664 | tf_op jit(solution)/shard_map/ppermute | solution.py:156
  10.7 0.0 copy-done
  10.7 0.0 copy-done.1
  10.7 0.7 %shard_map.29 = bf16[272,128]{1,0:T(8,128)(2,1)S(1)} custom-call(bf16[45,64,128]{2,1,0:T(8,128)(2,1)S(1)} %bitcast.3, f32[45,128]{1,0:T(8,128)S(1)} %copy-done.1, bf16[272,128]{1,0:T(8,128)(2,1)S(1)} %collective-permute-done.b_ref, bf16[272,128]{1,0:T(8,128)(2,1)S(1)} %collective-permute-done.1.a_ref), custom_call_target="tpu_custom_call" | custom-call | flops 1048576 | bytes 1048576 | tf_op jit(solution)/shard_map/pallas_call | solution.py:159
  11.4 1.5 %collective-permute-start.2 = (bf16[272,128]{1,0:T(8,128)(2,1)S(1)}, bf16[272,128]{1,0:T(8,128)(2,1)S(1)}, u32[]{:S(2)}, u32[]{:S(2)}) collective-permute-start(bf16[272,128]{1,0:T(8,128)(2,1)S(1)} %shard_map.29), channel_id=1, source_target_pairs={{0,1},{1,0},{2,3},{3,2},{4,5},{5,4},{6,7},{7,6},{8,9},{9,8},{10,11... | collective-permute-start | bytes 208904 | tf_op jit(solution)/shard_map/ppermute | solution.py:163
  12.9 2.8 %collective-permute-done.2.side_ref = bf16[272,128]{1,0:T(8,128)(2,1)S(1)} collective-permute-done((bf16[272,128]{1,0:T(8,128)(2,1)S(1)}, bf16[272,128]{1,0:T(8,128)(2,1)S(1)}, u32[]{:S(2)}, u32[]{:S(2)}) %collective-permute-start.2) | collective-permute-done | bytes 69664 | tf_op jit(solution)/shard_map/ppermute | solution.py:163
  15.7 4.2 %shard_map.30.own_ref.yo = bf16[45,64,128]{2,1,0:T(8,128)(2,1)S(1)} custom-call(bf16[45,64,128]{2,1,0:T(8,128)(2,1)S(1)} %bitcast.4, f32[45,128]{1,0:T(8,128)S(1)} %copy-done.1, bf16[272,128]{1,0:T(8,128)(2,1)S(1)} %collective-permute-done.2.side_ref, bf16[272,128]{1,0:T(8,128)(2,1)S(1)} %collective-permute-done.1.a_ref, ...), custom_call_target="tpu_custom_call" | custom-call | flops 1048576 | bytes 1048576 | tf_op jit(solution)/shard_map/pallas_call | solution.py:274
  20.0 0.1 collective-permute-start.3
  20.0 1.6 %collective-permute-start.6 = (bf16[45,64,128]{2,1,0:T(8,128)(2,1)S(1)}, bf16[45,64,128]{2,1,0:T(8,128)(2,1)S(1)}, u32[]{:S(2)}, u32[]{:S(2)}) collective-permute-start(bf16[45,64,128]{2,1,0:T(8,128)(2,1)S(1)} %shard_map.30.own_ref.yo), channel_id=1, source_target_pairs={{0,16},{8,24},{16,0},{24,8},{1,17},{9,25},{17,1},{25,9},{2,18},{10... | collective-permute-start | bytes 2211848 | tf_op jit(solution)/shard_map/ppermute | solution.py:521
  21.6 0.6 %collective-permute-done.3.other_ref.yp = bf16[45,64,128]{2,1,0:T(8,128)(2,1)S(1)} collective-permute-done((bf16[45,64,128]{2,1,0:T(8,128)(2,1)S(1)}, bf16[45,64,128]{2,1,0:T(8,128)(2,1)S(1)}, u32[]{:S(2)}, u32[]{:S(2)}) %collective-permute-start.3) | collective-permute-done | bytes 737312 | tf_op jit(solution)/shard_map/ppermute | solution.py:521
  22.2 2.0 %shard_map.31 = f32[8,48,128]{2,1,0:T(8,128)} custom-call(bf16[45,64,128]{2,1,0:T(8,128)(2,1)S(1)} %shard_map.30.own_ref.yo, bf16[45,64,128]{2,1,0:T(8,128)(2,1)S(1)} %collective-permute-done.3.other_ref.yp), custom_call_target="tpu_custom_call" | custom-call | flops 1048576 | bytes 1048576 | tf_op jit(solution)/shard_map/pallas_call | solution.py:537
  24.3 4.2 %all-to-all-start = ((f32[8,48,128]{2,1,0:T(8,128)}), f32[8,48,128]{2,1,0:T(8,128)S(1)}, u32[]{:S(2)}, u32[]{:S(2)}) async-start(f32[8,48,128]{2,1,0:T(8,128)} %shard_map.31), calls=%async_computation | async-start | bytes 393216 | tf_op jit(solution)/shard_map/all_to_all | solution.py:525
  28.5 10.5 %collective-permute-done.6.far_ref.yy = bf16[45,64,128]{2,1,0:T(8,128)(2,1)S(1)} collective-permute-done((bf16[45,64,128]{2,1,0:T(8,128)(2,1)S(1)}, bf16[45,64,128]{2,1,0:T(8,128)(2,1)S(1)}, u32[]{:S(2)}, u32[]{:S(2)}) %collective-permute-start.6) | collective-permute-done | bytes 737312 | tf_op jit(solution)/shard_map/ppermute | solution.py:521
  38.9 0.0 collective-permute-start.8
  39.0 1.3 %shard_map.33 = f32[8,64,128]{2,1,0:T(8,128)} custom-call(bf16[45,64,128]{2,1,0:T(8,128)(2,1)S(1)} %shard_map.30.own_ref.yo, bf16[45,64,128]{2,1,0:T(8,128)(2,1)S(1)} %collective-permute-done.3.other_ref.yp, bf16[45,64,128]{2,1,0:T(8,128)(2,1)S(1)} %collective-permute-done.6.far_ref.yy), custom_call_target="tpu_custom_call" | custom-call | flops 1048576 | bytes 1048576 | tf_op jit(solution)/shard_map/pallas_call | solution.py:539
  40.3 0.0 all-to-all-done
  40.3 4.2 %all-to-all-start.1 = ((f32[8,64,128]{2,1,0:T(8,128)}), f32[8,64,128]{2,1,0:T(8,128)S(1)}, u32[]{:S(2)}, u32[]{:S(2)}) async-start(f32[8,64,128]{2,1,0:T(8,128)} %shard_map.33), calls=%async_computation.1 | async-start | bytes 524288 | tf_op jit(solution)/shard_map/all_to_all | solution.py:525
  44.5 0.3 collective-permute-start.4
  44.8 1.0 %collective-permute-done.4.gp_ref = f32[48,128]{1,0:T(8,128)S(1)} collective-permute-done((f32[48,128]{1,0:T(8,128)S(1)}, f32[48,128]{1,0:T(8,128)S(1)}, u32[]{:S(2)}, u32[]{:S(2)}) %collective-permute-start.4) | collective-permute-done | bytes 24608 | tf_op jit(solution)/shard_map/ppermute | solution.py:521
  45.8 6.0 %shard_map.32 = (f32[64,128]{1,0:T(8,128)S(1)}, f32[64,32]{1,0:T(8,128)S(1)}) custom-call(f32[48,128]{1,0:T(8,128)S(1)} %reduce_sum.18.g_ref, f32[48,128]{1,0:T(8,128)S(1)} %collective-permute-done.4.gp_ref), custom_call_target="tpu_custom_call" | custom-call | flops 4294967296 | bytes 1048576 | tf_op jit(solution)/shard_map/pallas_call | solution.py:541
  51.8 1.6 %collective-permute-start.5 = (f32[64,128]{1,0:T(8,128)S(1)}, f32[64,128]{1,0:T(8,128)S(1)}, u32[]{:S(2)}, u32[]{:S(2)}) collective-permute-start(f32[64,128]{1,0:T(8,128)S(1)} %get-tuple-element.11.wh), channel_id=1, source_target_pairs={{0,16},{8,24},{16,0},{24,8},{1,17},{9,25},{17,1},{25,9},{2,18},{10... | collective-permute-start | bytes 98312 | tf_op jit(solution)/shard_map/ppermute | solution.py:521
  53.3 0.7 %all-to-all-done.1 = f32[8,64,128]{2,1,0:T(8,128)S(1)} async-done(((f32[8,64,128]{2,1,0:T(8,128)}), f32[8,64,128]{2,1,0:T(8,128)S(1)}, u32[]{:S(2)}, u32[]{:S(2)}) %all-to-all-start.1) | async-done | bytes 262176 | tf_op jit(solution)/shard_map/all_to_all | solution.py:525
  54.1 0.1 collective-permute-start.7
  54.2 1.5 %collective-permute-done.5.far_wh = f32[64,128]{1,0:T(8,128)S(1)} collective-permute-done((f32[64,128]{1,0:T(8,128)S(1)}, f32[64,128]{1,0:T(8,128)S(1)}, u32[]{:S(2)}, u32[]{:S(2)}) %collective-permute-start.5) | collective-permute-done | bytes 32800 | tf_op jit(solution)/shard_map/ppermute | solution.py:521
  55.7 0.0 collective-permute-done.7.twin
  55.7 0.0 collective-permute-done.8.yz
  55.7 4.8 %shard_map.34 = bf16[45,64,128]{2,1,0:T(8,128)(2,1)} custom-call(f32[64,128]{1,0:T(8,128)S(1)} %get-tuple-element.11.wh, f32[64,32]{1,0:T(8,128)S(1)} %get-tuple-element.12.c, f32[64,128]{1,0:T(8,128)S(1)} %collective-permute-done.5.far_wh, f32[64,128]{1,0:T(8,128)S(1)} %reduce_sum.19.cs, f32[64,128]{1,0:T(8,128)S(1)} %collective-permute-done.7.twin, ...), custom_call_target="tpu_custom_call" | custom-call | flops 1048576 | bytes 1048576 | tf_op jit(solution)/shard_map/pallas_call | solution.py:547
  (3 shorter events, 0.0 us)
Async XLA Ops:
  0.0 10.7 %copy-start = (bf16[64,45,128]{2,0,1:T(8,128)(2,1)S(1)}, bf16[64,45,128]{2,0,1:T(8,128)(2,1)}, u32[]{:S(2)}) copy-start(bf16[64,45,128]{2,0,1:T(8,128)(2,1)} %param.2) | copy-start | bytes 2211844
  0.0 10.7 %copy-start.1 = (f32[45,128]{1,0:T(8,128)S(1)}, f32[45,128]{1,0:T(8,128)}, u32[]{:S(2)}) copy-start(f32[45,128]{1,0:T(8,128)} %d_ref.3) | copy-start | bytes 69124
  1.6 6.6 %collective-permute-start = (bf16[272,128]{1,0:T(8,128)(2,1)}, bf16[272,128]{1,0:T(8,128)(2,1)S(1)}, u32[]{:S(2)}, u32[]{:S(2)}) collective-permute-start(bf16[272,128]{1,0:T(8,128)(2,1)} %get-tuple-element.9), channel_id=1, source_target_pairs={{2,4},{4,2},{3,5},{5,3},{10,12},{12,10},{11,13},{13,11},{18,20},{2... | collective-permute-start | bytes 208904 | tf_op jit(solution)/shard_map/ppermute | solution.py:156
  2.3 8.4 %collective-permute-start.1 = (bf16[272,128]{1,0:T(8,128)(2,1)}, bf16[272,128]{1,0:T(8,128)(2,1)S(1)}, u32[]{:S(2)}, u32[]{:S(2)}) collective-permute-start(bf16[272,128]{1,0:T(8,128)(2,1)} %get-tuple-element.10), channel_id=1, source_target_pairs={{0,2},{4,6},{2,0},{6,4},{1,3},{5,7},{3,1},{7,5},{8,10},{12,14},{10... | collective-permute-start | bytes 208904 | tf_op jit(solution)/shard_map/ppermute | solution.py:156
  11.4 4.3 %collective-permute-start.2 = (bf16[272,128]{1,0:T(8,128)(2,1)S(1)}, bf16[272,128]{1,0:T(8,128)(2,1)S(1)}, u32[]{:S(2)}, u32[]{:S(2)}) collective-permute-start(bf16[272,128]{1,0:T(8,128)(2,1)S(1)} %shard_map.29), channel_id=1, source_target_pairs={{0,1},{1,0},{2,3},{3,2},{4,5},{5,4},{6,7},{7,6},{8,9},{9,8},{10,11... | collective-permute-start | bytes 208904 | tf_op jit(solution)/shard_map/ppermute | solution.py:163
  20.0 2.3 %collective-permute-start.3 = (bf16[45,64,128]{2,1,0:T(8,128)(2,1)S(1)}, bf16[45,64,128]{2,1,0:T(8,128)(2,1)S(1)}, u32[]{:S(2)}, u32[]{:S(2)}) collective-permute-start(bf16[45,64,128]{2,1,0:T(8,128)(2,1)S(1)} %shard_map.30.own_ref.yo), channel_id=1, source_target_pairs={{0,8},{8,0},{16,24},{24,16},{1,9},{9,1},{17,25},{25,17},{2,10},{10... | collective-permute-start | bytes 2211848 | tf_op jit(solution)/shard_map/ppermute | solution.py:521
  20.0 18.9 %collective-permute-start.6 = (bf16[45,64,128]{2,1,0:T(8,128)(2,1)S(1)}, bf16[45,64,128]{2,1,0:T(8,128)(2,1)S(1)}, u32[]{:S(2)}, u32[]{:S(2)}) collective-permute-start(bf16[45,64,128]{2,1,0:T(8,128)(2,1)S(1)} %shard_map.30.own_ref.yo), channel_id=1, source_target_pairs={{0,16},{8,24},{16,0},{24,8},{1,17},{9,25},{17,1},{25,9},{2,18},{10... | collective-permute-start | bytes 2211848 | tf_op jit(solution)/shard_map/ppermute | solution.py:521
  24.3 16.0 %all-to-all-start = ((f32[8,48,128]{2,1,0:T(8,128)}), f32[8,48,128]{2,1,0:T(8,128)S(1)}, u32[]{:S(2)}, u32[]{:S(2)}) async-start(f32[8,48,128]{2,1,0:T(8,128)} %shard_map.31), calls=%async_computation | async-start | bytes 393216 | tf_op jit(solution)/shard_map/all_to_all | solution.py:525
  38.9 16.8 %collective-permute-start.8 = (bf16[45,64,128]{2,1,0:T(8,128)(2,1)S(1)}, bf16[45,64,128]{2,1,0:T(8,128)(2,1)S(1)}, u32[]{:S(2)}, u32[]{:S(2)}) collective-permute-start(bf16[45,64,128]{2,1,0:T(8,128)(2,1)S(1)} %collective-permute-done.6.far_ref.yy), channel_id=1, source_target_pairs={{0,8},{8,0},{16,24},{24,16},{1,9},{9,1},{17,25},{25,17},{2,10},{10... | collective-permute-start | bytes 2211848 | tf_op jit(solution)/shard_map/ppermute | solution.py:521
  40.3 13.8 %all-to-all-start.1 = ((f32[8,64,128]{2,1,0:T(8,128)}), f32[8,64,128]{2,1,0:T(8,128)S(1)}, u32[]{:S(2)}, u32[]{:S(2)}) async-start(f32[8,64,128]{2,1,0:T(8,128)} %shard_map.33), calls=%async_computation.1 | async-start | bytes 524288 | tf_op jit(solution)/shard_map/all_to_all | solution.py:525
  44.5 1.3 %collective-permute-start.4 = (f32[48,128]{1,0:T(8,128)S(1)}, f32[48,128]{1,0:T(8,128)S(1)}, u32[]{:S(2)}, u32[]{:S(2)}) collective-permute-start(f32[48,128]{1,0:T(8,128)S(1)} %reduce_sum.18.g_ref), channel_id=1, source_target_pairs={{0,8},{8,0},{16,24},{24,16},{1,9},{9,1},{17,25},{25,17},{2,10},{10... | collective-permute-start | bytes 73736 | tf_op jit(solution)/shard_map/ppermute | solution.py:521
  51.8 3.9 %collective-permute-start.5 = (f32[64,128]{1,0:T(8,128)S(1)}, f32[64,128]{1,0:T(8,128)S(1)}, u32[]{:S(2)}, u32[]{:S(2)}) collective-permute-start(f32[64,128]{1,0:T(8,128)S(1)} %get-tuple-element.11.wh), channel_id=1, source_target_pairs={{0,16},{8,24},{16,0},{24,8},{1,17},{9,25},{17,1},{25,9},{2,18},{10... | collective-permute-start | bytes 98312 | tf_op jit(solution)/shard_map/ppermute | solution.py:521
  54.1 1.6 %collective-permute-start.7 = (f32[64,128]{1,0:T(8,128)S(1)}, f32[64,128]{1,0:T(8,128)S(1)}, u32[]{:S(2)}, u32[]{:S(2)}) collective-permute-start(f32[64,128]{1,0:T(8,128)S(1)} %reduce_sum.19.cs), channel_id=1, source_target_pairs={{0,8},{8,0},{16,24},{24,16},{1,9},{9,1},{17,25},{25,17},{2,10},{10... | collective-permute-start | bytes 98312 | tf_op jit(solution)/shard_map/ppermute | solution.py:521

commit v7 on v6

--- a/solution.py
+++ b/solution.py
@@ -19,12 +19,12 @@
     return pl.BlockSpec(memory_space=VMEM)
 
 
-def kernel_call(body, outs, scratch=(), flops=1 << 20, specs=None, vmem=48 << 20):
+def kernel_call(body, outs, scratch=(), flops=1 << 20, specs=None, vmem=48 << 20, out_spec=None):
     return pl.pallas_call(
         body,
         out_shape=outs,
         **({} if specs is None else {"in_specs": specs}),
-        out_specs=jax.tree.map(lambda _: whole(), outs),
+        out_specs=jax.tree.map(lambda _: out_spec or whole(), outs),
         scratch_shapes=list(scratch),
         compiler_params=pltpu.CompilerParams(vmem_limit_bytes=vmem),
         cost_estimate=pl.CostEstimate(flops=flops, bytes_accessed=1 << 20, transcendentals=0),
@@ -357,13 +357,26 @@
     return mm(mmt(on, f), mm(f, out))
 
 
+def stack_of(*refs):
+    return lambda i: jnp.concatenate([ref[i] for ref in refs], axis=0)
+
+
+def gram_sum(left, right, rows):
+    acc = None
+    for i in range(0, rows, 2):
+        at = range(i, min(i + 2, rows))
+        part = dot_t(
+            jnp.concatenate([left(r) for r in at], axis=1),
+            jnp.concatenate([right(r) for r in at], axis=1),
+        )
+        acc = part if acc is None else acc + part
+    return acc
+
+
 def pair_gram_body(own_ref, other_ref, o_ref):
     n = own_ref.shape[1]
-    acc = None
-    for i in range(own_ref.shape[0]):
-        both = jnp.concatenate([own_ref[i], other_ref[i]], axis=0)
-        part = dot_t(both, both)
-        acc = part if acc is None else acc + part
+    both = stack_of(own_ref, other_ref)
+    acc = gram_sum(both, both, own_ref.shape[0])
     cross = jnp.where(odd(0), pltpu.roll(acc[n + n // 2 :], n, 1), acc[: n // 2])[:, n:]
     tall = o_ref.shape[1]
     packed = jnp.concatenate(
@@ -389,6 +402,32 @@
         o_ref[i] = jnp.dot(w, stacked(i), preferred_element_type=jnp.float32).astype(jnp.bfloat16)
 
 
+def put_result(w, stacked, o_hbm, buffer, sems):
+    rows = buffer.shape[0]
+    parts = sems.shape[0]
+    size = -(-rows // parts)
+    copies = []
+    for p in range(parts):
+        lo, hi = p * size, min(rows, p * size + size)
+        for i in range(lo, hi):
+            buffer[i] = jnp.dot(w, stacked(i), preferred_element_type=jnp.float32).astype(jnp.bfloat16)
+        at = pl.ds(lo, hi - lo)
+        copies.append(pltpu.make_async_copy(buffer.at[at], o_hbm.at[at], sems.at[p]))
+        copies[-1].start()
+    for copy in copies:
+        copy.wait()
+
+
+def result_call(body, rows, snaps, width):
+    parts = 5
+    return kernel_call(
+        body,
+        jax.ShapeDtypeStruct((rows, snaps, width), jnp.bfloat16),
+        [VMEM((rows, snaps, width), jnp.bfloat16), pltpu.SemaphoreType.DMA((parts,))],
+        out_spec=pl.BlockSpec(memory_space=pl.ANY),
+    )
+
+
 def put_modes(w, stacked, modes_ref, part_ref):
     rows, half = modes_ref.shape[0], part_ref.shape[0]
     put_rows(w, stacked, modes_ref)
@@ -412,10 +451,7 @@
 
 def far_gram_body(own_ref, other_ref, far_ref, o_ref):
     n = own_ref.shape[1]
-    acc = None
-    for i in range(own_ref.shape[0]):
-        part = dot_t(jnp.concatenate([own_ref[i], other_ref[i]], axis=0), far_ref[i])
-        acc = part if acc is None else acc + part
+    acc = gram_sum(stack_of(own_ref, other_ref), lambda i: far_ref[i], own_ref.shape[0])
     packed = jnp.concatenate([acc[:n], acc[n:]], axis=1)
     for j in range(o_ref.shape[0]):
         o_ref[j] = packed
@@ -453,14 +489,10 @@
     return diagonal_blocks(wa, wb), gram, jnp.concatenate([c_ref[...], on_b[:n]], axis=1)
 
 
-def stack_of(*refs):
-    return lambda i: jnp.concatenate([ref[i] for ref in refs], axis=0)
-
-
-def quad_project_body(wh, c, far_wh, cs, twin, yo, yp, yy, yz, o_ref):
+def quad_project_body(wh, c, far_wh, cs, twin, yo, yp, yy, yz, o_hbm, buffer, sems):
     w, gram, coef = quad_level(wh, c, far_wh, cs, twin)
     weights = projection(gram, coef, odd(1), w).astype(jnp.bfloat16)
-    put_rows(weights, stack_of(yo, yp, yy, yz), o_ref)
+    put_result(weights, stack_of(yo, yp, yy, yz), o_hbm, buffer, sems)
 
 
 def quad_modes_body(wh, c, far_wh, cs, twin, yo, yp, yy, yz, modes_ref, part_ref, h_ref, c_ref):
@@ -472,13 +504,9 @@
 
 
 def cross_body(here_ref, there_ref, y_ref, own_ref, o_ref):
-    acc = None
     rows = y_ref.shape[0]
     other = halves(rows, here_ref, there_ref)
-    for i in range(rows):
-        theirs = other(i)
-        part = dot_t(theirs, jnp.concatenate([y_ref[i], own_ref[i], theirs], axis=0))
-        acc = part if acc is None else acc + part
+    acc = gram_sum(other, lambda i: jnp.concatenate([y_ref[i], own_ref[i], other(i)], axis=0), rows)
     for j in range(o_ref.shape[0]):
         o_ref[j] = acc
 
@@ -509,11 +537,12 @@
     put_modes(w, lambda i: jnp.concatenate([own_ref[i], other(i)], axis=0), modes_ref, part_ref)
 
 
-def project_body(level, p_ref, h_ref, c_ref, own_ref, here_ref, there_ref, o_ref):
+def project_body(level, p_ref, h_ref, c_ref, own_ref, here_ref, there_ref, o_hbm, buffer, sems):
     gram, coef = merged_gram(p_ref, h_ref, c_ref, c_ref.shape[0])
     weights = projection(gram, coef, odd(level)).astype(jnp.bfloat16)
     other = halves(own_ref.shape[0], here_ref, there_ref)
-    put_rows(weights, lambda i: jnp.concatenate([own_ref[i], other(i)], axis=0), o_ref)
+    stacked = lambda i: jnp.concatenate([own_ref[i], other(i)], axis=0)
+    put_result(weights, stacked, o_hbm, buffer, sems)
 
 
 def exchanged(block, level):
@@ -536,15 +565,17 @@
     other, far = exchanged(y, 0), exchanged(y, 1)
     pair = kernel_call(pair_gram_body, f32(tiles, snaps * 3 // 4, 2 * snaps))(y, other)
     pair = jnp.sum(gathered(pair), axis=0)
+    pair_twin = exchanged(pair, 0)
+    far, pair_twin = lax.optimization_barrier((far, pair_twin))
     cross = kernel_call(far_gram_body, f32(tiles, snaps, 2 * snaps))(y, other, far)
     cross = jnp.sum(gathered(cross), axis=0)
     wh, c = kernel_call(
         pair_levels_body, (f32(2 * RANK, 2 * snaps), f32(snaps, RANK)), flops=1 << 32
-    )(pair, exchanged(pair, 0))
+    )(pair, pair_twin)
     operands = (wh, c, exchanged(wh, 1), cross, exchanged(cross, 0))
     operands += (y, other, far, exchanged(far, 0))
     if levels == 2:
-        out = kernel_call(quad_project_body, b16(rows, snaps, width))(*operands)
+        out = result_call(quad_project_body, rows, snaps, width)(*operands)
         return jnp.transpose(out, (1, 0, 2))
     block = (
         b16(rows, RANK, width),
@@ -561,7 +592,7 @@
             modes, part, h, c = kernel_call(functools.partial(merge_body, level), block)(
                 parts, h, c, modes, here, there
             )
-    out = kernel_call(functools.partial(project_body, levels - 1), b16(rows, snaps, width))(
+    out = result_call(functools.partial(project_body, levels - 1), rows, snaps, width)(
         parts, h, c, modes, here, there
     )
     return jnp.transpose(out, (1, 0, 2))

time: 60.8 us -> 60.3 us (level)
  blocking collectives: 0 us -> 12.3 us
  waiting for transfers between devices: 19.7 us -> 12.8 us
  starting transfers between devices: 20.1 us -> 15.7 us
  Pallas kernels: 20.6 us -> 19.2 us
    all_to_all x0 -> x1, blocking collectives: none -> 12.3 us  [gathered(): return lax.all_to_all(parts, ('lat', 'lon'), 0, 0, tiled=True)]
    ppermute x6, waiting for transfers between devices: 13.6 us -> 5.4 us  [exchanged(): lax.ppermute(block, 'tm', [(i, i ^ 1 << level) for i in range(count)])]
    all_to_all x2 -> x1, starting transfers between devices: 8.42 us -> 4.22 us  [gathered(): return lax.all_to_all(parts, ('lat', 'lon'), 0, 0, tiled=True)]
    all_to_all x2 -> x1, waiting for transfers between devices: 0.74 us -> 2.03 us  [gathered(): return lax.all_to_all(parts, ('lat', 'lon'), 0, 0, tiled=True)]
    pallas_call x1, Pallas kernels: 2.01 us -> 0.75 us  [shards(): kernel_call(pair_gram_body, f32(tiles, snaps * 3 // 4, 2 * snaps))(y, other)]
  transfers between devices with their start and end apart: 11 -> 10, of which waited for: 7 -> 7; matrix products, arithmetic and copies ran while one was open for 0% -> 0% of each run, Pallas kernels for 15% -> 13%
where the time goes in v7:
time: 60.3 us; the launch traced here: 60 us
  Pallas kernels  19.2 us (32%)
  starting transfers between devices  15.7 us (26%)
  waiting for transfers between devices  12.8 us (21%)
  blocking collectives  12.3 us (20%)
    all_to_all x1, blocking collectives, gathered(): return lax.all_to_all(parts, ('lat', 'lon'), 0, 0, tiled=True)  12.3 us
    ppermute x2, starting transfers between devices, swapped(): return lax.ppermute(message, 'lat', pairs + [(j, i) for i, j in pairs])  6.57 us
    pallas_call x1, Pallas kernels, shards(): kernel_call(pair_levels_body, (f32(2 * RANK, 2 * snaps), f32(snaps, RANK)...  6.02 us
    ppermute x6, waiting for transfers between devices, exchanged(): lax.ppermute(block, 'tm', [(i, i ^ 1 << level) for i in range(count)])  5.4 us
    pallas_call x1, Pallas kernels, shards(): out = result_call(quad_project_body, rows, snaps, width)(*operands)  4.62 us
    pallas_call x1, Pallas kernels, smooth(): kernel_call(smooth_body, jax.ShapeDtypeStruct((rows, snaps, width), jnp.b...  4.22 us
    all_to_all x1, starting transfers between devices, gathered(): return lax.all_to_all(parts, ('lat', 'lon'), 0, 0, tiled=True)  4.22 us
    ppermute x6, starting transfers between devices, exchanged(): lax.ppermute(block, 'tm', [(i, i ^ 1 << level) for i in range(count)])  3.33 us
  transfers between devices with their start and end apart: 10, of which 7 were waited for; matrix products, arithmetic and copies ran while one was open for 0% of the time, Pallas kernels for 13%

profile of v7, /device:TPU:0, one launch (start us, length us, event | category | flops | bytes accessed | tf_op | source)
XLA Modules:
  0.0 60.0 jit_solution(17862695532400117693)
XLA Ops:
  0.0 0.0 copy-start
  0.0 0.0 copy-start.1
  0.0 1.6 %shard_map.28 = (bf16[272,128]{1,0:T(8,128)(2,1)}, bf16[272,128]{1,0:T(8,128)(2,1)}) custom-call(bf16[45,64,128]{2,1,0:T(8,128)(2,1)} %bitcast.2, f32[45,128]{1,0:T(8,128)} %d_ref.3), custom_call_target="tpu_custom_call" | custom-call | flops 1048576 | bytes 1048576 | tf_op jit(solution)/shard_map/pallas_call | solution.py:145
  1.6 0.7 %collective-permute-start = (bf16[272,128]{1,0:T(8,128)(2,1)}, bf16[272,128]{1,0:T(8,128)(2,1)S(1)}, u32[]{:S(2)}, u32[]{:S(2)}) collective-permute-start(bf16[272,128]{1,0:T(8,128)(2,1)} %get-tuple-element.11), channel_id=1, source_target_pairs={{2,4},{4,2},{3,5},{5,3},{10,12},{12,10},{11,13},{13,11},{18,20},{2... | collective-permute-start | bytes 208904 | tf_op jit(solution)/shard_map/ppermute | solution.py:156
  2.3 5.9 %collective-permute-start.1 = (bf16[272,128]{1,0:T(8,128)(2,1)}, bf16[272,128]{1,0:T(8,128)(2,1)S(1)}, u32[]{:S(2)}, u32[]{:S(2)}) collective-permute-start(bf16[272,128]{1,0:T(8,128)(2,1)} %get-tuple-element.12), channel_id=1, source_target_pairs={{0,2},{4,6},{2,0},{6,4},{1,3},{5,7},{3,1},{7,5},{8,10},{12,14},{10... | collective-permute-start | bytes 208904 | tf_op jit(solution)/shard_map/ppermute | solution.py:156
  8.2 0.0 collective-permute-done.b_ref
  8.2 2.5 %collective-permute-done.1.a_ref = bf16[272,128]{1,0:T(8,128)(2,1)S(1)} collective-permute-done((bf16[272,128]{1,0:T(8,128)(2,1)}, bf16[272,128]{1,0:T(8,128)(2,1)S(1)}, u32[]{:S(2)}, u32[]{:S(2)}) %collective-permute-start.1) | collective-permute-done | bytes 69664 | tf_op jit(solution)/shard_map/ppermute | solution.py:156
  10.7 0.0 copy-done
  10.7 0.0 copy-done.1
  10.7 0.7 %shard_map.29 = bf16[272,128]{1,0:T(8,128)(2,1)S(1)} custom-call(bf16[45,64,128]{2,1,0:T(8,128)(2,1)S(1)} %bitcast.3, f32[45,128]{1,0:T(8,128)S(1)} %copy-done.1, bf16[272,128]{1,0:T(8,128)(2,1)S(1)} %collective-permute-done.b_ref, bf16[272,128]{1,0:T(8,128)(2,1)S(1)} %collective-permute-done.1.a_ref), custom_call_target="tpu_custom_call" | custom-call | flops 1048576 | bytes 1048576 | tf_op jit(solution)/shard_map/pallas_call | solution.py:159
  11.4 1.5 %collective-permute-start.2 = (bf16[272,128]{1,0:T(8,128)(2,1)S(1)}, bf16[272,128]{1,0:T(8,128)(2,1)S(1)}, u32[]{:S(2)}, u32[]{:S(2)}) collective-permute-start(bf16[272,128]{1,0:T(8,128)(2,1)S(1)} %shard_map.29), channel_id=1, source_target_pairs={{0,1},{1,0},{2,3},{3,2},{4,5},{5,4},{6,7},{7,6},{8,9},{9,8},{10,11... | collective-permute-start | bytes 208904 | tf_op jit(solution)/shard_map/ppermute | solution.py:163
  12.9 2.8 %collective-permute-done.2.side_ref = bf16[272,128]{1,0:T(8,128)(2,1)S(1)} collective-permute-done((bf16[272,128]{1,0:T(8,128)(2,1)S(1)}, bf16[272,128]{1,0:T(8,128)(2,1)S(1)}, u32[]{:S(2)}, u32[]{:S(2)}) %collective-permute-start.2) | collective-permute-done | bytes 69664 | tf_op jit(solution)/shard_map/ppermute | solution.py:163
  15.7 4.2 %shard_map.30.own_ref.yo = bf16[45,64,128]{2,1,0:T(8,128)(2,1)S(1)} custom-call(bf16[45,64,128]{2,1,0:T(8,128)(2,1)S(1)} %bitcast.4, f32[45,128]{1,0:T(8,128)S(1)} %copy-done.1, bf16[272,128]{1,0:T(8,128)(2,1)S(1)} %collective-permute-done.2.side_ref, bf16[272,128]{1,0:T(8,128)(2,1)S(1)} %collective-permute-done.1.a_ref, ...), custom_call_target="tpu_custom_call" | custom-call | flops 1048576 | bytes 1048576 | tf_op jit(solution)/shard_map/pallas_call | solution.py:274
  20.0 0.1 collective-permute-start.3
  20.0 1.6 %collective-permute-start.4 = (bf16[45,64,128]{2,1,0:T(8,128)(2,1)S(1)}, bf16[45,64,128]{2,1,0:T(8,128)(2,1)S(1)}, u32[]{:S(2)}, u32[]{:S(2)}) collective-permute-start(bf16[45,64,128]{2,1,0:T(8,128)(2,1)S(1)} %shard_map.30.own_ref.yo), channel_id=1, source_target_pairs={{0,16},{8,24},{16,0},{24,8},{1,17},{9,25},{17,1},{25,9},{2,18},{10... | collective-permute-start | bytes 2211848 | tf_op jit(solution)/shard_map/ppermute | solution.py:550
  21.6 0.6 %collective-permute-done.3.other_ref.yp = bf16[45,64,128]{2,1,0:T(8,128)(2,1)S(1)} collective-permute-done((bf16[45,64,128]{2,1,0:T(8,128)(2,1)S(1)}, bf16[45,64,128]{2,1,0:T(8,128)(2,1)S(1)}, u32[]{:S(2)}, u32[]{:S(2)}) %collective-permute-start.3) | collective-permute-done | bytes 737312 | tf_op jit(solution)/shard_map/ppermute | solution.py:550
  22.2 0.7 %shard_map.31 = f32[8,48,128]{2,1,0:T(8,128)S(1)} custom-call(bf16[45,64,128]{2,1,0:T(8,128)(2,1)S(1)} %shard_map.30.own_ref.yo, bf16[45,64,128]{2,1,0:T(8,128)(2,1)S(1)} %collective-permute-done.3.other_ref.yp), custom_call_target="tpu_custom_call" | custom-call | flops 1048576 | bytes 1048576 | tf_op jit(solution)/shard_map/pallas_call | solution.py:566
  23.0 12.3 %all_to_all.10 = f32[8,48,128]{2,1,0:T(8,128)S(1)} all-to-all(f32[8,48,128]{2,1,0:T(8,128)S(1)} %shard_map.31), channel_id=1, replica_groups=mesh['tm'=4,'lat'=4,'lon'=2] {'lat','lon'}, dimensions={0} | all-to-all | bytes 393216 | tf_op jit(solution)/shard_map/all_to_all | solution.py:554
  35.3 0.1 collective-permute-start.5
  35.4 3.6 %collective-permute-done.4.far_ref.yy = bf16[45,64,128]{2,1,0:T(8,128)(2,1)S(1)} collective-permute-done((bf16[45,64,128]{2,1,0:T(8,128)(2,1)S(1)}, bf16[45,64,128]{2,1,0:T(8,128)(2,1)S(1)}, u32[]{:S(2)}, u32[]{:S(2)}) %collective-permute-start.4) | collective-permute-done | bytes 737312 | tf_op jit(solution)/shard_map/ppermute | solution.py:550
  38.9 0.0 collective-permute-done.5.gp_ref
  38.9 0.0 collective-permute-start.8
  38.9 1.3 %shard_map.33 = f32[8,64,128]{2,1,0:T(8,128)} custom-call(bf16[45,64,128]{2,1,0:T(8,128)(2,1)S(1)} %shard_map.30.own_ref.yo, bf16[45,64,128]{2,1,0:T(8,128)(2,1)S(1)} %collective-permute-done.3.other_ref.yp, bf16[45,64,128]{2,1,0:T(8,128)(2,1)S(1)} %collective-permute-done.4.far_ref.yy), custom_call_target="tpu_custom_call" | custom-call | flops 1048576 | bytes 1048576 | tf_op jit(solution)/shard_map/pallas_call | solution.py:570
  40.3 4.2 %all-to-all-start.1 = ((f32[8,64,128]{2,1,0:T(8,128)}), f32[8,64,128]{2,1,0:T(8,128)S(1)}, u32[]{:S(2)}, u32[]{:S(2)}) async-start(f32[8,64,128]{2,1,0:T(8,128)} %shard_map.33), calls=%async_computation.1 | async-start | bytes 524288 | tf_op jit(solution)/shard_map/all_to_all | solution.py:554
  44.5 6.0 %shard_map.32 = (f32[64,128]{1,0:T(8,128)S(1)}, f32[64,32]{1,0:T(8,128)S(1)}) custom-call(f32[48,128]{1,0:T(8,128)S(1)} %reduce_sum.18.g_ref, f32[48,128]{1,0:T(8,128)S(1)} %collective-permute-done.5.gp_ref), custom_call_target="tpu_custom_call" | custom-call | flops 4294967296 | bytes 1048576 | tf_op jit(solution)/shard_map/pallas_call | solution.py:572
  50.5 1.5 %collective-permute-start.6 = (f32[64,128]{1,0:T(8,128)S(1)}, f32[64,128]{1,0:T(8,128)S(1)}, u32[]{:S(2)}, u32[]{:S(2)}) collective-permute-start(f32[64,128]{1,0:T(8,128)S(1)} %get-tuple-element.14.wh), channel_id=1, source_target_pairs={{0,16},{8,24},{16,0},{24,8},{1,17},{9,25},{17,1},{25,9},{2,18},{10... | collective-permute-start | bytes 98312 | tf_op jit(solution)/shard_map/ppermute | solution.py:550
  52.0 2.0 %all-to-all-done.1 = f32[8,64,128]{2,1,0:T(8,128)S(1)} async-done(((f32[8,64,128]{2,1,0:T(8,128)}), f32[8,64,128]{2,1,0:T(8,128)S(1)}, u32[]{:S(2)}, u32[]{:S(2)}) %all-to-all-start.1) | async-done | bytes 262176 | tf_op jit(solution)/shard_map/all_to_all | solution.py:554
  54.1 0.1 collective-permute-start.7
  54.2 0.3 collective-permute-done.6.far_wh
  54.4 0.9 %collective-permute-done.7.twin = f32[64,128]{1,0:T(8,128)S(1)} collective-permute-done((f32[64,128]{1,0:T(8,128)S(1)}, f32[64,128]{1,0:T(8,128)S(1)}, u32[]{:S(2)}, u32[]{:S(2)}) %collective-permute-start.7) | collective-permute-done | bytes 32800 | tf_op jit(solution)/shard_map/ppermute | solution.py:550
  55.4 0.0 collective-permute-done.8.yz
  55.4 4.6 %shard_map.34 = bf16[45,64,128]{2,1,0:T(8,128)(2,1)} custom-call(f32[64,128]{1,0:T(8,128)S(1)} %get-tuple-element.14.wh, f32[64,32]{1,0:T(8,128)S(1)} %get-tuple-element.15.c, f32[64,128]{1,0:T(8,128)S(1)} %collective-permute-done.6.far_wh, f32[64,128]{1,0:T(8,128)S(1)} %reduce_sum.19.cs, f32[64,128]{1,0:T(8,128)S(1)} %collective-permute-done.7.twin, ...), custom_call_target="tpu_custom_call" | custom-call | flops 1048576 | bytes 1048576 | tf_op jit(solution)/shard_map/pallas_call | solution.py:578
  (2 shorter events, 0.0 us)
Async XLA Ops:
  0.0 10.7 %copy-start = (bf16[64,45,128]{2,0,1:T(8,128)(2,1)S(1)}, bf16[64,45,128]{2,0,1:T(8,128)(2,1)}, u32[]{:S(2)}) copy-start(bf16[64,45,128]{2,0,1:T(8,128)(2,1)} %param.2) | copy-start | bytes 2211844
  0.0 10.7 %copy-start.1 = (f32[45,128]{1,0:T(8,128)S(1)}, f32[45,128]{1,0:T(8,128)}, u32[]{:S(2)}) copy-start(f32[45,128]{1,0:T(8,128)} %d_ref.3) | copy-start | bytes 69124
  1.6 6.6 %collective-permute-start = (bf16[272,128]{1,0:T(8,128)(2,1)}, bf16[272,128]{1,0:T(8,128)(2,1)S(1)}, u32[]{:S(2)}, u32[]{:S(2)}) collective-permute-start(bf16[272,128]{1,0:T(8,128)(2,1)} %get-tuple-element.11), channel_id=1, source_target_pairs={{2,4},{4,2},{3,5},{5,3},{10,12},{12,10},{11,13},{13,11},{18,20},{2... | collective-permute-start | bytes 208904 | tf_op jit(solution)/shard_map/ppermute | solution.py:156
  2.3 8.4 %collective-permute-start.1 = (bf16[272,128]{1,0:T(8,128)(2,1)}, bf16[272,128]{1,0:T(8,128)(2,1)S(1)}, u32[]{:S(2)}, u32[]{:S(2)}) collective-permute-start(bf16[272,128]{1,0:T(8,128)(2,1)} %get-tuple-element.12), channel_id=1, source_target_pairs={{0,2},{4,6},{2,0},{6,4},{1,3},{5,7},{3,1},{7,5},{8,10},{12,14},{10... | collective-permute-start | bytes 208904 | tf_op jit(solution)/shard_map/ppermute | solution.py:156
  11.4 4.3 %collective-permute-start.2 = (bf16[272,128]{1,0:T(8,128)(2,1)S(1)}, bf16[272,128]{1,0:T(8,128)(2,1)S(1)}, u32[]{:S(2)}, u32[]{:S(2)}) collective-permute-start(bf16[272,128]{1,0:T(8,128)(2,1)S(1)} %shard_map.29), channel_id=1, source_target_pairs={{0,1},{1,0},{2,3},{3,2},{4,5},{5,4},{6,7},{7,6},{8,9},{9,8},{10,11... | collective-permute-start | bytes 208904 | tf_op jit(solution)/shard_map/ppermute | solution.py:163
  20.0 2.3 %collective-permute-start.3 = (bf16[45,64,128]{2,1,0:T(8,128)(2,1)S(1)}, bf16[45,64,128]{2,1,0:T(8,128)(2,1)S(1)}, u32[]{:S(2)}, u32[]{:S(2)}) collective-permute-start(bf16[45,64,128]{2,1,0:T(8,128)(2,1)S(1)} %shard_map.30.own_ref.yo), channel_id=1, source_target_pairs={{0,8},{8,0},{16,24},{24,16},{1,9},{9,1},{17,25},{25,17},{2,10},{10... | collective-permute-start | bytes 2211848 | tf_op jit(solution)/shard_map/ppermute | solution.py:550
  20.0 18.9 %collective-permute-start.4 = (bf16[45,64,128]{2,1,0:T(8,128)(2,1)S(1)}, bf16[45,64,128]{2,1,0:T(8,128)(2,1)S(1)}, u32[]{:S(2)}, u32[]{:S(2)}) collective-permute-start(bf16[45,64,128]{2,1,0:T(8,128)(2,1)S(1)} %shard_map.30.own_ref.yo), channel_id=1, source_target_pairs={{0,16},{8,24},{16,0},{24,8},{1,17},{9,25},{17,1},{25,9},{2,18},{10... | collective-permute-start | bytes 2211848 | tf_op jit(solution)/shard_map/ppermute | solution.py:550
  35.3 3.7 %collective-permute-start.5 = (f32[48,128]{1,0:T(8,128)S(1)}, f32[48,128]{1,0:T(8,128)S(1)}, u32[]{:S(2)}, u32[]{:S(2)}) collective-permute-start(f32[48,128]{1,0:T(8,128)S(1)} %reduce_sum.18.g_ref), channel_id=1, source_target_pairs={{0,8},{8,0},{16,24},{24,16},{1,9},{9,1},{17,25},{25,17},{2,10},{10... | collective-permute-start | bytes 73736 | tf_op jit(solution)/shard_map/ppermute | solution.py:550
  38.9 16.4 %collective-permute-start.8 = (bf16[45,64,128]{2,1,0:T(8,128)(2,1)S(1)}, bf16[45,64,128]{2,1,0:T(8,128)(2,1)S(1)}, u32[]{:S(2)}, u32[]{:S(2)}) collective-permute-start(bf16[45,64,128]{2,1,0:T(8,128)(2,1)S(1)} %collective-permute-done.4.far_ref.yy), channel_id=1, source_target_pairs={{0,8},{8,0},{16,24},{24,16},{1,9},{9,1},{17,25},{25,17},{2,10},{10... | collective-permute-start | bytes 2211848 | tf_op jit(solution)/shard_map/ppermute | solution.py:550
  40.3 13.8 %all-to-all-start.1 = ((f32[8,64,128]{2,1,0:T(8,128)}), f32[8,64,128]{2,1,0:T(8,128)S(1)}, u32[]{:S(2)}, u32[]{:S(2)}) async-start(f32[8,64,128]{2,1,0:T(8,128)} %shard_map.33), calls=%async_computation.1 | async-start | bytes 524288 | tf_op jit(solution)/shard_map/all_to_all | solution.py:554
  50.5 3.9 %collective-permute-start.6 = (f32[64,128]{1,0:T(8,128)S(1)}, f32[64,128]{1,0:T(8,128)S(1)}, u32[]{:S(2)}, u32[]{:S(2)}) collective-permute-start(f32[64,128]{1,0:T(8,128)S(1)} %get-tuple-element.14.wh), channel_id=1, source_target_pairs={{0,16},{8,24},{16,0},{24,8},{1,17},{9,25},{17,1},{25,9},{2,18},{10... | collective-permute-start | bytes 98312 | tf_op jit(solution)/shard_map/ppermute | solution.py:550
  54.1 1.3 %collective-permute-start.7 = (f32[64,128]{1,0:T(8,128)S(1)}, f32[64,128]{1,0:T(8,128)S(1)}, u32[]{:S(2)}, u32[]{:S(2)}) collective-permute-start(f32[64,128]{1,0:T(8,128)S(1)} %reduce_sum.19.cs), channel_id=1, source_target_pairs={{0,8},{8,0},{16,24},{24,16},{1,9},{9,1},{17,25},{25,17},{2,10},{10... | collective-permute-start | bytes 98312 | tf_op jit(solution)/shard_map/ppermute | solution.py:550

commit v8 on v7

--- a/solution.py
+++ b/solution.py
@@ -167,63 +167,36 @@
     return side, a, b
 
 
-PADDED = 160
-
-
-def smooth_body(x_ref, d_ref, side_ref, a_ref, b_ref, y_ref, u0, u1, ce, cs, dn, dt):
-    rows, snaps, width = x_ref.shape
-    half = -(-rows // 2)
-    shift = rows - half
-    count = half + 2 * PASSES
+OWN = 16
+EDGE = 16
+EDGES = 8 + 2 * EDGE + 8
+
+
+def spread_faces(here, beside, k0, count, ce, cs, rows_at, snaps, shift):
+    n = here.shape[0]
+    lane = lane_iota((1, LANES))
+    faces = jnp.concatenate([here + beside, here + roll(here, -1)], axis=0) * 0.5
+    high, low = (v.astype(jnp.float32) for v in split2(faces))
+    terms = jnp.where(lane < LANES // 2, high, roll(low, LANES // 2)).astype(jnp.bfloat16)
+    source = lax.broadcasted_iota(jnp.int32, (LANES, LANES), 0) % (LANES // 2)
+    relative = source - jnp.where(lane_iota((LANES, LANES)) < snaps, 0, shift)
+    for k in range(count):
+        pick = (relative == k0 + k).astype(jnp.bfloat16)
+        spread = jnp.dot(terms, pick, preferred_element_type=jnp.float32)
+        ce[k, rows_at, :] = spread[:n]
+        cs[k, rows_at, :] = spread[n:]
+
+
+def smoothing_passes(u0, u1, ce, cs, low, high, own_low, own_high, half, left):
+    count = u0.shape[0]
     lats, lat = lax.axis_size("lat"), lax.axis_index("lat")
-    lane = lane_iota((1, LANES))
-    left = lane < snaps
-    own = 16
-    east = own + width
-    unit = eye(width)
-    edge = PASSES * snaps
-    picked = by_side(a_ref, b_ref)
-    north, south = picked(0, edge)
-    north_d, south_d = (v.astype(jnp.float32) for v in picked(edge, edge + 16))
-
-    for k in range(count):
-        u0[k, own:east, :] = dot_t(unit, tile_rows(x_ref, north, south, k - PASSES))
-        pair = side_ref[16 * (k // 2) : 16 * (k // 2) + 16, :].astype(jnp.float32)
-        halo = pair[8 * (k % 2) : 8 * (k % 2) + 8]
-        u0[k, own - 8 : own, :] = halo
-        u0[k, east : east + 8, :] = halo
-
-    extend_rows(dn, d_ref, north_d, south_d)
-    dt[own:east, :] = dn[...].T
-    side_d = side_ref[side_ref.shape[0] - 16 :, :].astype(jnp.float32)
-    halo = side_d[0:8] + side_d[8:16]
-    dt[0 : own - 8, :] = jnp.zeros((own - 8, LANES), jnp.float32)
-    dt[own - 8 : own, :] = halo
-    dt[east : east + 8, :] = halo
-    dt[east + 8 :, :] = jnp.zeros((PADDED - east - 8, LANES), jnp.float32)
-    low, high = own - 8, east + 8
-    here = dt[low:high, :]
-    faces = jnp.concatenate([here + dt[low + 1 : high + 1, :], here + roll(here, -1)], axis=0) * 0.5
-    f_high, f_low = split2(faces)
-    terms = jnp.where(lane < LANES // 2, f_high.astype(jnp.float32), roll(f_low.astype(jnp.float32), LANES // 2))
-    terms = terms.astype(jnp.bfloat16)
-    source = lax.broadcasted_iota(jnp.int32, (LANES, LANES), 0) % (LANES // 2)
-    offset = jnp.where(lane_iota((LANES, LANES)) < snaps, 0, shift)
-    relative = source - offset
-    for k in range(count):
-        spread = jnp.dot(
-            terms, (relative == k).astype(jnp.bfloat16), preferred_element_type=jnp.float32
-        )
-        ce[k, low:high, :] = spread[: high - low]
-        cs[k, low:high, :] = spread[high - low :]
-
     buffers = (u0, u1)
     first_row = lax.broadcasted_iota(jnp.int32, (8, LANES), 0) == 0
     for step in range(PASSES):
         src, dst = buffers[step % 2], buffers[(step + 1) % 2]
         final = step == PASSES - 1
         start, stop = step + 1, count - 1 - step
-        blocks = range(own, east, 8) if final else range(low, high, 8)
+        blocks = range(own_low, own_high, 8) if final else range(low, high, 8)
         current = [src[start, r : r + 8, :] for r in blocks]
         above = [
             cs[start - 1, r : r + 8, :] * (c - src[start - 1, r : r + 8, :])
@@ -235,8 +208,9 @@
 
         for k in range(start, stop):
             before = None
-            if final:
-                before = pltpu.roll(eastward(k, low, src[k, low:own, :]), 1, 0)
+            if blocks[0] > low:
+                r = blocks[0] - 8
+                before = pltpu.roll(eastward(k, r, src[k, r : r + 8, :]), 1, 0)
             for i, r in enumerate(blocks):
                 here = current[i]
                 east_flux = eastward(k, r, here)
@@ -247,35 +221,113 @@
                 dst[k, r : r + 8, :] = here + ((south_flux - above[i]) + (east_flux - west_flux))
                 current[i], above[i], before = below, south_flux, turned
         if not final:
+            north, beyond, at = PASSES - 1, PASSES + half, slice(low, high)
 
             @pl.when(lat == 0)
             def _():
-                dst[PASSES - 1, low:high, :] = jnp.where(left, 0.0, dst[PASSES - 1, low:high, :])
+                dst[north, at, :] = jnp.where(left, 0.0, dst[north, at, :])
 
             @pl.when(lat == lats - 1)
             def _():
-                dst[PASSES + half, low:high, :] = jnp.where(left, dst[PASSES + half, low:high, :], 0.0)
-
-    tall = -(-half // 8) * 8
-    row = lax.broadcasted_iota(jnp.int32, (tall, LANES), 0) + jnp.where(lane_iota((tall, LANES)) < snaps, 0, shift)
+                dst[beyond, at, :] = jnp.where(left, dst[beyond, at, :], 0.0)
+
+    return buffers[PASSES % 2]
+
+
+def area_scale(rows, snaps):
+    half = -(-rows // 2)
+    shape = (-(-half // 8) * 8, LANES)
+    lats, lat = lax.axis_size("lat"), lax.axis_index("lat")
+    row = lax.broadcasted_iota(jnp.int32, shape, 0) + jnp.where(lane_iota(shape) < snaps, 0, rows - half)
     angle = ((row + lat * rows).astype(jnp.float32) + 0.5) * math.pi / (rows * lats) - math.pi / 2
-    scale = jnp.sqrt(jnp.maximum(jnp.cos(angle), 0.0))
+    return jnp.sqrt(jnp.maximum(jnp.cos(angle), 0.0))
+
+
+def interior_body(x_ref, d_ref, b_ref, a_ref, y_ref, ends_ref, dt_ref, u0, u1, ce, cs, dn):
+    rows, snaps, width = x_ref.shape
+    half = -(-rows // 2)
+    shift = rows - half
+    count = half + 2 * PASSES
+    lane = lane_iota((1, LANES))
+    east = OWN + width
+    unit = eye(width)
+    edge = PASSES * snaps
+    picked = by_side(a_ref, b_ref)
+    north, south = picked(0, edge)
+    north_d, south_d = (v.astype(jnp.float32) for v in picked(edge, edge + 16))
+    outside = jnp.zeros((8, LANES), jnp.float32)
+    for k in range(count):
+        tile = dot_t(unit, tile_rows(x_ref, north, south, k - PASSES))
+        u0[k, OWN:east, :] = tile
+        ends_ref[k, :EDGE, :] = tile[:EDGE]
+        ends_ref[k, EDGE:, :] = tile[width - EDGE :]
+        u0[k, east : east + 8, :] = outside
+        u1[k, east : east + 8, :] = outside
+    extend_rows(dn, d_ref, north_d, south_d)
+    dt = dn[...].T
+    dt_ref[:EDGE, :] = dt[:EDGE]
+    dt_ref[EDGE:, :] = dt[width - EDGE :]
+    beside = jnp.concatenate([dt[1:], jnp.zeros((1, LANES), jnp.float32)], axis=0)
+    spread_faces(dt, beside, 0, count, ce, cs, slice(OWN, east), snaps, shift)
+    done = smoothing_passes(u0, u1, ce, cs, OWN, east, OWN, east, half, lane < snaps)
+    scale = area_scale(rows, snaps)
     for t in range(half):
-        weighted = (dst[t + PASSES, own:east, :] * scale[t : t + 1]).astype(jnp.bfloat16)
+        weighted = (done[t + PASSES, OWN:east, :] * scale[t : t + 1]).astype(jnp.bfloat16)
         both = dot_t(unit, weighted).astype(jnp.bfloat16)
         y_ref[t] = both[:snaps]
         y_ref[t + shift] = both[snaps:]
 
 
+def ends_body(y_in, ends_ref, dt_ref, side_ref, y_ref, u0, u1, ce, cs):
+    rows, snaps, width = y_in.shape
+    half = -(-rows // 2)
+    shift = rows - half
+    count = half + 2 * PASSES
+    lane = lane_iota((1, LANES))
+    low, high = 8, 8 + EDGES
+    inner = high - 8
+    for k in range(count):
+        pair = side_ref[16 * (k // 2) : 16 * (k // 2) + 16, :].astype(jnp.float32)
+        halo = pair[8 * (k % 2) : 8 * (k % 2) + 8]
+        u0[k, low : low + 8, :] = halo
+        u0[k, low + 8 : inner, :] = ends_ref[k]
+        u0[k, inner:high, :] = halo
+    side_d = side_ref[side_ref.shape[0] - 16 :, :].astype(jnp.float32)
+    halo = side_d[0:8] + side_d[8:16]
+    here = jnp.concatenate([halo, dt_ref[...], halo], axis=0)
+    beside = jnp.concatenate([here[1:], jnp.zeros((1, LANES), jnp.float32)], axis=0)
+    spread_faces(here, beside, 0, count, ce, cs, slice(low, high), snaps, shift)
+    outside = jnp.zeros((8, LANES), jnp.float32)
+    for buffer in (u0, u1):
+        for k in range(count):
+            buffer[k, high : high + 8, :] = outside
+    done = smoothing_passes(u0, u1, ce, cs, low, high, low + 8, inner, half, lane < snaps)
+    scale = area_scale(rows, snaps)
+    unit = eye(width)
+    middle = jnp.zeros((width - 16, LANES), jnp.float32)
+    ends = (lane < PASSES) | (lane >= width - PASSES)
+    for t in range(half):
+        west = done[t + PASSES, low + 8 : low + 16, :]
+        east = done[t + PASSES, inner - 8 : inner, :]
+        weighted = (jnp.concatenate([west, middle, east], axis=0) * scale[t : t + 1]).astype(jnp.bfloat16)
+        both = dot_t(unit, weighted)
+        for r, part in ((t, both[:snaps]), (t + shift, both[snaps:])):
+            y_ref[r] = jnp.where(ends, part, y_in[r].astype(jnp.float32)).astype(jnp.bfloat16)
+
+
 def smooth(x, d, side, a, b):
     rows, snaps, width = x.shape
     count = -(-rows // 2) + 2 * PASSES
-    field = VMEM((count, PADDED, LANES), jnp.float32)
-    return kernel_call(
-        smooth_body,
-        jax.ShapeDtypeStruct((rows, snaps, width), jnp.bfloat16),
-        [field] * 4 + [VMEM((width, LANES), jnp.float32), VMEM((PADDED, LANES), jnp.float32)],
-    )(x, d, side, a, b)
+    f32 = lambda *shape: jax.ShapeDtypeStruct(shape, jnp.float32)
+    field = lambda n: VMEM((count, n, LANES), jnp.float32)
+    out = jax.ShapeDtypeStruct(x.shape, jnp.bfloat16)
+    y, ends, dt = kernel_call(
+        interior_body,
+        (out, f32(count, 2 * EDGE, LANES), f32(2 * EDGE, LANES)),
+        [field(OWN + width + 16)] * 4 + [VMEM((width, LANES), jnp.float32)],
+        flops=1 << 32,
+    )(x, d, b, a)
+    return kernel_call(ends_body, out, [field(EDGES + 16)] * 4)(y, ends, dt, side)
 
 
 def mm(a, b):

time: 60.3 us -> 58.5 us (0.970)
  waiting for transfers between devices: 12.8 us -> 10.9 us
  Pallas kernels: 19.2 us -> 20.6 us
  blocking collectives: 12.3 us -> 11.3 us
    ppermute x1, waiting for transfers between devices: 2.82 us -> 0.01 us  [halo_exchange(): side = lax.ppermute(packed, 'lon', forward)]
    pallas_call x1 -> x2, Pallas kernels: 4.22 us -> 5.61 us  [the longest x1 3.85 us: smooth(): kernel_call(interior_body, (out, f32(count, 2 * EDGE, LANES), f32(2 * EDG...]
    all_to_all x1, blocking collectives: 12.3 us -> 11.3 us  [gathered(): return lax.all_to_all(parts, ('lat', 'lon'), 0, 0, tiled=True)]
    ppermute x6, waiting for transfers between devices: 5.4 us -> 6.31 us  [exchanged(): lax.ppermute(block, 'tm', [(i, i ^ 1 << level) for i in range(count)])]
    all_to_all x1, starting transfers between devices: 4.22 us -> 3.59 us  [gathered(): return lax.all_to_all(parts, ('lat', 'lon'), 0, 0, tiled=True)]
  transfers between devices with their start and end apart: 10 -> 10, of which waited for: 7 -> 6; matrix products, arithmetic and copies ran while one was open for 0% -> 0% of each run, Pallas kernels for 13% -> 20%
where the time goes in v8:
time: 58.5 us; the launch traced here: 58.2 us
  Pallas kernels  20.6 us (35%)
  starting transfers between devices  15.1 us (26%)
  blocking collectives  11.3 us (19%)
  waiting for transfers between devices  10.9 us (19%)
    all_to_all x1, blocking collectives, gathered(): return lax.all_to_all(parts, ('lat', 'lon'), 0, 0, tiled=True)  11.3 us
    ppermute x2, starting transfers between devices, swapped(): return lax.ppermute(message, 'lat', pairs + [(j, i) for i, j in pairs])  6.57 us
    ppermute x6, waiting for transfers between devices, exchanged(): lax.ppermute(block, 'tm', [(i, i ^ 1 << level) for i in range(count)])  6.31 us
    pallas_call x1, Pallas kernels, shards(): kernel_call(pair_levels_body, (f32(2 * RANK, 2 * snaps), f32(snaps, RANK)...  6.02 us
    pallas_call x1, Pallas kernels, shards(): out = result_call(quad_project_body, rows, snaps, width)(*operands)  4.63 us
    pallas_call x1, Pallas kernels, smooth(): kernel_call(interior_body, (out, f32(count, 2 * EDGE, LANES), f32(2 * EDG...  3.85 us
    all_to_all x1, starting transfers between devices, gathered(): return lax.all_to_all(parts, ('lat', 'lon'), 0, 0, tiled=True)  3.59 us
    ppermute x6, starting transfers between devices, exchanged(): lax.ppermute(block, 'tm', [(i, i ^ 1 << level) for i in range(count)])  3.36 us
  transfers between devices with their start and end apart: 10, of which 6 were waited for; matrix products, arithmetic and copies ran while one was open for 0% of the time, Pallas kernels for 20%

profile of v8, /device:TPU:0, one launch (start us, length us, event | category | flops | bytes accessed | tf_op | source)
XLA Modules:
  0.0 58.2 jit_solution(13415587145751507578)
XLA Ops:
  0.0 0.0 copy-start
  0.0 1.6 %shard_map.28 = (bf16[272,128]{1,0:T(8,128)(2,1)}, bf16[272,128]{1,0:T(8,128)(2,1)}) custom-call(bf16[45,64,128]{2,1,0:T(8,128)(2,1)} %bitcast.2, f32[45,128]{1,0:T(8,128)} %d_ref.3), custom_call_target="tpu_custom_call" | custom-call | flops 1048576 | bytes 1048576 | tf_op jit(solution)/shard_map/pallas_call | solution.py:145
  1.6 0.7 %collective-permute-start = (bf16[272,128]{1,0:T(8,128)(2,1)}, bf16[272,128]{1,0:T(8,128)(2,1)S(1)}, u32[]{:S(2)}, u32[]{:S(2)}) collective-permute-start(bf16[272,128]{1,0:T(8,128)(2,1)} %get-tuple-element.14), channel_id=1, source_target_pairs={{2,4},{4,2},{3,5},{5,3},{10,12},{12,10},{11,13},{13,11},{18,20},{2... | collective-permute-start | bytes 208904 | tf_op jit(solution)/shard_map/ppermute | solution.py:156
  2.3 5.9 %collective-permute-start.1 = (bf16[272,128]{1,0:T(8,128)(2,1)}, bf16[272,128]{1,0:T(8,128)(2,1)S(1)}, u32[]{:S(2)}, u32[]{:S(2)}) collective-permute-start(bf16[272,128]{1,0:T(8,128)(2,1)} %get-tuple-element.15), channel_id=1, source_target_pairs={{0,2},{4,6},{2,0},{6,4},{1,3},{5,7},{3,1},{7,5},{8,10},{12,14},{10... | collective-permute-start | bytes 208904 | tf_op jit(solution)/shard_map/ppermute | solution.py:156
  8.2 0.0 collective-permute-done.b_ref
  8.2 2.5 %collective-permute-done.1.a_ref = bf16[272,128]{1,0:T(8,128)(2,1)S(1)} collective-permute-done((bf16[272,128]{1,0:T(8,128)(2,1)}, bf16[272,128]{1,0:T(8,128)(2,1)S(1)}, u32[]{:S(2)}, u32[]{:S(2)}) %collective-permute-start.1) | collective-permute-done | bytes 69664 | tf_op jit(solution)/shard_map/ppermute | solution.py:156
  10.7 0.0 copy-done
  10.7 0.0 copy-done.1
  10.7 0.7 %shard_map.30 = bf16[272,128]{1,0:T(8,128)(2,1)S(1)} custom-call(bf16[45,64,128]{2,1,0:T(8,128)(2,1)S(1)} %bitcast.3, f32[45,128]{1,0:T(8,128)S(1)} %copy-done.1, bf16[272,128]{1,0:T(8,128)(2,1)S(1)} %collective-permute-done.b_ref, bf16[272,128]{1,0:T(8,128)(2,1)S(1)} %collective-permute-done.1.a_ref), custom_call_target="tpu_custom_call" | custom-call | flops 1048576 | bytes 1048576 | tf_op jit(solution)/shard_map/pallas_call | solution.py:159
  11.4 1.5 %collective-permute-start.2 = (bf16[272,128]{1,0:T(8,128)(2,1)S(1)}, bf16[272,128]{1,0:T(8,128)(2,1)S(1)}, u32[]{:S(2)}, u32[]{:S(2)}) collective-permute-start(bf16[272,128]{1,0:T(8,128)(2,1)S(1)} %shard_map.30), channel_id=1, source_target_pairs={{0,1},{1,0},{2,3},{3,2},{4,5},{5,4},{6,7},{7,6},{8,9},{9,8},{10,11... | collective-permute-start | bytes 208904 | tf_op jit(solution)/shard_map/ppermute | solution.py:163
  12.9 3.8 %shard_map.29 = (bf16[45,64,128]{2,1,0:T(8,128)(2,1)S(1)}, f32[31,32,128]{2,1,0:T(8,128)S(1)}, f32[32,128]{1,0:T(8,128)S(1)}) custom-call(bf16[45,64,128]{2,1,0:T(8,128)(2,1)S(1)} %bitcast.4, f32[45,128]{1,0:T(8,128)S(1)} %copy-done.1, bf16[272,128]{1,0:T(8,128)(2,1)S(1)} %collective-permute-done.b_ref, bf16[272,128]{1,0:T(8,128)(2,1)S(1)} %collective-permute-done.1.a_ref), custom_call_target="tpu_custom_call" | custom-call | flops 4294967296 | bytes 1048576 | tf_op jit(solution)/shard_map/pallas_call | solution.py:324
  16.8 0.0 collective-permute-done.2.side_ref
  16.8 1.8 %shard_map.31.own_ref.yo = bf16[45,64,128]{2,1,0:T(8,128)(2,1)S(1)} custom-call(bf16[45,64,128]{2,1,0:T(8,128)(2,1)S(1)} %get-tuple-element.16.y_in, f32[31,32,128]{2,1,0:T(8,128)S(1)} %get-tuple-element.17.ends_ref, f32[32,128]{1,0:T(8,128)S(1)} %get-tuple-element.18.dt_ref, bf16[272,128]{1,0:T(8,128)(2,1)S(1)} %collective-permute-done.2.side_ref), custom_call_target="tpu_custom_call" | custom-call | flops 1048576 | bytes 1048576 | tf_op jit(solution)/shard_map/pallas_call | solution.py:330
  18.5 0.1 collective-permute-start.3
  18.6 1.6 %collective-permute-start.4 = (bf16[45,64,128]{2,1,0:T(8,128)(2,1)S(1)}, bf16[45,64,128]{2,1,0:T(8,128)(2,1)S(1)}, u32[]{:S(2)}, u32[]{:S(2)}) collective-permute-start(bf16[45,64,128]{2,1,0:T(8,128)(2,1)S(1)} %shard_map.31.own_ref.yo), channel_id=1, source_target_pairs={{0,16},{8,24},{16,0},{24,8},{1,17},{9,25},{17,1},{25,9},{2,18},{10... | collective-permute-start | bytes 2211848 | tf_op jit(solution)/shard_map/ppermute | solution.py:602
  20.2 0.6 %collective-permute-done.3.other_ref.yp = bf16[45,64,128]{2,1,0:T(8,128)(2,1)S(1)} collective-permute-done((bf16[45,64,128]{2,1,0:T(8,128)(2,1)S(1)}, bf16[45,64,128]{2,1,0:T(8,128)(2,1)S(1)}, u32[]{:S(2)}, u32[]{:S(2)}) %collective-permute-start.3) | collective-permute-done | bytes 737312 | tf_op jit(solution)/shard_map/ppermute | solution.py:602
  20.8 0.7 %shard_map.32 = f32[8,48,128]{2,1,0:T(8,128)S(1)} custom-call(bf16[45,64,128]{2,1,0:T(8,128)(2,1)S(1)} %shard_map.31.own_ref.yo, bf16[45,64,128]{2,1,0:T(8,128)(2,1)S(1)} %collective-permute-done.3.other_ref.yp), custom_call_target="tpu_custom_call" | custom-call | flops 1048576 | bytes 1048576 | tf_op jit(solution)/shard_map/pallas_call | solution.py:618
  21.6 11.3 %all_to_all.10 = f32[8,48,128]{2,1,0:T(8,128)S(1)} all-to-all(f32[8,48,128]{2,1,0:T(8,128)S(1)} %shard_map.32), channel_id=1, replica_groups=mesh['tm'=4,'lat'=4,'lon'=2] {'lat','lon'}, dimensions={0} | all-to-all | bytes 393216 | tf_op jit(solution)/shard_map/all_to_all | solution.py:606
  32.9 0.1 collective-permute-start.5
  33.0 4.5 %collective-permute-done.4.far_ref.yy = bf16[45,64,128]{2,1,0:T(8,128)(2,1)S(1)} collective-permute-done((bf16[45,64,128]{2,1,0:T(8,128)(2,1)S(1)}, bf16[45,64,128]{2,1,0:T(8,128)(2,1)S(1)}, u32[]{:S(2)}, u32[]{:S(2)}) %collective-permute-start.4) | collective-permute-done | bytes 737312 | tf_op jit(solution)/shard_map/ppermute | solution.py:602
  37.5 0.0 collective-permute-done.5.gp_ref
  37.5 0.0 collective-permute-start.8
  37.5 1.3 %shard_map.34 = f32[8,64,128]{2,1,0:T(8,128)} custom-call(bf16[45,64,128]{2,1,0:T(8,128)(2,1)S(1)} %shard_map.31.own_ref.yo, bf16[45,64,128]{2,1,0:T(8,128)(2,1)S(1)} %collective-permute-done.3.other_ref.yp, bf16[45,64,128]{2,1,0:T(8,128)(2,1)S(1)} %collective-permute-done.4.far_ref.yy), custom_call_target="tpu_custom_call" | custom-call | flops 1048576 | bytes 1048576 | tf_op jit(solution)/shard_map/pallas_call | solution.py:622
  38.8 3.6 %all-to-all-start.1 = ((f32[8,64,128]{2,1,0:T(8,128)}), f32[8,64,128]{2,1,0:T(8,128)S(1)}, u32[]{:S(2)}, u32[]{:S(2)}) async-start(f32[8,64,128]{2,1,0:T(8,128)} %shard_map.34), calls=%async_computation.1 | async-start | bytes 524288 | tf_op jit(solution)/shard_map/all_to_all | solution.py:606
  42.4 6.0 %shard_map.33 = (f32[64,128]{1,0:T(8,128)S(1)}, f32[64,32]{1,0:T(8,128)S(1)}) custom-call(f32[48,128]{1,0:T(8,128)S(1)} %reduce_sum.18.g_ref, f32[48,128]{1,0:T(8,128)S(1)} %collective-permute-done.5.gp_ref), custom_call_target="tpu_custom_call" | custom-call | flops 4294967296 | bytes 1048576 | tf_op jit(solution)/shard_map/pallas_call | solution.py:624
  48.5 1.6 %collective-permute-start.6 = (f32[64,128]{1,0:T(8,128)S(1)}, f32[64,128]{1,0:T(8,128)S(1)}, u32[]{:S(2)}, u32[]{:S(2)}) collective-permute-start(f32[64,128]{1,0:T(8,128)S(1)} %get-tuple-element.20.wh), channel_id=1, source_target_pairs={{0,16},{8,24},{16,0},{24,8},{1,17},{9,25},{17,1},{25,9},{2,18},{10... | collective-permute-start | bytes 98312 | tf_op jit(solution)/shard_map/ppermute | solution.py:602
  50.0 2.1 %all-to-all-done.1 = f32[8,64,128]{2,1,0:T(8,128)S(1)} async-done(((f32[8,64,128]{2,1,0:T(8,128)}), f32[8,64,128]{2,1,0:T(8,128)S(1)}, u32[]{:S(2)}, u32[]{:S(2)}) %all-to-all-start.1) | async-done | bytes 262176 | tf_op jit(solution)/shard_map/all_to_all | solution.py:606
  52.1 0.1 collective-permute-start.7
  52.2 0.2 collective-permute-done.6.far_wh
  52.4 1.0 %collective-permute-done.7.twin = f32[64,128]{1,0:T(8,128)S(1)} collective-permute-done((f32[64,128]{1,0:T(8,128)S(1)}, f32[64,128]{1,0:T(8,128)S(1)}, u32[]{:S(2)}, u32[]{:S(2)}) %collective-permute-start.7) | collective-permute-done | bytes 32800 | tf_op jit(solution)/shard_map/ppermute | solution.py:602
  53.4 0.0 collective-permute-done.8.yz
  53.4 4.6 %shard_map.35 = bf16[45,64,128]{2,1,0:T(8,128)(2,1)} custom-call(f32[64,128]{1,0:T(8,128)S(1)} %get-tuple-element.20.wh, f32[64,32]{1,0:T(8,128)S(1)} %get-tuple-element.21.c, f32[64,128]{1,0:T(8,128)S(1)} %collective-permute-done.6.far_wh, f32[64,128]{1,0:T(8,128)S(1)} %reduce_sum.19.cs, f32[64,128]{1,0:T(8,128)S(1)} %collective-permute-done.7.twin, ...), custom_call_target="tpu_custom_call" | custom-call | flops 1048576 | bytes 1048576 | tf_op jit(solution)/shard_map/pallas_call | solution.py:630
  (3 shorter events, 0.0 us)
Async XLA Ops:
  0.0 10.7 %copy-start = (bf16[64,45,128]{2,0,1:T(8,128)(2,1)S(1)}, bf16[64,45,128]{2,0,1:T(8,128)(2,1)}, u32[]{:S(2)}) copy-start(bf16[64,45,128]{2,0,1:T(8,128)(2,1)} %param.2) | copy-start | bytes 2211844
  0.0 10.7 %copy-start.1 = (f32[45,128]{1,0:T(8,128)S(1)}, f32[45,128]{1,0:T(8,128)}, u32[]{:S(2)}) copy-start(f32[45,128]{1,0:T(8,128)} %d_ref.3) | copy-start | bytes 69124
  1.6 6.6 %collective-permute-start = (bf16[272,128]{1,0:T(8,128)(2,1)}, bf16[272,128]{1,0:T(8,128)(2,1)S(1)}, u32[]{:S(2)}, u32[]{:S(2)}) collective-permute-start(bf16[272,128]{1,0:T(8,128)(2,1)} %get-tuple-element.14), channel_id=1, source_target_pairs={{2,4},{4,2},{3,5},{5,3},{10,12},{12,10},{11,13},{13,11},{18,20},{2... | collective-permute-start | bytes 208904 | tf_op jit(solution)/shard_map/ppermute | solution.py:156
  2.3 8.4 %collective-permute-start.1 = (bf16[272,128]{1,0:T(8,128)(2,1)}, bf16[272,128]{1,0:T(8,128)(2,1)S(1)}, u32[]{:S(2)}, u32[]{:S(2)}) collective-permute-start(bf16[272,128]{1,0:T(8,128)(2,1)} %get-tuple-element.15), channel_id=1, source_target_pairs={{0,2},{4,6},{2,0},{6,4},{1,3},{5,7},{3,1},{7,5},{8,10},{12,14},{10... | collective-permute-start | bytes 208904 | tf_op jit(solution)/shard_map/ppermute | solution.py:156
  11.4 5.4 %collective-permute-start.2 = (bf16[272,128]{1,0:T(8,128)(2,1)S(1)}, bf16[272,128]{1,0:T(8,128)(2,1)S(1)}, u32[]{:S(2)}, u32[]{:S(2)}) collective-permute-start(bf16[272,128]{1,0:T(8,128)(2,1)S(1)} %shard_map.30), channel_id=1, source_target_pairs={{0,1},{1,0},{2,3},{3,2},{4,5},{5,4},{6,7},{7,6},{8,9},{9,8},{10,11... | collective-permute-start | bytes 208904 | tf_op jit(solution)/shard_map/ppermute | solution.py:163
  18.5 2.3 %collective-permute-start.3 = (bf16[45,64,128]{2,1,0:T(8,128)(2,1)S(1)}, bf16[45,64,128]{2,1,0:T(8,128)(2,1)S(1)}, u32[]{:S(2)}, u32[]{:S(2)}) collective-permute-start(bf16[45,64,128]{2,1,0:T(8,128)(2,1)S(1)} %shard_map.31.own_ref.yo), channel_id=1, source_target_pairs={{0,8},{8,0},{16,24},{24,16},{1,9},{9,1},{17,25},{25,17},{2,10},{10... | collective-permute-start | bytes 2211848 | tf_op jit(solution)/shard_map/ppermute | solution.py:602
  18.6 18.9 %collective-permute-start.4 = (bf16[45,64,128]{2,1,0:T(8,128)(2,1)S(1)}, bf16[45,64,128]{2,1,0:T(8,128)(2,1)S(1)}, u32[]{:S(2)}, u32[]{:S(2)}) collective-permute-start(bf16[45,64,128]{2,1,0:T(8,128)(2,1)S(1)} %shard_map.31.own_ref.yo), channel_id=1, source_target_pairs={{0,16},{8,24},{16,0},{24,8},{1,17},{9,25},{17,1},{25,9},{2,18},{10... | collective-permute-start | bytes 2211848 | tf_op jit(solution)/shard_map/ppermute | solution.py:602
  32.9 4.6 %collective-permute-start.5 = (f32[48,128]{1,0:T(8,128)S(1)}, f32[48,128]{1,0:T(8,128)S(1)}, u32[]{:S(2)}, u32[]{:S(2)}) collective-permute-start(f32[48,128]{1,0:T(8,128)S(1)} %reduce_sum.18.g_ref), channel_id=1, source_target_pairs={{0,8},{8,0},{16,24},{24,16},{1,9},{9,1},{17,25},{25,17},{2,10},{10... | collective-permute-start | bytes 73736 | tf_op jit(solution)/shard_map/ppermute | solution.py:602
  37.5 15.8 %collective-permute-start.8 = (bf16[45,64,128]{2,1,0:T(8,128)(2,1)S(1)}, bf16[45,64,128]{2,1,0:T(8,128)(2,1)S(1)}, u32[]{:S(2)}, u32[]{:S(2)}) collective-permute-start(bf16[45,64,128]{2,1,0:T(8,128)(2,1)S(1)} %collective-permute-done.4.far_ref.yy), channel_id=1, source_target_pairs={{0,8},{8,0},{16,24},{24,16},{1,9},{9,1},{17,25},{25,17},{2,10},{10... | collective-permute-start | bytes 2211848 | tf_op jit(solution)/shard_map/ppermute | solution.py:602
  38.8 13.2 %all-to-all-start.1 = ((f32[8,64,128]{2,1,0:T(8,128)}), f32[8,64,128]{2,1,0:T(8,128)S(1)}, u32[]{:S(2)}, u32[]{:S(2)}) async-start(f32[8,64,128]{2,1,0:T(8,128)} %shard_map.34), calls=%async_computation.1 | async-start | bytes 524288 | tf_op jit(solution)/shard_map/all_to_all | solution.py:606
  48.5 3.9 %collective-permute-start.6 = (f32[64,128]{1,0:T(8,128)S(1)}, f32[64,128]{1,0:T(8,128)S(1)}, u32[]{:S(2)}, u32[]{:S(2)}) collective-permute-start(f32[64,128]{1,0:T(8,128)S(1)} %get-tuple-element.20.wh), channel_id=1, source_target_pairs={{0,16},{8,24},{16,0},{24,8},{1,17},{9,25},{17,1},{25,9},{2,18},{10... | collective-permute-start | bytes 98312 | tf_op jit(solution)/shard_map/ppermute | solution.py:602
  52.1 1.3 %collective-permute-start.7 = (f32[64,128]{1,0:T(8,128)S(1)}, f32[64,128]{1,0:T(8,128)S(1)}, u32[]{:S(2)}, u32[]{:S(2)}) collective-permute-start(f32[64,128]{1,0:T(8,128)S(1)} %reduce_sum.19.cs), channel_id=1, source_target_pairs={{0,8},{8,0},{16,24},{24,16},{1,9},{9,1},{17,25},{25,17},{2,10},{10... | collective-permute-start | bytes 98312 | tf_op jit(solution)/shard_map/ppermute | solution.py:602

commit v9 on v8

--- a/solution.py
+++ b/solution.py
@@ -113,19 +113,38 @@
     dn[PASSES + rows : 2 * PASSES + rows, :] = south_d[0:PASSES] + south_d[PASSES : 2 * PASSES]
 
 
-def pack_body(x_ref, d_ref, b_ref, a_ref, m_ref, dn):
+def edge_picks(width):
+    row = lax.broadcasted_iota(jnp.int32, (16, width), 0)
+    lane = lane_iota((16, width))
+    column = jnp.where(row % 8 < PASSES, row % 8, width - 8 + row % 8)
+    return [((lane == column) & (row // 8 == k)).astype(jnp.bfloat16) for k in range(2)]
+
+
+def own_body(x_ref, m_ref, tiles_ref):
+    rows, snaps, width = x_ref.shape
+    half = tiles_ref.shape[0]
+    pick, unit = edge_picks(width), eye(width)
+    for t in range(half):
+        tiles_ref[t] = dot_t(unit, tile_rows(x_ref, None, None, t))
+    for t in range(0, half - 1, 2):
+        first, second = (tile_rows(x_ref, None, None, t + j) for j in range(2))
+        m_ref[8 * t : 8 * t + 16, :] = (dot_t(pick[0], first) + dot_t(pick[1], second)).astype(jnp.bfloat16)
+
+
+def pack_body(x_ref, d_ref, b_ref, a_ref, own_ref, m_ref, dn):
     rows, snaps, width = x_ref.shape
     half = -(-rows // 2)
     count = half + 2 * PASSES
     edge = PASSES * snaps
-    row = lax.broadcasted_iota(jnp.int32, (16, width), 0)
-    lane = lane_iota((16, width))
-    column = jnp.where(row % 8 < PASSES, row % 8, width - 8 + row % 8)
-    pick = [((lane == column) & (row // 8 == k)).astype(jnp.bfloat16) for k in range(2)]
+    pick = edge_picks(width)
     picked = by_side(a_ref, b_ref)
     north, south = picked(0, edge)
     north_d, south_d = (v.astype(jnp.float32) for v in picked(edge, edge + 16))
+    begin, end = 8 * PASSES, 8 * PASSES + own_ref.shape[0]
+    m_ref[begin:end, :] = own_ref[...]
     for k in range(0, count, 2):
+        if begin <= 8 * k < end:
+            continue
         out = dot_t(pick[0], tile_rows(x_ref, north, south, k - PASSES))
         if k + 1 < count:
             out = out + dot_t(pick[1], tile_rows(x_ref, north, south, k + 1 - PASSES))
@@ -156,19 +175,23 @@
         return lax.ppermute(message, "lat", pairs + [(j, i) for i, j in pairs])
 
     a, b = swapped(a, 0), swapped(b, 1)
+    half = -(-rows // 2)
+    own, tiles = kernel_call(
+        own_body, (shape(16 * (half // 2)), jax.ShapeDtypeStruct((half, width, 2 * snaps), jnp.float32))
+    )(x)
     packed = kernel_call(
         pack_body, shape(16 * (-(-count // 2)) + 16), [VMEM((width, LANES), jnp.float32)]
-    )(x, d, b, a)
+    )(x, d, b, a, own)
     forward = [(i, (i + 1) % lons) for i in range(lons)]
     side = lax.ppermute(packed, "lon", forward)
     if lons > 2:
         from_east = lax.ppermute(packed, "lon", [(j, i) for i, j in forward])
         side = jnp.where(lax.broadcasted_iota(jnp.int32, side.shape, 0) % 8 < PASSES, from_east, side)
-    return side, a, b
+    return side, a, b, tiles
 
 
 OWN = 16
-EDGE = 16
+EDGE = 8
 EDGES = 8 + 2 * EDGE + 8
 
 
@@ -243,7 +266,7 @@
     return jnp.sqrt(jnp.maximum(jnp.cos(angle), 0.0))
 
 
-def interior_body(x_ref, d_ref, b_ref, a_ref, y_ref, ends_ref, dt_ref, u0, u1, ce, cs, dn):
+def interior_body(x_ref, d_ref, b_ref, a_ref, tiles_ref, y_ref, ends_ref, dt_ref, u0, u1, ce, cs, dn):
     rows, snaps, width = x_ref.shape
     half = -(-rows // 2)
     shift = rows - half
@@ -257,7 +280,11 @@
     north_d, south_d = (v.astype(jnp.float32) for v in picked(edge, edge + 16))
     outside = jnp.zeros((8, LANES), jnp.float32)
     for k in range(count):
-        tile = dot_t(unit, tile_rows(x_ref, north, south, k - PASSES))
+        t = k - PASSES
+        if 0 <= t < half:
+            tile = tiles_ref[t]
+        else:
+            tile = dot_t(unit, tile_rows(x_ref, north, south, t))
         u0[k, OWN:east, :] = tile
         ends_ref[k, :EDGE, :] = tile[:EDGE]
         ends_ref[k, EDGE:, :] = tile[width - EDGE :]
@@ -315,7 +342,7 @@
             y_ref[r] = jnp.where(ends, part, y_in[r].astype(jnp.float32)).astype(jnp.bfloat16)
 
 
-def smooth(x, d, side, a, b):
+def smooth(x, d, side, a, b, tiles):
     rows, snaps, width = x.shape
     count = -(-rows // 2) + 2 * PASSES
     f32 = lambda *shape: jax.ShapeDtypeStruct(shape, jnp.float32)
@@ -326,7 +353,7 @@
         (out, f32(count, 2 * EDGE, LANES), f32(2 * EDGE, LANES)),
         [field(OWN + width + 16)] * 4 + [VMEM((width, LANES), jnp.float32)],
         flops=1 << 32,
-    )(x, d, b, a)
+    )(x, d, b, a, tiles)
     return kernel_call(ends_body, out, [field(EDGES + 16)] * 4)(y, ends, dt, side)
 
 

time: 58.5 us -> 57.6 us (0.985)
  waiting for transfers between devices: 10.9 us -> 8.65 us
  local copies, waits for them, and re-layouts: 0.01 us -> 1.12 us
    ppermute x2, waiting for transfers between devices: 2.5 us -> 0.39 us  [swapped(): return lax.ppermute(message, 'lat', pairs + [(j, i) for i, j in pairs])]
    unnamed x4, local copies, waits for them, and re-layouts: 0.01 us -> 1.12 us
    pallas_call x0 -> x1, Pallas kernels: none -> 1 us  [halo_exchange(): kernel_call(own_body, (shape(16 * (half // 2)), jax.ShapeDtypeStruct((hal...]
  transfers between devices with their start and end apart: 10 -> 10, of which waited for: 6 -> 6; matrix products, arithmetic and copies ran while one was open for 0% -> 0% of each run, Pallas kernels for 20% -> 22%
where the time goes in v9:
time: 57.6 us; the launch traced here: 57.3 us
  Pallas kernels  20.7 us (36%)
  starting transfers between devices  15 us (26%)
  blocking collectives  11.5 us (20%)
  waiting for transfers between devices  8.65 us (15%)
  local copies, waits for them, and re-layouts  1.12 us (2%)
    all_to_all x1, blocking collectives, gathered(): return lax.all_to_all(parts, ('lat', 'lon'), 0, 0, tiled=True)  11.5 us
    ppermute x2, starting transfers between devices, swapped(): return lax.ppermute(message, 'lat', pairs + [(j, i) for i, j in pairs])  6.57 us
    ppermute x6, waiting for transfers between devices, exchanged(): lax.ppermute(block, 'tm', [(i, i ^ 1 << level) for i in range(count)])  6.2 us
    pallas_call x1, Pallas kernels, shards(): kernel_call(pair_levels_body, (f32(2 * RANK, 2 * snaps), f32(snaps, RANK)...  6.02 us
    pallas_call x1, Pallas kernels, shards(): out = result_call(quad_project_body, rows, snaps, width)(*operands)  4.63 us
    pallas_call x1, Pallas kernels, smooth(): kernel_call(interior_body, (out, f32(count, 2 * EDGE, LANES), f32(2 * EDG...  3.62 us
    all_to_all x1, starting transfers between devices, gathered(): return lax.all_to_all(parts, ('lat', 'lon'), 0, 0, tiled=True)  3.59 us
    ppermute x6, starting transfers between devices, exchanged(): lax.ppermute(block, 'tm', [(i, i ^ 1 << level) for i in range(count)])  3.35 us
  transfers between devices with their start and end apart: 10, of which 6 were waited for; matrix products, arithmetic and copies ran while one was open for 0% of the time, Pallas kernels for 22%

profile of v9, /device:TPU:0, one launch (start us, length us, event | category | flops | bytes accessed | tf_op | source)
XLA Modules:
  0.0 57.3 jit_solution(12298277815700392649)
XLA Ops:
  0.0 1.6 %shard_map.28 = (bf16[272,128]{1,0:T(8,128)(2,1)}, bf16[272,128]{1,0:T(8,128)(2,1)}) custom-call(bf16[45,64,128]{2,1,0:T(8,128)(2,1)} %bitcast.2, f32[45,128]{1,0:T(8,128)} %d_ref.3), custom_call_target="tpu_custom_call" | custom-call | flops 1048576 | bytes 1048576 | tf_op jit(solution)/shard_map/pallas_call | solution.py:164
  1.6 0.7 %collective-permute-start = (bf16[272,128]{1,0:T(8,128)(2,1)}, bf16[272,128]{1,0:T(8,128)(2,1)S(1)}, u32[]{:S(2)}, u32[]{:S(2)}) collective-permute-start(bf16[272,128]{1,0:T(8,128)(2,1)} %get-tuple-element.16), channel_id=1, source_target_pairs={{2,4},{4,2},{3,5},{5,3},{10,12},{12,10},{11,13},{13,11},{18,20},{2... | collective-permute-start | bytes 208904 | tf_op jit(solution)/shard_map/ppermute | solution.py:175
  2.3 5.9 %collective-permute-start.1 = (bf16[272,128]{1,0:T(8,128)(2,1)}, bf16[272,128]{1,0:T(8,128)(2,1)S(1)}, u32[]{:S(2)}, u32[]{:S(2)}) collective-permute-start(bf16[272,128]{1,0:T(8,128)(2,1)} %get-tuple-element.17), channel_id=1, source_target_pairs={{0,2},{4,6},{2,0},{6,4},{1,3},{5,7},{3,1},{7,5},{8,10},{12,14},{10... | collective-permute-start | bytes 208904 | tf_op jit(solution)/shard_map/ppermute | solution.py:175
  8.2 1.1 %copy-done = bf16[64,45,128]{2,0,1:T(8,128)(2,1)S(1)} copy-done((bf16[64,45,128]{2,0,1:T(8,128)(2,1)S(1)}, bf16[64,45,128]{2,0,1:T(8,128)(2,1)}, u32[]{:S(2)}) %copy-start) | copy-done | bytes 737304
  9.3 1.0 %shard_map.29 = (bf16[176,128]{1,0:T(8,128)(2,1)S(1)}, f32[23,128,128]{2,1,0:T(8,128)S(1)}) custom-call(bf16[45,64,128]{2,1,0:T(8,128)(2,1)S(1)} %bitcast.3), custom_call_target="tpu_custom_call" | custom-call | flops 1048576 | bytes 1048576 | tf_op jit(solution)/shard_map/pallas_call | solution.py:179
  10.3 0.0 collective-permute-done.b_ref
  10.3 0.4 collective-permute-done.1.a_ref
  10.7 0.0 copy-done.1
  10.7 0.3 shard_map.31
  11.0 1.5 %collective-permute-start.2 = (bf16[272,128]{1,0:T(8,128)(2,1)S(1)}, bf16[272,128]{1,0:T(8,128)(2,1)S(1)}, u32[]{:S(2)}, u32[]{:S(2)}) collective-permute-start(bf16[272,128]{1,0:T(8,128)(2,1)S(1)} %shard_map.31), channel_id=1, source_target_pairs={{0,1},{1,0},{2,3},{3,2},{4,5},{5,4},{6,7},{7,6},{8,9},{9,8},{10,11... | collective-permute-start | bytes 208904 | tf_op jit(solution)/shard_map/ppermute | solution.py:186
  12.5 3.6 %shard_map.30 = (bf16[45,64,128]{2,1,0:T(8,128)(2,1)S(1)}, f32[31,16,128]{2,1,0:T(8,128)S(1)}, f32[16,128]{1,0:T(8,128)S(1)}) custom-call(bf16[45,64,128]{2,1,0:T(8,128)(2,1)S(1)} %bitcast.5, f32[45,128]{1,0:T(8,128)S(1)} %copy-done.1, bf16[272,128]{1,0:T(8,128)(2,1)S(1)} %collective-permute-done.b_ref, bf16[272,128]{1,0:T(8,128)(2,1)S(1)} %collective-permute-done.1.a_ref, ...), custom_call_target="tpu_custom_call" | custom-call | flops 4294967296 | bytes 1048576 | tf_op jit(solution)/shard_map/pallas_call | solution.py:351
  16.1 0.0 collective-permute-done.2.side_ref
  16.1 1.5 %shard_map.32.own_ref.yo = bf16[45,64,128]{2,1,0:T(8,128)(2,1)S(1)} custom-call(bf16[45,64,128]{2,1,0:T(8,128)(2,1)S(1)} %get-tuple-element.19.y_in, f32[31,16,128]{2,1,0:T(8,128)S(1)} %get-tuple-element.20.ends_ref, f32[16,128]{1,0:T(8,128)S(1)} %get-tuple-element.21.dt_ref, bf16[272,128]{1,0:T(8,128)(2,1)S(1)} %collective-permute-done.2.side_ref), custom_call_target="tpu_custom_call" | custom-call | flops 1048576 | bytes 1048576 | tf_op jit(solution)/shard_map/pallas_call | solution.py:357
  17.7 0.1 collective-permute-start.3
  17.7 1.6 %collective-permute-start.4 = (bf16[45,64,128]{2,1,0:T(8,128)(2,1)S(1)}, bf16[45,64,128]{2,1,0:T(8,128)(2,1)S(1)}, u32[]{:S(2)}, u32[]{:S(2)}) collective-permute-start(bf16[45,64,128]{2,1,0:T(8,128)(2,1)S(1)} %shard_map.32.own_ref.yo), channel_id=1, source_target_pairs={{0,16},{8,24},{16,0},{24,8},{1,17},{9,25},{17,1},{25,9},{2,18},{10... | collective-permute-start | bytes 2211848 | tf_op jit(solution)/shard_map/ppermute | solution.py:629
  19.3 0.6 %collective-permute-done.3.other_ref.yp = bf16[45,64,128]{2,1,0:T(8,128)(2,1)S(1)} collective-permute-done((bf16[45,64,128]{2,1,0:T(8,128)(2,1)S(1)}, bf16[45,64,128]{2,1,0:T(8,128)(2,1)S(1)}, u32[]{:S(2)}, u32[]{:S(2)}) %collective-permute-start.3) | collective-permute-done | bytes 737312 | tf_op jit(solution)/shard_map/ppermute | solution.py:629
  19.9 0.7 %shard_map.33 = f32[8,48,128]{2,1,0:T(8,128)S(1)} custom-call(bf16[45,64,128]{2,1,0:T(8,128)(2,1)S(1)} %shard_map.32.own_ref.yo, bf16[45,64,128]{2,1,0:T(8,128)(2,1)S(1)} %collective-permute-done.3.other_ref.yp), custom_call_target="tpu_custom_call" | custom-call | flops 1048576 | bytes 1048576 | tf_op jit(solution)/shard_map/pallas_call | solution.py:645
  20.7 11.5 %all_to_all.10 = f32[8,48,128]{2,1,0:T(8,128)S(1)} all-to-all(f32[8,48,128]{2,1,0:T(8,128)S(1)} %shard_map.33), channel_id=1, replica_groups=mesh['tm'=4,'lat'=4,'lon'=2] {'lat','lon'}, dimensions={0} | all-to-all | bytes 393216 | tf_op jit(solution)/shard_map/all_to_all | solution.py:633
  32.2 0.1 collective-permute-start.5
  32.3 4.4 %collective-permute-done.4.far_ref.yy = bf16[45,64,128]{2,1,0:T(8,128)(2,1)S(1)} collective-permute-done((bf16[45,64,128]{2,1,0:T(8,128)(2,1)S(1)}, bf16[45,64,128]{2,1,0:T(8,128)(2,1)S(1)}, u32[]{:S(2)}, u32[]{:S(2)}) %collective-permute-start.4) | collective-permute-done | bytes 737312 | tf_op jit(solution)/shard_map/ppermute | solution.py:629
  36.6 0.0 collective-permute-done.5.gp_ref
  36.6 0.0 collective-permute-start.8
  36.6 1.3 %shard_map.35 = f32[8,64,128]{2,1,0:T(8,128)} custom-call(bf16[45,64,128]{2,1,0:T(8,128)(2,1)S(1)} %shard_map.32.own_ref.yo, bf16[45,64,128]{2,1,0:T(8,128)(2,1)S(1)} %collective-permute-done.3.other_ref.yp, bf16[45,64,128]{2,1,0:T(8,128)(2,1)S(1)} %collective-permute-done.4.far_ref.yy), custom_call_target="tpu_custom_call" | custom-call | flops 1048576 | bytes 1048576 | tf_op jit(solution)/shard_map/pallas_call | solution.py:649
  38.0 3.6 %all-to-all-start.1 = ((f32[8,64,128]{2,1,0:T(8,128)}), f32[8,64,128]{2,1,0:T(8,128)S(1)}, u32[]{:S(2)}, u32[]{:S(2)}) async-start(f32[8,64,128]{2,1,0:T(8,128)} %shard_map.35), calls=%async_computation.1 | async-start | bytes 524288 | tf_op jit(solution)/shard_map/all_to_all | solution.py:633
  41.6 6.0 %shard_map.34 = (f32[64,128]{1,0:T(8,128)S(1)}, f32[64,32]{1,0:T(8,128)S(1)}) custom-call(f32[48,128]{1,0:T(8,128)S(1)} %reduce_sum.18.g_ref, f32[48,128]{1,0:T(8,128)S(1)} %collective-permute-done.5.gp_ref), custom_call_target="tpu_custom_call" | custom-call | flops 4294967296 | bytes 1048576 | tf_op jit(solution)/shard_map/pallas_call | solution.py:651
  47.6 1.5 %collective-permute-start.6 = (f32[64,128]{1,0:T(8,128)S(1)}, f32[64,128]{1,0:T(8,128)S(1)}, u32[]{:S(2)}, u32[]{:S(2)}) collective-permute-start(f32[64,128]{1,0:T(8,128)S(1)} %get-tuple-element.24.wh), channel_id=1, source_target_pairs={{0,16},{8,24},{16,0},{24,8},{1,17},{9,25},{17,1},{25,9},{2,18},{10... | collective-permute-start | bytes 98312 | tf_op jit(solution)/shard_map/ppermute | solution.py:629
  49.1 2.1 %all-to-all-done.1 = f32[8,64,128]{2,1,0:T(8,128)S(1)} async-done(((f32[8,64,128]{2,1,0:T(8,128)}), f32[8,64,128]{2,1,0:T(8,128)S(1)}, u32[]{:S(2)}, u32[]{:S(2)}) %all-to-all-start.1) | async-done | bytes 262176 | tf_op jit(solution)/shard_map/all_to_all | solution.py:633
  51.2 0.1 collective-permute-start.7
  51.3 0.2 collective-permute-done.6.far_wh
  51.5 1.0 %collective-permute-done.7.twin = f32[64,128]{1,0:T(8,128)S(1)} collective-permute-done((f32[64,128]{1,0:T(8,128)S(1)}, f32[64,128]{1,0:T(8,128)S(1)}, u32[]{:S(2)}, u32[]{:S(2)}) %collective-permute-start.7) | collective-permute-done | bytes 32800 | tf_op jit(solution)/shard_map/ppermute | solution.py:629
  52.5 0.0 collective-permute-done.8.yz
  52.5 4.6 %shard_map.36 = bf16[45,64,128]{2,1,0:T(8,128)(2,1)} custom-call(f32[64,128]{1,0:T(8,128)S(1)} %get-tuple-element.24.wh, f32[64,32]{1,0:T(8,128)S(1)} %get-tuple-element.25.c, f32[64,128]{1,0:T(8,128)S(1)} %collective-permute-done.6.far_wh, f32[64,128]{1,0:T(8,128)S(1)} %reduce_sum.19.cs, f32[64,128]{1,0:T(8,128)S(1)} %collective-permute-done.7.twin, ...), custom_call_target="tpu_custom_call" | custom-call | flops 1048576 | bytes 1048576 | tf_op jit(solution)/shard_map/pallas_call | solution.py:657
  (4 shorter events, 0.0 us)
Async XLA Ops:
  0.0 10.7 %copy-start.1 = (f32[45,128]{1,0:T(8,128)S(1)}, f32[45,128]{1,0:T(8,128)}, u32[]{:S(2)}) copy-start(f32[45,128]{1,0:T(8,128)} %d_ref.3) | copy-start | bytes 69124
  1.6 8.7 %collective-permute-start = (bf16[272,128]{1,0:T(8,128)(2,1)}, bf16[272,128]{1,0:T(8,128)(2,1)S(1)}, u32[]{:S(2)}, u32[]{:S(2)}) collective-permute-start(bf16[272,128]{1,0:T(8,128)(2,1)} %get-tuple-element.16), channel_id=1, source_target_pairs={{2,4},{4,2},{3,5},{5,3},{10,12},{12,10},{11,13},{13,11},{18,20},{2... | collective-permute-start | bytes 208904 | tf_op jit(solution)/shard_map/ppermute | solution.py:175
  2.3 8.4 %collective-permute-start.1 = (bf16[272,128]{1,0:T(8,128)(2,1)}, bf16[272,128]{1,0:T(8,128)(2,1)S(1)}, u32[]{:S(2)}, u32[]{:S(2)}) collective-permute-start(bf16[272,128]{1,0:T(8,128)(2,1)} %get-tuple-element.17), channel_id=1, source_target_pairs={{0,2},{4,6},{2,0},{6,4},{1,3},{5,7},{3,1},{7,5},{8,10},{12,14},{10... | collective-permute-start | bytes 208904 | tf_op jit(solution)/shard_map/ppermute | solution.py:175
  8.2 1.1 %copy-start = (bf16[64,45,128]{2,0,1:T(8,128)(2,1)S(1)}, bf16[64,45,128]{2,0,1:T(8,128)(2,1)}, u32[]{:S(2)}) copy-start(bf16[64,45,128]{2,0,1:T(8,128)(2,1)} %param.2) | copy-start | bytes 2211844
  11.0 5.1 %collective-permute-start.2 = (bf16[272,128]{1,0:T(8,128)(2,1)S(1)}, bf16[272,128]{1,0:T(8,128)(2,1)S(1)}, u32[]{:S(2)}, u32[]{:S(2)}) collective-permute-start(bf16[272,128]{1,0:T(8,128)(2,1)S(1)} %shard_map.31), channel_id=1, source_target_pairs={{0,1},{1,0},{2,3},{3,2},{4,5},{5,4},{6,7},{7,6},{8,9},{9,8},{10,11... | collective-permute-start | bytes 208904 | tf_op jit(solution)/shard_map/ppermute | solution.py:186
  17.7 2.3 %collective-permute-start.3 = (bf16[45,64,128]{2,1,0:T(8,128)(2,1)S(1)}, bf16[45,64,128]{2,1,0:T(8,128)(2,1)S(1)}, u32[]{:S(2)}, u32[]{:S(2)}) collective-permute-start(bf16[45,64,128]{2,1,0:T(8,128)(2,1)S(1)} %shard_map.32.own_ref.yo), channel_id=1, source_target_pairs={{0,8},{8,0},{16,24},{24,16},{1,9},{9,1},{17,25},{25,17},{2,10},{10... | collective-permute-start | bytes 2211848 | tf_op jit(solution)/shard_map/ppermute | solution.py:629
  17.7 18.9 %collective-permute-start.4 = (bf16[45,64,128]{2,1,0:T(8,128)(2,1)S(1)}, bf16[45,64,128]{2,1,0:T(8,128)(2,1)S(1)}, u32[]{:S(2)}, u32[]{:S(2)}) collective-permute-start(bf16[45,64,128]{2,1,0:T(8,128)(2,1)S(1)} %shard_map.32.own_ref.yo), channel_id=1, source_target_pairs={{0,16},{8,24},{16,0},{24,8},{1,17},{9,25},{17,1},{25,9},{2,18},{10... | collective-permute-start | bytes 2211848 | tf_op jit(solution)/shard_map/ppermute | solution.py:629
  32.2 4.5 %collective-permute-start.5 = (f32[48,128]{1,0:T(8,128)S(1)}, f32[48,128]{1,0:T(8,128)S(1)}, u32[]{:S(2)}, u32[]{:S(2)}) collective-permute-start(f32[48,128]{1,0:T(8,128)S(1)} %reduce_sum.18.g_ref), channel_id=1, source_target_pairs={{0,8},{8,0},{16,24},{24,16},{1,9},{9,1},{17,25},{25,17},{2,10},{10... | collective-permute-start | bytes 73736 | tf_op jit(solution)/shard_map/ppermute | solution.py:629
  36.6 15.8 %collective-permute-start.8 = (bf16[45,64,128]{2,1,0:T(8,128)(2,1)S(1)}, bf16[45,64,128]{2,1,0:T(8,128)(2,1)S(1)}, u32[]{:S(2)}, u32[]{:S(2)}) collective-permute-start(bf16[45,64,128]{2,1,0:T(8,128)(2,1)S(1)} %collective-permute-done.4.far_ref.yy), channel_id=1, source_target_pairs={{0,8},{8,0},{16,24},{24,16},{1,9},{9,1},{17,25},{25,17},{2,10},{10... | collective-permute-start | bytes 2211848 | tf_op jit(solution)/shard_map/ppermute | solution.py:629
  38.0 13.2 %all-to-all-start.1 = ((f32[8,64,128]{2,1,0:T(8,128)}), f32[8,64,128]{2,1,0:T(8,128)S(1)}, u32[]{:S(2)}, u32[]{:S(2)}) async-start(f32[8,64,128]{2,1,0:T(8,128)} %shard_map.35), calls=%async_computation.1 | async-start | bytes 524288 | tf_op jit(solution)/shard_map/all_to_all | solution.py:633
  47.6 3.9 %collective-permute-start.6 = (f32[64,128]{1,0:T(8,128)S(1)}, f32[64,128]{1,0:T(8,128)S(1)}, u32[]{:S(2)}, u32[]{:S(2)}) collective-permute-start(f32[64,128]{1,0:T(8,128)S(1)} %get-tuple-element.24.wh), channel_id=1, source_target_pairs={{0,16},{8,24},{16,0},{24,8},{1,17},{9,25},{17,1},{25,9},{2,18},{10... | collective-permute-start | bytes 98312 | tf_op jit(solution)/shard_map/ppermute | solution.py:629
  51.2 1.3 %collective-permute-start.7 = (f32[64,128]{1,0:T(8,128)S(1)}, f32[64,128]{1,0:T(8,128)S(1)}, u32[]{:S(2)}, u32[]{:S(2)}) collective-permute-start(f32[64,128]{1,0:T(8,128)S(1)} %reduce_sum.19.cs), channel_id=1, source_target_pairs={{0,8},{8,0},{16,24},{24,16},{1,9},{9,1},{17,25},{25,17},{2,10},{10... | collective-permute-start | bytes 98312 | tf_op jit(solution)/shard_map/ppermute | solution.py:629

commit v10 on v9

--- a/solution.py
+++ b/solution.py
@@ -3,6 +3,7 @@
 
 import jax
 import jax.numpy as jnp
+import numpy as np
 from jax import lax
 from jax.experimental import pallas as pl
 from jax.experimental.pallas import tpu as pltpu
@@ -195,17 +196,14 @@
 EDGES = 8 + 2 * EDGE + 8
 
 
-def spread_faces(here, beside, k0, count, ce, cs, rows_at, snaps, shift):
+def spread_faces(here, beside, select_ref, ce, cs, rows_at):
     n = here.shape[0]
     lane = lane_iota((1, LANES))
     faces = jnp.concatenate([here + beside, here + roll(here, -1)], axis=0) * 0.5
     high, low = (v.astype(jnp.float32) for v in split2(faces))
     terms = jnp.where(lane < LANES // 2, high, roll(low, LANES // 2)).astype(jnp.bfloat16)
-    source = lax.broadcasted_iota(jnp.int32, (LANES, LANES), 0) % (LANES // 2)
-    relative = source - jnp.where(lane_iota((LANES, LANES)) < snaps, 0, shift)
-    for k in range(count):
-        pick = (relative == k0 + k).astype(jnp.bfloat16)
-        spread = jnp.dot(terms, pick, preferred_element_type=jnp.float32)
+    for k in range(select_ref.shape[0]):
+        spread = jnp.dot(terms, select_ref[k], preferred_element_type=jnp.float32)
         ce[k, rows_at, :] = spread[:n]
         cs[k, rows_at, :] = spread[n:]
 
@@ -266,7 +264,7 @@
     return jnp.sqrt(jnp.maximum(jnp.cos(angle), 0.0))
 
 
-def interior_body(x_ref, d_ref, b_ref, a_ref, tiles_ref, y_ref, ends_ref, dt_ref, u0, u1, ce, cs, dn):
+def interior_body(x_ref, d_ref, b_ref, a_ref, tiles_ref, select_ref, y_ref, ends_ref, dt_ref, scale_ref, u0, u1, ce, cs, dn):
     rows, snaps, width = x_ref.shape
     half = -(-rows // 2)
     shift = rows - half
@@ -295,9 +293,10 @@
     dt_ref[:EDGE, :] = dt[:EDGE]
     dt_ref[EDGE:, :] = dt[width - EDGE :]
     beside = jnp.concatenate([dt[1:], jnp.zeros((1, LANES), jnp.float32)], axis=0)
-    spread_faces(dt, beside, 0, count, ce, cs, slice(OWN, east), snaps, shift)
+    spread_faces(dt, beside, select_ref, ce, cs, slice(OWN, east))
     done = smoothing_passes(u0, u1, ce, cs, OWN, east, OWN, east, half, lane < snaps)
     scale = area_scale(rows, snaps)
+    scale_ref[...] = scale
     for t in range(half):
         weighted = (done[t + PASSES, OWN:east, :] * scale[t : t + 1]).astype(jnp.bfloat16)
         both = dot_t(unit, weighted).astype(jnp.bfloat16)
@@ -305,7 +304,7 @@
         y_ref[t + shift] = both[snaps:]
 
 
-def ends_body(y_in, ends_ref, dt_ref, side_ref, y_ref, u0, u1, ce, cs):
+def ends_body(y_in, ends_ref, dt_ref, scale_ref, select_ref, side_ref, y_ref, u0, u1, ce, cs):
     rows, snaps, width = y_in.shape
     half = -(-rows // 2)
     shift = rows - half
@@ -323,23 +322,22 @@
     halo = side_d[0:8] + side_d[8:16]
     here = jnp.concatenate([halo, dt_ref[...], halo], axis=0)
     beside = jnp.concatenate([here[1:], jnp.zeros((1, LANES), jnp.float32)], axis=0)
-    spread_faces(here, beside, 0, count, ce, cs, slice(low, high), snaps, shift)
+    spread_faces(here, beside, select_ref, ce, cs, slice(low, high))
     outside = jnp.zeros((8, LANES), jnp.float32)
     for buffer in (u0, u1):
         for k in range(count):
             buffer[k, high : high + 8, :] = outside
     done = smoothing_passes(u0, u1, ce, cs, low, high, low + 8, inner, half, lane < snaps)
-    scale = area_scale(rows, snaps)
     unit = eye(width)
     middle = jnp.zeros((width - 16, LANES), jnp.float32)
     ends = (lane < PASSES) | (lane >= width - PASSES)
     for t in range(half):
         west = done[t + PASSES, low + 8 : low + 16, :]
         east = done[t + PASSES, inner - 8 : inner, :]
-        weighted = (jnp.concatenate([west, middle, east], axis=0) * scale[t : t + 1]).astype(jnp.bfloat16)
+        weighted = (jnp.concatenate([west, middle, east], axis=0) * scale_ref[t : t + 1, :]).astype(jnp.bfloat16)
         both = dot_t(unit, weighted)
         for r, part in ((t, both[:snaps]), (t + shift, both[snaps:])):
-            y_ref[r] = jnp.where(ends, part, y_in[r].astype(jnp.float32)).astype(jnp.bfloat16)
+            y_ref[r] = jnp.where(ends, part.astype(jnp.bfloat16), y_in[r])
 
 
 def smooth(x, d, side, a, b, tiles):
@@ -347,14 +345,18 @@
     count = -(-rows // 2) + 2 * PASSES
     f32 = lambda *shape: jax.ShapeDtypeStruct(shape, jnp.float32)
     field = lambda n: VMEM((count, n, LANES), jnp.float32)
+    source = np.arange(LANES) % (LANES // 2)
+    wanted = np.arange(count)[:, None] + np.where(np.arange(LANES) < snaps, 0, rows // 2)
+    select = jnp.asarray(source[None, :, None] == wanted[:, None, :], jnp.bfloat16)
     out = jax.ShapeDtypeStruct(x.shape, jnp.bfloat16)
-    y, ends, dt = kernel_call(
+    tall = -(-(-(-rows // 2)) // 8) * 8
+    y, ends, dt, scale = kernel_call(
         interior_body,
-        (out, f32(count, 2 * EDGE, LANES), f32(2 * EDGE, LANES)),
+        (out, f32(count, 2 * EDGE, LANES), f32(2 * EDGE, LANES), f32(tall, LANES)),
         [field(OWN + width + 16)] * 4 + [VMEM((width, LANES), jnp.float32)],
         flops=1 << 32,
-    )(x, d, b, a, tiles)
-    return kernel_call(ends_body, out, [field(EDGES + 16)] * 4)(y, ends, dt, side)
+    )(x, d, b, a, tiles, select)
+    return kernel_call(ends_body, out, [field(EDGES + 16)] * 4)(y, ends, dt, scale, select, side)
 
 
 def mm(a, b):

time: 57.6 us -> 57.5 us (level)
  no operation moved by 1% of the time
where the time goes in v10:
time: 57.5 us; the launch traced here: 57.1 us
  Pallas kernels  20.6 us (36%)
  starting transfers between devices  15 us (26%)
  blocking collectives  11.6 us (20%)
  waiting for transfers between devices  8.52 us (15%)
  local copies, waits for them, and re-layouts  1.12 us (2%)
    all_to_all x1, blocking collectives, gathered(): return lax.all_to_all(parts, ('lat', 'lon'), 0, 0, tiled=True)  11.6 us
    ppermute x2, starting transfers between devices, swapped(): return lax.ppermute(message, 'lat', pairs + [(j, i) for i, j in pairs])  6.57 us
    ppermute x6, waiting for transfers between devices, exchanged(): lax.ppermute(block, 'tm', [(i, i ^ 1 << level) for i in range(count)])  6.07 us
    pallas_call x1, Pallas kernels, shards(): kernel_call(pair_levels_body, (f32(2 * RANK, 2 * snaps), f32(snaps, RANK)...  6.02 us
    pallas_call x1, Pallas kernels, shards(): out = result_call(quad_project_body, rows, snaps, width)(*operands)  4.63 us
    all_to_all x1, starting transfers between devices, gathered(): return lax.all_to_all(parts, ('lat', 'lon'), 0, 0, tiled=True)  3.59 us
    pallas_call x1, Pallas kernels, smooth(): kernel_call(interior_body, (out, f32(count, 2 * EDGE, LANES), f32(2 * EDG...  3.49 us
    ppermute x6, starting transfers between devices, exchanged(): lax.ppermute(block, 'tm', [(i, i ^ 1 << level) for i in range(count)])  3.35 us
  transfers between devices with their start and end apart: 10, of which 6 were waited for; matrix products, arithmetic and copies ran while one was open for 0% of the time, Pallas kernels for 22%

profile of v10, /device:TPU:0, one launch (start us, length us, event | category | flops | bytes accessed | tf_op | source)
XLA Modules:
  0.0 57.1 jit_solution(15724675538097544162)
XLA Ops:
  0.0 1.6 %shard_map.37 = (bf16[272,128]{1,0:T(8,128)(2,1)}, bf16[272,128]{1,0:T(8,128)(2,1)}) custom-call(bf16[45,64,128]{2,1,0:T(8,128)(2,1)} %bitcast.2, f32[45,128]{1,0:T(8,128)} %d_ref.3), custom_call_target="tpu_custom_call" | custom-call | flops 1048576 | bytes 1048576 | tf_op jit(solution)/shard_map/pallas_call | solution.py:165
  1.6 0.7 %collective-permute-start = (bf16[272,128]{1,0:T(8,128)(2,1)}, bf16[272,128]{1,0:T(8,128)(2,1)S(1)}, u32[]{:S(2)}, u32[]{:S(2)}) collective-permute-start(bf16[272,128]{1,0:T(8,128)(2,1)} %get-tuple-element.17), channel_id=1, source_target_pairs={{2,4},{4,2},{3,5},{5,3},{10,12},{12,10},{11,13},{13,11},{18,20},{2... | collective-permute-start | bytes 208904 | tf_op jit(solution)/shard_map/ppermute | solution.py:176
  2.3 5.9 %collective-permute-start.1 = (bf16[272,128]{1,0:T(8,128)(2,1)}, bf16[272,128]{1,0:T(8,128)(2,1)S(1)}, u32[]{:S(2)}, u32[]{:S(2)}) collective-permute-start(bf16[272,128]{1,0:T(8,128)(2,1)} %get-tuple-element.18), channel_id=1, source_target_pairs={{0,2},{4,6},{2,0},{6,4},{1,3},{5,7},{3,1},{7,5},{8,10},{12,14},{10... | collective-permute-start | bytes 208904 | tf_op jit(solution)/shard_map/ppermute | solution.py:176
  8.2 1.1 %copy-done = bf16[64,45,128]{2,0,1:T(8,128)(2,1)S(1)} copy-done((bf16[64,45,128]{2,0,1:T(8,128)(2,1)S(1)}, bf16[64,45,128]{2,0,1:T(8,128)(2,1)}, u32[]{:S(2)}) %copy-start) | copy-done | bytes 737304
  9.3 1.0 %shard_map.38 = (bf16[176,128]{1,0:T(8,128)(2,1)S(1)}, f32[23,128,128]{2,1,0:T(8,128)S(1)}) custom-call(bf16[45,64,128]{2,1,0:T(8,128)(2,1)S(1)} %bitcast.3), custom_call_target="tpu_custom_call" | custom-call | flops 1048576 | bytes 1048576 | tf_op jit(solution)/shard_map/pallas_call | solution.py:180
  10.3 0.0 collective-permute-done.b_ref
  10.3 0.4 collective-permute-done.1.a_ref
  10.7 0.3 shard_map.40
  11.0 1.5 %collective-permute-start.2 = (bf16[272,128]{1,0:T(8,128)(2,1)S(1)}, bf16[272,128]{1,0:T(8,128)(2,1)S(1)}, u32[]{:S(2)}, u32[]{:S(2)}) collective-permute-start(bf16[272,128]{1,0:T(8,128)(2,1)S(1)} %shard_map.40), channel_id=1, source_target_pairs={{0,1},{1,0},{2,3},{3,2},{4,5},{5,4},{6,7},{7,6},{8,9},{9,8},{10,11... | collective-permute-start | bytes 208904 | tf_op jit(solution)/shard_map/ppermute | solution.py:187
  12.5 0.0 copy-done.1
  12.5 3.5 %shard_map.39 = (bf16[45,64,128]{2,1,0:T(8,128)(2,1)S(1)}, f32[31,16,128]{2,1,0:T(8,128)S(1)}, f32[16,128]{1,0:T(8,128)S(1)}, f32[24,128]{1,0:T(8,128)S(1)}) custom-call(bf16[45,64,128]{2,1,0:T(8,128)(2,1)S(1)} %bitcast.5, f32[45,128]{1,0:T(8,128)S(1)} %copy-done.2, bf16[272,128]{1,0:T(8,128)(2,1)S(1)} %collective-permute-done.b_ref, ...), custom_call_target="tpu_custom_call" | custom-call | flops 4294967296 | bytes 1048576 | tf_op jit(solution)/shard_map/pallas_call | solution.py:353
  16.0 0.0 collective-permute-done.2.side_ref
  16.0 1.5 %shard_map.41.own_ref.yo = bf16[45,64,128]{2,1,0:T(8,128)(2,1)S(1)} custom-call(bf16[45,64,128]{2,1,0:T(8,128)(2,1)S(1)} %get-tuple-element.20.y_in, f32[31,16,128]{2,1,0:T(8,128)S(1)} %get-tuple-element.21.ends_ref, f32[16,128]{1,0:T(8,128)S(1)} %get-tuple-element.22.dt_ref, f32[24,128]{1,0:T(8,128)S(1)} %get-tuple-element.23.scale_ref, ...), custom_call_target="tpu_custom_call" | custom-call | flops 1048576 | bytes 1048576 | tf_op jit(solution)/shard_map/pallas_call | solution.py:359
  17.5 0.1 collective-permute-start.3
  17.6 1.6 %collective-permute-start.4 = (bf16[45,64,128]{2,1,0:T(8,128)(2,1)S(1)}, bf16[45,64,128]{2,1,0:T(8,128)(2,1)S(1)}, u32[]{:S(2)}, u32[]{:S(2)}) collective-permute-start(bf16[45,64,128]{2,1,0:T(8,128)(2,1)S(1)} %shard_map.41.own_ref.yo), channel_id=1, source_target_pairs={{0,16},{8,24},{16,0},{24,8},{1,17},{9,25},{17,1},{25,9},{2,18},{10... | collective-permute-start | bytes 2211848 | tf_op jit(solution)/shard_map/ppermute | solution.py:631
  19.2 0.6 %collective-permute-done.3.other_ref.yp = bf16[45,64,128]{2,1,0:T(8,128)(2,1)S(1)} collective-permute-done((bf16[45,64,128]{2,1,0:T(8,128)(2,1)S(1)}, bf16[45,64,128]{2,1,0:T(8,128)(2,1)S(1)}, u32[]{:S(2)}, u32[]{:S(2)}) %collective-permute-start.3) | collective-permute-done | bytes 737312 | tf_op jit(solution)/shard_map/ppermute | solution.py:631
  19.8 0.7 %shard_map.42 = f32[8,48,128]{2,1,0:T(8,128)S(1)} custom-call(bf16[45,64,128]{2,1,0:T(8,128)(2,1)S(1)} %shard_map.41.own_ref.yo, bf16[45,64,128]{2,1,0:T(8,128)(2,1)S(1)} %collective-permute-done.3.other_ref.yp), custom_call_target="tpu_custom_call" | custom-call | flops 1048576 | bytes 1048576 | tf_op jit(solution)/shard_map/pallas_call | solution.py:647
  20.5 11.6 %all_to_all.10 = f32[8,48,128]{2,1,0:T(8,128)S(1)} all-to-all(f32[8,48,128]{2,1,0:T(8,128)S(1)} %shard_map.42), channel_id=1, replica_groups=mesh['tm'=4,'lat'=4,'lon'=2] {'lat','lon'}, dimensions={0} | all-to-all | bytes 393216 | tf_op jit(solution)/shard_map/all_to_all | solution.py:635
  32.1 0.1 collective-permute-start.5
  32.2 4.3 %collective-permute-done.4.far_ref.yy = bf16[45,64,128]{2,1,0:T(8,128)(2,1)S(1)} collective-permute-done((bf16[45,64,128]{2,1,0:T(8,128)(2,1)S(1)}, bf16[45,64,128]{2,1,0:T(8,128)(2,1)S(1)}, u32[]{:S(2)}, u32[]{:S(2)}) %collective-permute-start.4) | collective-permute-done | bytes 737312 | tf_op jit(solution)/shard_map/ppermute | solution.py:631
  36.5 0.0 collective-permute-done.5.gp_ref
  36.5 0.0 collective-permute-start.8
  36.5 1.3 %shard_map.44 = f32[8,64,128]{2,1,0:T(8,128)} custom-call(bf16[45,64,128]{2,1,0:T(8,128)(2,1)S(1)} %shard_map.41.own_ref.yo, bf16[45,64,128]{2,1,0:T(8,128)(2,1)S(1)} %collective-permute-done.3.other_ref.yp, bf16[45,64,128]{2,1,0:T(8,128)(2,1)S(1)} %collective-permute-done.4.far_ref.yy), custom_call_target="tpu_custom_call" | custom-call | flops 1048576 | bytes 1048576 | tf_op jit(solution)/shard_map/pallas_call | solution.py:651
  37.8 3.6 %all-to-all-start.1 = ((f32[8,64,128]{2,1,0:T(8,128)}), f32[8,64,128]{2,1,0:T(8,128)S(1)}, u32[]{:S(2)}, u32[]{:S(2)}) async-start(f32[8,64,128]{2,1,0:T(8,128)} %shard_map.44), calls=%async_computation.1 | async-start | bytes 524288 | tf_op jit(solution)/shard_map/all_to_all | solution.py:635
  41.4 6.0 %shard_map.43 = (f32[64,128]{1,0:T(8,128)S(1)}, f32[64,32]{1,0:T(8,128)S(1)}) custom-call(f32[48,128]{1,0:T(8,128)S(1)} %reduce_sum.18.g_ref, f32[48,128]{1,0:T(8,128)S(1)} %collective-permute-done.5.gp_ref), custom_call_target="tpu_custom_call" | custom-call | flops 4294967296 | bytes 1048576 | tf_op jit(solution)/shard_map/pallas_call | solution.py:653
  47.4 1.5 %collective-permute-start.6 = (f32[64,128]{1,0:T(8,128)S(1)}, f32[64,128]{1,0:T(8,128)S(1)}, u32[]{:S(2)}, u32[]{:S(2)}) collective-permute-start(f32[64,128]{1,0:T(8,128)S(1)} %get-tuple-element.26.wh), channel_id=1, source_target_pairs={{0,16},{8,24},{16,0},{24,8},{1,17},{9,25},{17,1},{25,9},{2,18},{10... | collective-permute-start | bytes 98312 | tf_op jit(solution)/shard_map/ppermute | solution.py:631
  49.0 2.1 %all-to-all-done.1 = f32[8,64,128]{2,1,0:T(8,128)S(1)} async-done(((f32[8,64,128]{2,1,0:T(8,128)}), f32[8,64,128]{2,1,0:T(8,128)S(1)}, u32[]{:S(2)}, u32[]{:S(2)}) %all-to-all-start.1) | async-done | bytes 262176 | tf_op jit(solution)/shard_map/all_to_all | solution.py:635
  51.0 0.1 collective-permute-start.7
  51.1 0.2 collective-permute-done.6.far_wh
  51.4 1.0 %collective-permute-done.7.twin = f32[64,128]{1,0:T(8,128)S(1)} collective-permute-done((f32[64,128]{1,0:T(8,128)S(1)}, f32[64,128]{1,0:T(8,128)S(1)}, u32[]{:S(2)}, u32[]{:S(2)}) %collective-permute-start.7) | collective-permute-done | bytes 32800 | tf_op jit(solution)/shard_map/ppermute | solution.py:631
  52.3 0.0 collective-permute-done.8.yz
  52.3 4.6 %shard_map.45 = bf16[45,64,128]{2,1,0:T(8,128)(2,1)} custom-call(f32[64,128]{1,0:T(8,128)S(1)} %get-tuple-element.26.wh, f32[64,32]{1,0:T(8,128)S(1)} %get-tuple-element.27.c, f32[64,128]{1,0:T(8,128)S(1)} %collective-permute-done.6.far_wh, f32[64,128]{1,0:T(8,128)S(1)} %reduce_sum.19.cs, f32[64,128]{1,0:T(8,128)S(1)} %collective-permute-done.7.twin, ...), custom_call_target="tpu_custom_call" | custom-call | flops 1048576 | bytes 1048576 | tf_op jit(solution)/shard_map/pallas_call | solution.py:659
  (6 shorter events, 0.0 us)
Async XLA Ops:
  0.0 10.7 %copy-start.2 = (f32[45,128]{1,0:T(8,128)S(1)}, f32[45,128]{1,0:T(8,128)}, u32[]{:S(2)}) copy-start(f32[45,128]{1,0:T(8,128)} %d_ref.3) | copy-start | bytes 69124
  1.6 8.7 %collective-permute-start = (bf16[272,128]{1,0:T(8,128)(2,1)}, bf16[272,128]{1,0:T(8,128)(2,1)S(1)}, u32[]{:S(2)}, u32[]{:S(2)}) collective-permute-start(bf16[272,128]{1,0:T(8,128)(2,1)} %get-tuple-element.17), channel_id=1, source_target_pairs={{2,4},{4,2},{3,5},{5,3},{10,12},{12,10},{11,13},{13,11},{18,20},{2... | collective-permute-start | bytes 208904 | tf_op jit(solution)/shard_map/ppermute | solution.py:176
  2.3 8.4 %collective-permute-start.1 = (bf16[272,128]{1,0:T(8,128)(2,1)}, bf16[272,128]{1,0:T(8,128)(2,1)S(1)}, u32[]{:S(2)}, u32[]{:S(2)}) collective-permute-start(bf16[272,128]{1,0:T(8,128)(2,1)} %get-tuple-element.18), channel_id=1, source_target_pairs={{0,2},{4,6},{2,0},{6,4},{1,3},{5,7},{3,1},{7,5},{8,10},{12,14},{10... | collective-permute-start | bytes 208904 | tf_op jit(solution)/shard_map/ppermute | solution.py:176
  8.2 1.1 %copy-start = (bf16[64,45,128]{2,0,1:T(8,128)(2,1)S(1)}, bf16[64,45,128]{2,0,1:T(8,128)(2,1)}, u32[]{:S(2)}) copy-start(bf16[64,45,128]{2,0,1:T(8,128)(2,1)} %param.3) | copy-start | bytes 2211844
  9.3 3.2 %copy-start.1 = (bf16[31,128,128]{2,1,0:T(8,128)(2,1)S(1)}, bf16[31,128,128]{2,1,0:T(8,128)(2,1)}, u32[]{:S(2)}) copy-start(bf16[31,128,128]{2,1,0:T(8,128)(2,1)} %constant.4.clone.select_ref) | copy-start | bytes 3047428
  11.0 5.0 %collective-permute-start.2 = (bf16[272,128]{1,0:T(8,128)(2,1)S(1)}, bf16[272,128]{1,0:T(8,128)(2,1)S(1)}, u32[]{:S(2)}, u32[]{:S(2)}) collective-permute-start(bf16[272,128]{1,0:T(8,128)(2,1)S(1)} %shard_map.40), channel_id=1, source_target_pairs={{0,1},{1,0},{2,3},{3,2},{4,5},{5,4},{6,7},{7,6},{8,9},{9,8},{10,11... | collective-permute-start | bytes 208904 | tf_op jit(solution)/shard_map/ppermute | solution.py:187
  17.5 2.3 %collective-permute-start.3 = (bf16[45,64,128]{2,1,0:T(8,128)(2,1)S(1)}, bf16[45,64,128]{2,1,0:T(8,128)(2,1)S(1)}, u32[]{:S(2)}, u32[]{:S(2)}) collective-permute-start(bf16[45,64,128]{2,1,0:T(8,128)(2,1)S(1)} %shard_map.41.own_ref.yo), channel_id=1, source_target_pairs={{0,8},{8,0},{16,24},{24,16},{1,9},{9,1},{17,25},{25,17},{2,10},{10... | collective-permute-start | bytes 2211848 | tf_op jit(solution)/shard_map/ppermute | solution.py:631
  17.6 18.9 %collective-permute-start.4 = (bf16[45,64,128]{2,1,0:T(8,128)(2,1)S(1)}, bf16[45,64,128]{2,1,0:T(8,128)(2,1)S(1)}, u32[]{:S(2)}, u32[]{:S(2)}) collective-permute-start(bf16[45,64,128]{2,1,0:T(8,128)(2,1)S(1)} %shard_map.41.own_ref.yo), channel_id=1, source_target_pairs={{0,16},{8,24},{16,0},{24,8},{1,17},{9,25},{17,1},{25,9},{2,18},{10... | collective-permute-start | bytes 2211848 | tf_op jit(solution)/shard_map/ppermute | solution.py:631
  32.1 4.3 %collective-permute-start.5 = (f32[48,128]{1,0:T(8,128)S(1)}, f32[48,128]{1,0:T(8,128)S(1)}, u32[]{:S(2)}, u32[]{:S(2)}) collective-permute-start(f32[48,128]{1,0:T(8,128)S(1)} %reduce_sum.18.g_ref), channel_id=1, source_target_pairs={{0,8},{8,0},{16,24},{24,16},{1,9},{9,1},{17,25},{25,17},{2,10},{10... | collective-permute-start | bytes 73736 | tf_op jit(solution)/shard_map/ppermute | solution.py:631
  36.5 15.8 %collective-permute-start.8 = (bf16[45,64,128]{2,1,0:T(8,128)(2,1)S(1)}, bf16[45,64,128]{2,1,0:T(8,128)(2,1)S(1)}, u32[]{:S(2)}, u32[]{:S(2)}) collective-permute-start(bf16[45,64,128]{2,1,0:T(8,128)(2,1)S(1)} %collective-permute-done.4.far_ref.yy), channel_id=1, source_target_pairs={{0,8},{8,0},{16,24},{24,16},{1,9},{9,1},{17,25},{25,17},{2,10},{10... | collective-permute-start | bytes 2211848 | tf_op jit(solution)/shard_map/ppermute | solution.py:631
  37.8 13.2 %all-to-all-start.1 = ((f32[8,64,128]{2,1,0:T(8,128)}), f32[8,64,128]{2,1,0:T(8,128)S(1)}, u32[]{:S(2)}, u32[]{:S(2)}) async-start(f32[8,64,128]{2,1,0:T(8,128)} %shard_map.44), calls=%async_computation.1 | async-start | bytes 524288 | tf_op jit(solution)/shard_map/all_to_all | solution.py:635
  47.4 3.9 %collective-permute-start.6 = (f32[64,128]{1,0:T(8,128)S(1)}, f32[64,128]{1,0:T(8,128)S(1)}, u32[]{:S(2)}, u32[]{:S(2)}) collective-permute-start(f32[64,128]{1,0:T(8,128)S(1)} %get-tuple-element.26.wh), channel_id=1, source_target_pairs={{0,16},{8,24},{16,0},{24,8},{1,17},{9,25},{17,1},{25,9},{2,18},{10... | collective-permute-start | bytes 98312 | tf_op jit(solution)/shard_map/ppermute | solution.py:631
  51.0 1.3 %collective-permute-start.7 = (f32[64,128]{1,0:T(8,128)S(1)}, f32[64,128]{1,0:T(8,128)S(1)}, u32[]{:S(2)}, u32[]{:S(2)}) collective-permute-start(f32[64,128]{1,0:T(8,128)S(1)} %reduce_sum.19.cs), channel_id=1, source_target_pairs={{0,8},{8,0},{16,24},{24,16},{1,9},{9,1},{17,25},{25,17},{2,10},{10... | collective-permute-start | bytes 98312 | tf_op jit(solution)/shard_map/ppermute | solution.py:631

commit v11 on v10

--- a/solution.py
+++ b/solution.py
@@ -328,14 +328,16 @@
         for k in range(count):
             buffer[k, high : high + 8, :] = outside
     done = smoothing_passes(u0, u1, ce, cs, low, high, low + 8, inner, half, lane < snaps)
-    unit = eye(width)
-    middle = jnp.zeros((width - 16, LANES), jnp.float32)
+    row, column = (lax.broadcasted_iota(jnp.int32, (16, width), axis) for axis in range(2))
+    place = (column == jnp.where(row < 8, row, width - 16 + row)).astype(jnp.bfloat16)
     ends = (lane < PASSES) | (lane >= width - PASSES)
     for t in range(half):
         west = done[t + PASSES, low + 8 : low + 16, :]
         east = done[t + PASSES, inner - 8 : inner, :]
-        weighted = (jnp.concatenate([west, middle, east], axis=0) * scale_ref[t : t + 1, :]).astype(jnp.bfloat16)
-        both = dot_t(unit, weighted)
+        weighted = (jnp.concatenate([west, east], axis=0) * scale_ref[t : t + 1, :]).astype(jnp.bfloat16)
+        both = lax.dot_general(
+            weighted, place, (((0,), (0,)), ((), ())), preferred_element_type=jnp.float32
+        )
         for r, part in ((t, both[:snaps]), (t + shift, both[snaps:])):
             y_ref[r] = jnp.where(ends, part.astype(jnp.bfloat16), y_in[r])
 

time: 57.5 us -> 57.2 us (level)
  no operation moved by 1% of the time
where the time goes in v11:
time: 57.2 us; the launch traced here: 56.9 us
  Pallas kernels  20.3 us (35%)
  starting transfers between devices  15 us (26%)
  blocking collectives  11.6 us (20%)
  waiting for transfers between devices  8.53 us (15%)
  local copies, waits for them, and re-layouts  1.12 us (2%)
    all_to_all x1, blocking collectives, gathered(): return lax.all_to_all(parts, ('lat', 'lon'), 0, 0, tiled=True)  11.6 us
    ppermute x2, starting transfers between devices, swapped(): return lax.ppermute(message, 'lat', pairs + [(j, i) for i, j in pairs])  6.57 us
    ppermute x6, waiting for transfers between devices, exchanged(): lax.ppermute(block, 'tm', [(i, i ^ 1 << level) for i in range(count)])  6.08 us
    pallas_call x1, Pallas kernels, shards(): kernel_call(pair_levels_body, (f32(2 * RANK, 2 * snaps), f32(snaps, RANK)...  6.02 us
    pallas_call x1, Pallas kernels, shards(): out = result_call(quad_project_body, rows, snaps, width)(*operands)  4.62 us
    all_to_all x1, starting transfers between devices, gathered(): return lax.all_to_all(parts, ('lat', 'lon'), 0, 0, tiled=True)  3.59 us
    pallas_call x1, Pallas kernels, smooth(): kernel_call(interior_body, (out, f32(count, 2 * EDGE, LANES), f32(2 * EDG...  3.49 us
    ppermute x6, starting transfers between devices, exchanged(): lax.ppermute(block, 'tm', [(i, i ^ 1 << level) for i in range(count)])  3.35 us
  transfers between devices with their start and end apart: 10, of which 6 were waited for; matrix products, arithmetic and copies ran while one was open for 0% of the time, Pallas kernels for 22%

profile of v11, /device:TPU:0, one launch (start us, length us, event | category | flops | bytes accessed | tf_op | source)
XLA Modules:
  0.0 56.9 jit_solution(3863442871681808821)
XLA Ops:
  0.0 1.6 %shard_map.37 = (bf16[272,128]{1,0:T(8,128)(2,1)}, bf16[272,128]{1,0:T(8,128)(2,1)}) custom-call(bf16[45,64,128]{2,1,0:T(8,128)(2,1)} %bitcast.2, f32[45,128]{1,0:T(8,128)} %d_ref.3), custom_call_target="tpu_custom_call" | custom-call | flops 1048576 | bytes 1048576 | tf_op jit(solution)/shard_map/pallas_call | solution.py:165
  1.6 0.7 %collective-permute-start = (bf16[272,128]{1,0:T(8,128)(2,1)}, bf16[272,128]{1,0:T(8,128)(2,1)S(1)}, u32[]{:S(2)}, u32[]{:S(2)}) collective-permute-start(bf16[272,128]{1,0:T(8,128)(2,1)} %get-tuple-element.17), channel_id=1, source_target_pairs={{2,4},{4,2},{3,5},{5,3},{10,12},{12,10},{11,13},{13,11},{18,20},{2... | collective-permute-start | bytes 208904 | tf_op jit(solution)/shard_map/ppermute | solution.py:176
  2.3 5.9 %collective-permute-start.1 = (bf16[272,128]{1,0:T(8,128)(2,1)}, bf16[272,128]{1,0:T(8,128)(2,1)S(1)}, u32[]{:S(2)}, u32[]{:S(2)}) collective-permute-start(bf16[272,128]{1,0:T(8,128)(2,1)} %get-tuple-element.18), channel_id=1, source_target_pairs={{0,2},{4,6},{2,0},{6,4},{1,3},{5,7},{3,1},{7,5},{8,10},{12,14},{10... | collective-permute-start | bytes 208904 | tf_op jit(solution)/shard_map/ppermute | solution.py:176
  8.2 1.1 %copy-done = bf16[64,45,128]{2,0,1:T(8,128)(2,1)S(1)} copy-done((bf16[64,45,128]{2,0,1:T(8,128)(2,1)S(1)}, bf16[64,45,128]{2,0,1:T(8,128)(2,1)}, u32[]{:S(2)}) %copy-start) | copy-done | bytes 737304
  9.3 1.0 %shard_map.38 = (bf16[176,128]{1,0:T(8,128)(2,1)S(1)}, f32[23,128,128]{2,1,0:T(8,128)S(1)}) custom-call(bf16[45,64,128]{2,1,0:T(8,128)(2,1)S(1)} %bitcast.3), custom_call_target="tpu_custom_call" | custom-call | flops 1048576 | bytes 1048576 | tf_op jit(solution)/shard_map/pallas_call | solution.py:180
  10.3 0.0 collective-permute-done.b_ref
  10.3 0.4 collective-permute-done.1.a_ref
  10.7 0.0 copy-done.2
  10.7 0.3 shard_map.40
  11.0 1.5 %collective-permute-start.2 = (bf16[272,128]{1,0:T(8,128)(2,1)S(1)}, bf16[272,128]{1,0:T(8,128)(2,1)S(1)}, u32[]{:S(2)}, u32[]{:S(2)}) collective-permute-start(bf16[272,128]{1,0:T(8,128)(2,1)S(1)} %shard_map.40), channel_id=1, source_target_pairs={{0,1},{1,0},{2,3},{3,2},{4,5},{5,4},{6,7},{7,6},{8,9},{9,8},{10,11... | collective-permute-start | bytes 208904 | tf_op jit(solution)/shard_map/ppermute | solution.py:187
  12.5 3.5 %shard_map.39 = (bf16[45,64,128]{2,1,0:T(8,128)(2,1)S(1)}, f32[31,16,128]{2,1,0:T(8,128)S(1)}, f32[16,128]{1,0:T(8,128)S(1)}, f32[24,128]{1,0:T(8,128)S(1)}) custom-call(bf16[45,64,128]{2,1,0:T(8,128)(2,1)S(1)} %bitcast.5, f32[45,128]{1,0:T(8,128)S(1)} %copy-done.2, bf16[272,128]{1,0:T(8,128)(2,1)S(1)} %collective-permute-done.b_ref, ...), custom_call_target="tpu_custom_call" | custom-call | flops 4294967296 | bytes 1048576 | tf_op jit(solution)/shard_map/pallas_call | solution.py:355
  16.0 0.0 collective-permute-done.2.side_ref
  16.0 1.2 %shard_map.41.own_ref.yo = bf16[45,64,128]{2,1,0:T(8,128)(2,1)S(1)} custom-call(bf16[45,64,128]{2,1,0:T(8,128)(2,1)S(1)} %get-tuple-element.20.y_in, f32[31,16,128]{2,1,0:T(8,128)S(1)} %get-tuple-element.21.ends_ref, f32[16,128]{1,0:T(8,128)S(1)} %get-tuple-element.22.dt_ref, f32[24,128]{1,0:T(8,128)S(1)} %get-tuple-element.23.scale_ref, ...), custom_call_target="tpu_custom_call" | custom-call | flops 1048576 | bytes 1048576 | tf_op jit(solution)/shard_map/pallas_call | solution.py:361
  17.2 0.1 collective-permute-start.3
  17.3 1.6 %collective-permute-start.4 = (bf16[45,64,128]{2,1,0:T(8,128)(2,1)S(1)}, bf16[45,64,128]{2,1,0:T(8,128)(2,1)S(1)}, u32[]{:S(2)}, u32[]{:S(2)}) collective-permute-start(bf16[45,64,128]{2,1,0:T(8,128)(2,1)S(1)} %shard_map.41.own_ref.yo), channel_id=1, source_target_pairs={{0,16},{8,24},{16,0},{24,8},{1,17},{9,25},{17,1},{25,9},{2,18},{10... | collective-permute-start | bytes 2211848 | tf_op jit(solution)/shard_map/ppermute | solution.py:633
  18.9 0.6 %collective-permute-done.3.other_ref.yp = bf16[45,64,128]{2,1,0:T(8,128)(2,1)S(1)} collective-permute-done((bf16[45,64,128]{2,1,0:T(8,128)(2,1)S(1)}, bf16[45,64,128]{2,1,0:T(8,128)(2,1)S(1)}, u32[]{:S(2)}, u32[]{:S(2)}) %collective-permute-start.3) | collective-permute-done | bytes 737312 | tf_op jit(solution)/shard_map/ppermute | solution.py:633
  19.5 0.7 %shard_map.42 = f32[8,48,128]{2,1,0:T(8,128)S(1)} custom-call(bf16[45,64,128]{2,1,0:T(8,128)(2,1)S(1)} %shard_map.41.own_ref.yo, bf16[45,64,128]{2,1,0:T(8,128)(2,1)S(1)} %collective-permute-done.3.other_ref.yp), custom_call_target="tpu_custom_call" | custom-call | flops 1048576 | bytes 1048576 | tf_op jit(solution)/shard_map/pallas_call | solution.py:649
  20.3 11.6 %all_to_all.10 = f32[8,48,128]{2,1,0:T(8,128)S(1)} all-to-all(f32[8,48,128]{2,1,0:T(8,128)S(1)} %shard_map.42), channel_id=1, replica_groups=mesh['tm'=4,'lat'=4,'lon'=2] {'lat','lon'}, dimensions={0} | all-to-all | bytes 393216 | tf_op jit(solution)/shard_map/all_to_all | solution.py:637
  31.9 0.1 collective-permute-start.5
  32.0 4.3 %collective-permute-done.4.far_ref.yy = bf16[45,64,128]{2,1,0:T(8,128)(2,1)S(1)} collective-permute-done((bf16[45,64,128]{2,1,0:T(8,128)(2,1)S(1)}, bf16[45,64,128]{2,1,0:T(8,128)(2,1)S(1)}, u32[]{:S(2)}, u32[]{:S(2)}) %collective-permute-start.4) | collective-permute-done | bytes 737312 | tf_op jit(solution)/shard_map/ppermute | solution.py:633
  36.2 0.0 collective-permute-done.5.gp_ref
  36.2 0.0 collective-permute-start.8
  36.2 1.3 %shard_map.44 = f32[8,64,128]{2,1,0:T(8,128)} custom-call(bf16[45,64,128]{2,1,0:T(8,128)(2,1)S(1)} %shard_map.41.own_ref.yo, bf16[45,64,128]{2,1,0:T(8,128)(2,1)S(1)} %collective-permute-done.3.other_ref.yp, bf16[45,64,128]{2,1,0:T(8,128)(2,1)S(1)} %collective-permute-done.4.far_ref.yy), custom_call_target="tpu_custom_call" | custom-call | flops 1048576 | bytes 1048576 | tf_op jit(solution)/shard_map/pallas_call | solution.py:653
  37.5 3.6 %all-to-all-start.1 = ((f32[8,64,128]{2,1,0:T(8,128)}), f32[8,64,128]{2,1,0:T(8,128)S(1)}, u32[]{:S(2)}, u32[]{:S(2)}) async-start(f32[8,64,128]{2,1,0:T(8,128)} %shard_map.44), calls=%async_computation.1 | async-start | bytes 524288 | tf_op jit(solution)/shard_map/all_to_all | solution.py:637
  41.1 6.0 %shard_map.43 = (f32[64,128]{1,0:T(8,128)S(1)}, f32[64,32]{1,0:T(8,128)S(1)}) custom-call(f32[48,128]{1,0:T(8,128)S(1)} %reduce_sum.18.g_ref, f32[48,128]{1,0:T(8,128)S(1)} %collective-permute-done.5.gp_ref), custom_call_target="tpu_custom_call" | custom-call | flops 4294967296 | bytes 1048576 | tf_op jit(solution)/shard_map/pallas_call | solution.py:655
  47.2 1.5 %collective-permute-start.6 = (f32[64,128]{1,0:T(8,128)S(1)}, f32[64,128]{1,0:T(8,128)S(1)}, u32[]{:S(2)}, u32[]{:S(2)}) collective-permute-start(f32[64,128]{1,0:T(8,128)S(1)} %get-tuple-element.26.wh), channel_id=1, source_target_pairs={{0,16},{8,24},{16,0},{24,8},{1,17},{9,25},{17,1},{25,9},{2,18},{10... | collective-permute-start | bytes 98312 | tf_op jit(solution)/shard_map/ppermute | solution.py:633
  48.7 2.1 %all-to-all-done.1 = f32[8,64,128]{2,1,0:T(8,128)S(1)} async-done(((f32[8,64,128]{2,1,0:T(8,128)}), f32[8,64,128]{2,1,0:T(8,128)S(1)}, u32[]{:S(2)}, u32[]{:S(2)}) %all-to-all-start.1) | async-done | bytes 262176 | tf_op jit(solution)/shard_map/all_to_all | solution.py:637
  50.8 0.1 collective-permute-start.7
  50.9 0.2 collective-permute-done.6.far_wh
  51.1 1.0 %collective-permute-done.7.twin = f32[64,128]{1,0:T(8,128)S(1)} collective-permute-done((f32[64,128]{1,0:T(8,128)S(1)}, f32[64,128]{1,0:T(8,128)S(1)}, u32[]{:S(2)}, u32[]{:S(2)}) %collective-permute-start.7) | collective-permute-done | bytes 32800 | tf_op jit(solution)/shard_map/ppermute | solution.py:633
  52.1 0.0 collective-permute-done.8.yz
  52.1 4.6 %shard_map.45 = bf16[45,64,128]{2,1,0:T(8,128)(2,1)} custom-call(f32[64,128]{1,0:T(8,128)S(1)} %get-tuple-element.26.wh, f32[64,32]{1,0:T(8,128)S(1)} %get-tuple-element.27.c, f32[64,128]{1,0:T(8,128)S(1)} %collective-permute-done.6.far_wh, f32[64,128]{1,0:T(8,128)S(1)} %reduce_sum.19.cs, f32[64,128]{1,0:T(8,128)S(1)} %collective-permute-done.7.twin, ...), custom_call_target="tpu_custom_call" | custom-call | flops 1048576 | bytes 1048576 | tf_op jit(solution)/shard_map/pallas_call | solution.py:661
  (6 shorter events, 0.0 us)
Async XLA Ops:
  0.0 10.7 %copy-start.2 = (f32[45,128]{1,0:T(8,128)S(1)}, f32[45,128]{1,0:T(8,128)}, u32[]{:S(2)}) copy-start(f32[45,128]{1,0:T(8,128)} %d_ref.3) | copy-start | bytes 69124
  1.6 8.7 %collective-permute-start = (bf16[272,128]{1,0:T(8,128)(2,1)}, bf16[272,128]{1,0:T(8,128)(2,1)S(1)}, u32[]{:S(2)}, u32[]{:S(2)}) collective-permute-start(bf16[272,128]{1,0:T(8,128)(2,1)} %get-tuple-element.17), channel_id=1, source_target_pairs={{2,4},{4,2},{3,5},{5,3},{10,12},{12,10},{11,13},{13,11},{18,20},{2... | collective-permute-start | bytes 208904 | tf_op jit(solution)/shard_map/ppermute | solution.py:176
  2.3 8.4 %collective-permute-start.1 = (bf16[272,128]{1,0:T(8,128)(2,1)}, bf16[272,128]{1,0:T(8,128)(2,1)S(1)}, u32[]{:S(2)}, u32[]{:S(2)}) collective-permute-start(bf16[272,128]{1,0:T(8,128)(2,1)} %get-tuple-element.18), channel_id=1, source_target_pairs={{0,2},{4,6},{2,0},{6,4},{1,3},{5,7},{3,1},{7,5},{8,10},{12,14},{10... | collective-permute-start | bytes 208904 | tf_op jit(solution)/shard_map/ppermute | solution.py:176
  8.2 1.1 %copy-start = (bf16[64,45,128]{2,0,1:T(8,128)(2,1)S(1)}, bf16[64,45,128]{2,0,1:T(8,128)(2,1)}, u32[]{:S(2)}) copy-start(bf16[64,45,128]{2,0,1:T(8,128)(2,1)} %param.3) | copy-start | bytes 2211844
  9.3 3.2 %copy-start.1 = (bf16[31,128,128]{2,1,0:T(8,128)(2,1)S(1)}, bf16[31,128,128]{2,1,0:T(8,128)(2,1)}, u32[]{:S(2)}) copy-start(bf16[31,128,128]{2,1,0:T(8,128)(2,1)} %constant.4.clone.select_ref) | copy-start | bytes 3047428
  11.0 5.0 %collective-permute-start.2 = (bf16[272,128]{1,0:T(8,128)(2,1)S(1)}, bf16[272,128]{1,0:T(8,128)(2,1)S(1)}, u32[]{:S(2)}, u32[]{:S(2)}) collective-permute-start(bf16[272,128]{1,0:T(8,128)(2,1)S(1)} %shard_map.40), channel_id=1, source_target_pairs={{0,1},{1,0},{2,3},{3,2},{4,5},{5,4},{6,7},{7,6},{8,9},{9,8},{10,11... | collective-permute-start | bytes 208904 | tf_op jit(solution)/shard_map/ppermute | solution.py:187
  17.2 2.3 %collective-permute-start.3 = (bf16[45,64,128]{2,1,0:T(8,128)(2,1)S(1)}, bf16[45,64,128]{2,1,0:T(8,128)(2,1)S(1)}, u32[]{:S(2)}, u32[]{:S(2)}) collective-permute-start(bf16[45,64,128]{2,1,0:T(8,128)(2,1)S(1)} %shard_map.41.own_ref.yo), channel_id=1, source_target_pairs={{0,8},{8,0},{16,24},{24,16},{1,9},{9,1},{17,25},{25,17},{2,10},{10... | collective-permute-start | bytes 2211848 | tf_op jit(solution)/shard_map/ppermute | solution.py:633
  17.3 18.9 %collective-permute-start.4 = (bf16[45,64,128]{2,1,0:T(8,128)(2,1)S(1)}, bf16[45,64,128]{2,1,0:T(8,128)(2,1)S(1)}, u32[]{:S(2)}, u32[]{:S(2)}) collective-permute-start(bf16[45,64,128]{2,1,0:T(8,128)(2,1)S(1)} %shard_map.41.own_ref.yo), channel_id=1, source_target_pairs={{0,16},{8,24},{16,0},{24,8},{1,17},{9,25},{17,1},{25,9},{2,18},{10... | collective-permute-start | bytes 2211848 | tf_op jit(solution)/shard_map/ppermute | solution.py:633
  31.9 4.3 %collective-permute-start.5 = (f32[48,128]{1,0:T(8,128)S(1)}, f32[48,128]{1,0:T(8,128)S(1)}, u32[]{:S(2)}, u32[]{:S(2)}) collective-permute-start(f32[48,128]{1,0:T(8,128)S(1)} %reduce_sum.18.g_ref), channel_id=1, source_target_pairs={{0,8},{8,0},{16,24},{24,16},{1,9},{9,1},{17,25},{25,17},{2,10},{10... | collective-permute-start | bytes 73736 | tf_op jit(solution)/shard_map/ppermute | solution.py:633
  36.2 15.8 %collective-permute-start.8 = (bf16[45,64,128]{2,1,0:T(8,128)(2,1)S(1)}, bf16[45,64,128]{2,1,0:T(8,128)(2,1)S(1)}, u32[]{:S(2)}, u32[]{:S(2)}) collective-permute-start(bf16[45,64,128]{2,1,0:T(8,128)(2,1)S(1)} %collective-permute-done.4.far_ref.yy), channel_id=1, source_target_pairs={{0,8},{8,0},{16,24},{24,16},{1,9},{9,1},{17,25},{25,17},{2,10},{10... | collective-permute-start | bytes 2211848 | tf_op jit(solution)/shard_map/ppermute | solution.py:633
  37.5 13.2 %all-to-all-start.1 = ((f32[8,64,128]{2,1,0:T(8,128)}), f32[8,64,128]{2,1,0:T(8,128)S(1)}, u32[]{:S(2)}, u32[]{:S(2)}) async-start(f32[8,64,128]{2,1,0:T(8,128)} %shard_map.44), calls=%async_computation.1 | async-start | bytes 524288 | tf_op jit(solution)/shard_map/all_to_all | solution.py:637
  47.2 3.9 %collective-permute-start.6 = (f32[64,128]{1,0:T(8,128)S(1)}, f32[64,128]{1,0:T(8,128)S(1)}, u32[]{:S(2)}, u32[]{:S(2)}) collective-permute-start(f32[64,128]{1,0:T(8,128)S(1)} %get-tuple-element.26.wh), channel_id=1, source_target_pairs={{0,16},{8,24},{16,0},{24,8},{1,17},{9,25},{17,1},{25,9},{2,18},{10... | collective-permute-start | bytes 98312 | tf_op jit(solution)/shard_map/ppermute | solution.py:633
  50.8 1.3 %collective-permute-start.7 = (f32[64,128]{1,0:T(8,128)S(1)}, f32[64,128]{1,0:T(8,128)S(1)}, u32[]{:S(2)}, u32[]{:S(2)}) collective-permute-start(f32[64,128]{1,0:T(8,128)S(1)} %reduce_sum.19.cs), channel_id=1, source_target_pairs={{0,8},{8,0},{16,24},{24,16},{1,9},{9,1},{17,25},{25,17},{2,10},{10... | collective-permute-start | bytes 98312 | tf_op jit(solution)/shard_map/ppermute | solution.py:633
